TPU v7x, 256 devices: a whole 4x4x8 slice. The times are simulated.
256 devices in a mesh: lon: 16 (over z, x_hi), lat: 8 (over y, x_lo), mem: 2 (over core).
Axes of the slice: x: 4 (x_hi: 2, x_lo: 2; x = x_hi * 2 + x_lo), y: 4, z: 8, core: 2. Of those that a mesh axis runs over, the one named last changes fastest.
Arguments:
- alpha_fields: float32 [2, 10, 512, 1024], P('mem', None, 'lon', 'lat'), may hold values from -6 to 6
- anomalies: float32 [2, 10, 512, 1024], P('mem', None, 'lon', 'lat'), may hold values from -6 to 6
- lon_faces: float32 [10, 512, 1024], P(None, 'lon', 'lat'), may hold values from 0.02 to 0.24
- lat_faces: float32 [10, 512, 1024], P(None, 'lon', 'lat'), may hold values from 0.02 to 0.24
- normalizer: float32 [10, 512, 1024], P(None, 'lon', 'lat'), may hold values from 0.5 to 2
- innovation: float32 [10, 512, 1024], P(None, 'lon', 'lat'), may hold values from -6 to 6
- misfit_weight: float32 [10, 512, 1024], P(None, 'lon', 'lat'), may hold values from 0.3 to 3
- vertical: float32 [10, 10], replicated, may hold values from -0.2 to 1.2
Outputs:
- increment: float32 [10, 512, 1024], P('mem', 'lon', 'lat')
- gradient: float32 [2, 10, 512, 1024], P('mem', None, 'lon', 'lat')
All inputs are finite; a program needn't handle non-finite values.
Results may differ from a plain program's by a relative error of at most 0.00015.
Values sent between devices are 32-bit elements; how exact they have to be, the bound alone decides.
No kernel may reach another device: no remote copies, remote signals or barrier semaphores. Data moves between devices by JAX's collectives and lax.ppermute only.
A program may use at most 64 MiB of HBM per device.

v0:
```python
import functools
import math

import jax
import jax.numpy as jnp
from jax import lax
from jax.experimental import pallas as pl
from jax.experimental.pallas import tpu as pltpu
from jax.sharding import PartitionSpec as P

STEPS = 8
DEEP = 2 * STEPS
LANES = 128
VMEM = pl.BlockSpec(memory_space=pltpu.VMEM)
SMEM = pl.BlockSpec(memory_space=pltpu.SMEM)
PARAMS = pltpu.CompilerParams(vmem_limit_bytes=32 * 1024 * 1024)


def f32(*shape):
    return jax.ShapeDtypeStruct(shape, jnp.float32)


def around(value, axis, steps):
    count = lax.axis_size(axis)
    pairs = [(source, (source + steps) % count) for source in range(count)]
    return lax.ppermute(value, axis, pairs)


def lane_places(deep, shallow):
    at = 0
    places = []
    for width, count in ((DEEP, deep), (STEPS, shallow)):
        for _ in range(count):
            places.append((at // LANES, at % LANES, width))
            at += width
    return places, -(-at // LANES)


def mixed(vertical_ref, alpha_ref, level):
    total = vertical_ref[level, 0] * alpha_ref[0, 0]
    for k in range(1, alpha_ref.shape[1]):
        total = total + vertical_ref[level, k] * alpha_ref[0, k]
    return total


def prepare_kernel(
    half, vertical, alpha, anomaly, lon_faces, lat_faces, normalizer, innovation, weight, keep, give
):
    base = lax.axis_index("mem") * half
    other = half - base
    last = lax.axis_index("lat") == lax.axis_size("lat") - 1
    lane = lax.broadcasted_iota(jnp.int32, lon_faces.shape[1:], 1)
    closed = jnp.logical_and(last, lane == lon_faces.shape[2] - 1)
    for i in range(half):
        mine, theirs = base + i, other + i
        root = jnp.sqrt(weight[mine])
        keep[i] = mixed(vertical, alpha, mine)
        keep[half + i] = lon_faces[mine]
        keep[2 * half + i] = jnp.where(closed, 0.0, lat_faces[mine])
        keep[3 * half + i] = normalizer[mine] * anomaly[0, mine] * root
        keep[4 * half + i] = root * innovation[mine]
        keep[5 * half + i] = 1.0 / root
        give[i] = mixed(vertical, alpha, theirs)
        give[half + i] = normalizer[theirs] * anomaly[0, theirs] * jnp.sqrt(weight[theirs])


def field_refs(half, keep, got):
    deep = [keep.at[i] for i in range(half)]
    deep += [got.at[i] for i in range(half)]
    deep += [keep.at[half + i] for i in range(2 * half)]
    shallow = [keep.at[3 * half + i] for i in range(half)]
    shallow += [got.at[half + i] for i in range(half)]
    shallow += [keep.at[4 * half + i] for i in range(half)]
    return deep, shallow


def lon_pack_kernel(half, keep, got, first, final):
    deep, shallow = field_refs(half, keep, got)
    rows = keep.shape[1]
    at = 0
    for width, fields in ((DEEP, deep), (STEPS, shallow)):
        for ref in fields:
            first[at : at + width] = ref[:width]
            final[at : at + width] = ref[rows - width :]
            at += width


def lat_pack_kernel(half, keep, got, below, above, deep_out, shallow_out, first, final):
    deep, shallow = field_refs(half, keep, got)
    rows, lanes = keep.shape[1:]
    places, _ = lane_places(len(deep), len(shallow))
    first[...] = jnp.zeros_like(first)
    final[...] = jnp.zeros_like(final)
    lane = lax.broadcasted_iota(jnp.int32, (1, lanes), 1)
    at = 0
    index = 0
    for width, fields, out in ((DEEP, deep, deep_out), (STEPS, shallow, shallow_out)):
        start = DEEP - width
        stop = rows + DEEP + width
        for i, ref in enumerate(fields):
            out[i, :width] = below[at : at + width]
            out[i, width : width + rows] = ref[...]
            out[i, width + rows :] = above[at : at + width]
            at += width
            group, place, _ = places[index]
            index += 1
            block = out[i]
            inside = jnp.logical_and(lane >= place, lane < place + width)
            head = pltpu.roll(block, place, axis=1) if place else block
            shift = (place + width) % lanes
            tail = pltpu.roll(block, shift, axis=1) if shift else block
            first[group, start:stop] = jnp.where(inside, head, first[group, start:stop])
            final[group, start:stop] = jnp.where(inside, tail, final[group, start:stop])


def diffusion_step(field, lon_coef, lat_coef):
    rows, lanes = field.shape
    flux_x = lon_coef * (pltpu.roll(field, rows - 1, axis=0) - field)
    flux_y = lat_coef * (pltpu.roll(field, lanes - 1, axis=1) - field)
    return (
        field
        + (flux_x - pltpu.roll(flux_x, 1, axis=0))
        + (flux_y - pltpu.roll(flux_y, 1, axis=1))
    )


def diffuse_kernel(
    half, deep, shallow, keep, left, right, increment, mine, theirs, deep_side, shallow_side
):
    lanes = deep.shape[2]
    rows = keep.shape[1]
    places, _ = lane_places(deep.shape[0], shallow.shape[0])
    lane = lax.broadcasted_iota(jnp.int32, (1, lanes), 1)
    index = 0
    for width, side in ((DEEP, deep_side), (STEPS, shallow_side)):
        start = DEEP - width
        stop = rows + DEEP + width
        for i in range(side.shape[0]):
            group, place, _ = places[index]
            index += 1
            after = pltpu.roll(right[group, start:stop], (lanes - place) % lanes, axis=1)
            before = pltpu.roll(left[group, start:stop], (2 * lanes - width - place) % lanes, axis=1)
            side[i] = jnp.where(
                lane < width, after, jnp.where(lane >= lanes - width, before, 0.0)
            )

    def level(i, carry):
        def deep_field(n):
            return jnp.concatenate([deep[n * half + i], deep_side[n * half + i]], axis=1)

        def shallow_field(n):
            return jnp.concatenate([shallow[n * half + i], shallow_side[n * half + i]], axis=1)

        cut = DEEP - STEPS
        lon_coef, lat_coef = deep_field(2), deep_field(3)
        roots = []
        for n in range(2):
            field = deep_field(n)
            for _ in range(STEPS):
                field = diffusion_step(field, lon_coef, lat_coef)
            roots.append(field[cut:-cut])
        gains = [shallow_field(0), shallow_field(1)]
        total = gains[0] * roots[0] + gains[1] * roots[1]
        increment[i] = total[STEPS : STEPS + rows, :lanes] * keep[5 * half + i]
        residual = total - shallow_field(2)
        lon_coef, lat_coef = lon_coef[cut:-cut], lat_coef[cut:-cut]
        for gain, out in zip(gains, (mine, theirs)):
            field = gain * residual
            for _ in range(STEPS):
                field = diffusion_step(field, lon_coef, lat_coef)
            out[i] = field[STEPS : STEPS + rows, :lanes]
        return carry

    lax.fori_loop(0, half, level, 0)


def gradient_kernel(half, vertical, alpha, mine, got, gradient):
    base = lax.axis_index("mem") * half
    other = half - base
    for k in range(2 * half):
        total = alpha[0, k]
        for i in range(half):
            total = total + vertical[base + i, k] * mine[i]
            total = total + vertical[other + i, k] * got[i]
        gradient[0, k] = total


def local(
    alpha_fields, anomalies, lon_faces, lat_faces, normalizer, innovation, misfit_weight, vertical
):
    levels, rows, lanes = lon_faces.shape
    half = levels // 2
    deep_count, shallow_count = 4 * half, 3 * half
    _, groups = lane_places(deep_count, shallow_count)
    pack_rows = DEEP * deep_count + STEPS * shallow_count
    deep_shape = (deep_count, rows + 2 * DEEP, lanes)
    shallow_shape = (shallow_count, rows + 2 * STEPS, lanes)

    keep, give = pl.pallas_call(
        functools.partial(prepare_kernel, half),
        out_shape=(f32(6 * half, rows, lanes), f32(levels, rows, lanes)),
        in_specs=[SMEM] + [VMEM] * 7,
        out_specs=(VMEM, VMEM),
        compiler_params=PARAMS,
        name="prepare",
    )(vertical, alpha_fields, anomalies, lon_faces, lat_faces, normalizer, innovation, misfit_weight)
    got = around(give, "mem", 1)

    first, final = pl.pallas_call(
        functools.partial(lon_pack_kernel, half),
        out_shape=(f32(pack_rows, lanes), f32(pack_rows, lanes)),
        in_specs=[VMEM] * 2,
        out_specs=(VMEM, VMEM),
        compiler_params=PARAMS,
        name="lon_pack",
    )(keep, got)
    below = around(final, "lon", 1)
    above = around(first, "lon", -1)

    pack_shape = f32(groups, rows + 2 * DEEP, lanes)
    deep, shallow, first, final = pl.pallas_call(
        functools.partial(lat_pack_kernel, half),
        out_shape=(f32(*deep_shape), f32(*shallow_shape), pack_shape, pack_shape),
        in_specs=[VMEM] * 4,
        out_specs=(VMEM,) * 4,
        compiler_params=PARAMS,
        name="lat_pack",
    )(keep, got, below, above)
    left = around(final, "lat", 1)
    right = around(first, "lat", -1)

    block = f32(half, rows, lanes)
    increment, mine, theirs = pl.pallas_call(
        functools.partial(diffuse_kernel, half),
        out_shape=(block, block, block),
        in_specs=[VMEM] * 5,
        out_specs=(VMEM,) * 3,
        scratch_shapes=[
            pltpu.VMEM(deep_shape, jnp.float32),
            pltpu.VMEM(shallow_shape, jnp.float32),
        ],
        compiler_params=PARAMS,
        name="diffuse",
    )(deep, shallow, keep, left, right)
    got = around(theirs, "mem", 1)

    gradient = pl.pallas_call(
        functools.partial(gradient_kernel, half),
        out_shape=f32(*alpha_fields.shape),
        in_specs=[SMEM] + [VMEM] * 3,
        out_specs=VMEM,
        compiler_params=PARAMS,
        name="gradient",
    )(vertical, alpha_fields, mine, got)
    return (increment, gradient)


def solution(mesh):
    return jax.shard_map(
        local,
        mesh=mesh,
        in_specs=(
            P("mem", None, "lon", "lat"),
            P("mem", None, "lon", "lat"),
            P(None, "lon", "lat"),
            P(None, "lon", "lat"),
            P(None, "lon", "lat"),
            P(None, "lon", "lat"),
            P(None, "lon", "lat"),
            P(),
        ),
        out_specs=(P("mem", "lon", "lat"), P("mem", None, "lon", "lat")),
        check_vma=False,
    )
```

profile of v0, /device:TPU:1, one launch (start us, length us, event | category | flops | bytes accessed | tf_op | source)
XLA Modules:
  0.0 52.3 jit_solution(14822004376523569166)
XLA Ops:
  0.6 0.0 copy-start
  0.6 0.9 %copy-done = f32[1,10,32,128]{3,2,1,0:T(8,128)S(1)} copy-done((f32[1,10,32,128]{3,2,1,0:T(8,128)S(1)}, f32[1,10,32,128]{3,2,1,0:T(8,128)}, u32[]{:S(2)}) %copy-start) | copy-done | bytes 163864
  1.5 0.0 copy-start.1
  1.6 0.9 %copy-done.1 = f32[1,10,32,128]{3,2,1,0:T(8,128)S(1)} copy-done((f32[1,10,32,128]{3,2,1,0:T(8,128)S(1)}, f32[1,10,32,128]{3,2,1,0:T(8,128)}, u32[]{:S(2)}) %copy-start.1) | copy-done | bytes 163864
  2.5 0.0 copy-start.2
  2.5 0.9 %copy-done.2 = f32[10,32,128]{2,1,0:T(8,128)S(1)} copy-done((f32[10,32,128]{2,1,0:T(8,128)S(1)}, f32[10,32,128]{2,1,0:T(8,128)}, u32[]{:S(2)}) %copy-start.2) | copy-done | bytes 163864
  3.4 0.0 copy-start.3
  3.4 0.9 %copy-done.3 = f32[10,32,128]{2,1,0:T(8,128)S(1)} copy-done((f32[10,32,128]{2,1,0:T(8,128)S(1)}, f32[10,32,128]{2,1,0:T(8,128)}, u32[]{:S(2)}) %copy-start.3) | copy-done | bytes 163864
  4.3 0.0 copy-start.4
  4.3 0.9 %copy-done.4 = f32[10,32,128]{2,1,0:T(8,128)S(1)} copy-done((f32[10,32,128]{2,1,0:T(8,128)S(1)}, f32[10,32,128]{2,1,0:T(8,128)}, u32[]{:S(2)}) %copy-start.4) | copy-done | bytes 163864
  5.2 0.0 copy-start.5
  5.2 0.9 %copy-done.5 = f32[10,32,128]{2,1,0:T(8,128)S(1)} copy-done((f32[10,32,128]{2,1,0:T(8,128)S(1)}, f32[10,32,128]{2,1,0:T(8,128)}, u32[]{:S(2)}) %copy-start.5) | copy-done | bytes 163864
  6.1 0.0 copy-start.6
  6.1 0.9 %copy-done.6 = f32[10,32,128]{2,1,0:T(8,128)S(1)} copy-done((f32[10,32,128]{2,1,0:T(8,128)S(1)}, f32[10,32,128]{2,1,0:T(8,128)}, u32[]{:S(2)}) %copy-start.6) | copy-done | bytes 163864
  7.0 0.0 copy-start.7
  7.0 0.7 %copy-done.7 = f32[10,10]{1,0:T(8,128)S(1)} copy-done((f32[10,10]{1,0:T(8,128)S(1)}, f32[10,10]{1,0:T(8,128)}, u32[]{:S(2)}) %copy-start.7) | copy-done | bytes 424
  7.7 0.9 %prepare.1 = (f32[30,32,128]{2,1,0:T(8,128)S(1)}, f32[10,32,128]{2,1,0:T(8,128)S(1)}) custom-call(f32[10,10]{1,0:T(8,128)S(1)} %copy-done.7, f32[1,10,32,128]{3,2,1,0:T(8,128)S(1)} %copy-done, f32[1,10,32,128]{3,2,1,0:T(8,128)S(1)} %copy-done.1, f32[10,32,128]{2,1,0:T(8,128)S(1)} %copy-done.2, f32[10,32,128]{2,1,0:T(8,128)S(1)} %copy-done.3, ...), custom_call_target="tpu_custom_call" | custom-call | tf_op jit(solution)/shard_map/prepare/pallas_call | solution.py:199
  8.6 3.3 %collective-permute-start = (f32[10,32,128]{2,1,0:T(8,128)S(1)}, f32[10,32,128]{2,1,0:T(8,128)S(1)}, u32[]{:S(2)}, u32[]{:S(2)}) collective-permute-start(f32[10,32,128]{2,1,0:T(8,128)S(1)} %get-tuple-element.14), channel_id=1, source_target_pairs={{0,1},{1,0},{2,3},{3,2},{4,5},{5,4},{6,7},{7,6},{8,9},{9,8},{10,11... | collective-permute-start | bytes 491528 | tf_op jit(solution)/shard_map/ppermute | solution.py:26
  11.9 1.0 %collective-permute-done.got = f32[10,32,128]{2,1,0:T(8,128)S(1)} collective-permute-done((f32[10,32,128]{2,1,0:T(8,128)S(1)}, f32[10,32,128]{2,1,0:T(8,128)S(1)}, u32[]{:S(2)}, u32[]{:S(2)}) %collective-permute-start) | collective-permute-done | bytes 163872 | tf_op jit(solution)/shard_map/ppermute | solution.py:26
  13.0 1.1 %collective-permute-start.1 = (f32[440,128]{1,0:T(8,128)S(1)}, f32[440,128]{1,0:T(8,128)S(1)}, u32[]{:S(2)}, u32[]{:S(2)}) collective-permute-start(f32[440,128]{1,0:T(8,128)S(1)} %get-tuple-element.15), channel_id=1, source_target_pairs={{0,16},{16,32},{32,48},{48,64},{64,80},{80,96},{96,112},{112,128},... | collective-permute-start | bytes 675848 | tf_op jit(solution)/shard_map/ppermute | solution.py:26
  14.1 5.4 %collective-permute-start.2 = (f32[440,128]{1,0:T(8,128)S(1)}, f32[440,128]{1,0:T(8,128)S(1)}, u32[]{:S(2)}, u32[]{:S(2)}) collective-permute-start(f32[440,128]{1,0:T(8,128)S(1)} %get-tuple-element.16), channel_id=1, source_target_pairs={{0,240},{16,0},{32,16},{48,32},{64,48},{80,64},{96,80},{112,96},{1... | collective-permute-start | bytes 675848 | tf_op jit(solution)/shard_map/ppermute | solution.py:26
  19.5 5.5 %collective-permute-done.1.below = f32[440,128]{1,0:T(8,128)S(1)} collective-permute-done((f32[440,128]{1,0:T(8,128)S(1)}, f32[440,128]{1,0:T(8,128)S(1)}, u32[]{:S(2)}, u32[]{:S(2)}) %collective-permute-start.1) | collective-permute-done | bytes 225312 | tf_op jit(solution)/shard_map/ppermute | solution.py:26
  25.0 1.8 %collective-permute-done.2.above = f32[440,128]{1,0:T(8,128)S(1)} collective-permute-done((f32[440,128]{1,0:T(8,128)S(1)}, f32[440,128]{1,0:T(8,128)S(1)}, u32[]{:S(2)}, u32[]{:S(2)}) %collective-permute-start.2) | collective-permute-done | bytes 225312 | tf_op jit(solution)/shard_map/ppermute | solution.py:26
  26.8 0.6 %lat_pack.1 = (f32[20,64,128]{2,1,0:T(8,128)S(1)}, f32[15,48,128]{2,1,0:T(8,128)S(1)}, f32[4,64,128]{2,1,0:T(8,128)S(1)}, f32[4,64,128]{2,1,0:T(8,128)S(1)}) custom-call(f32[30,32,128]{2,1,0:T(8,128)S(1)} %get-tuple-element.13.keep, f32[10,32,128]{2,1,0:T(8,128)S(1)} %collective-permute-done.got, f32[440,128]{1,0:T(8,128)S(1)} %collective-permute-done.1.below, ...), custom_call_target="tpu_custom_call" | custom-call | tf_op jit(solution)/shard_map/lat_pack/pallas_call | solution.py:221
  27.4 0.4 collective-permute-start.3
  27.8 3.3 %collective-permute-start.4 = (f32[4,64,128]{2,1,0:T(8,128)S(1)}, f32[4,64,128]{2,1,0:T(8,128)S(1)}, u32[]{:S(2)}, u32[]{:S(2)}) collective-permute-start(f32[4,64,128]{2,1,0:T(8,128)S(1)} %get-tuple-element.20), channel_id=1, source_target_pairs={{0,14},{2,0},{4,2},{6,4},{8,6},{10,8},{12,10},{14,12},{1,15},{3,1}... | collective-permute-start | bytes 393224 | tf_op jit(solution)/shard_map/ppermute | solution.py:26
  31.0 2.4 %collective-permute-done.3.left = f32[4,64,128]{2,1,0:T(8,128)S(1)} collective-permute-done((f32[4,64,128]{2,1,0:T(8,128)S(1)}, f32[4,64,128]{2,1,0:T(8,128)S(1)}, u32[]{:S(2)}, u32[]{:S(2)}) %collective-permute-start.3) | collective-permute-done | bytes 131104 | tf_op jit(solution)/shard_map/ppermute | solution.py:26
  33.4 1.4 %collective-permute-done.4.right = f32[4,64,128]{2,1,0:T(8,128)S(1)} collective-permute-done((f32[4,64,128]{2,1,0:T(8,128)S(1)}, f32[4,64,128]{2,1,0:T(8,128)S(1)}, u32[]{:S(2)}, u32[]{:S(2)}) %collective-permute-start.4) | collective-permute-done | bytes 131104 | tf_op jit(solution)/shard_map/ppermute | solution.py:26
  34.8 12.6 %diffuse.1 = (f32[5,32,128]{2,1,0:T(8,128)}, f32[5,32,128]{2,1,0:T(8,128)S(1)}, f32[5,32,128]{2,1,0:T(8,128)S(1)}) custom-call(f32[20,64,128]{2,1,0:T(8,128)S(1)} %get-tuple-element.17.deep, f32[15,48,128]{2,1,0:T(8,128)S(1)} %get-tuple-element.18.shallow, f32[30,32,128]{2,1,0:T(8,128)S(1)} %get-tuple-element.13.keep, ...), custom_call_target="tpu_custom_call" | custom-call | tf_op jit(solution)/shard_map/diffuse/pallas_call | solution.py:233
  47.4 2.5 %collective-permute-start.5 = (f32[5,32,128]{2,1,0:T(8,128)S(1)}, f32[5,32,128]{2,1,0:T(8,128)S(1)}, u32[]{:S(2)}, u32[]{:S(2)}) collective-permute-start(f32[5,32,128]{2,1,0:T(8,128)S(1)} %get-tuple-element.23), channel_id=1, source_target_pairs={{0,1},{1,0},{2,3},{3,2},{4,5},{5,4},{6,7},{7,6},{8,9},{9,8},{10,11... | collective-permute-start | bytes 245768 | tf_op jit(solution)/shard_map/ppermute | solution.py:26
  49.9 0.9 %collective-permute-done.5.got = f32[5,32,128]{2,1,0:T(8,128)S(1)} collective-permute-done((f32[5,32,128]{2,1,0:T(8,128)S(1)}, f32[5,32,128]{2,1,0:T(8,128)S(1)}, u32[]{:S(2)}, u32[]{:S(2)}) %collective-permute-start.5) | collective-permute-done | bytes 81952 | tf_op jit(solution)/shard_map/ppermute | solution.py:26
  50.8 1.5 %gradient.1 = f32[1,10,32,128]{3,2,1,0:T(8,128)} custom-call(f32[10,10]{1,0:T(8,128)S(1)} %copy-done.7, f32[1,10,32,128]{3,2,1,0:T(8,128)S(1)} %copy-done, f32[5,32,128]{2,1,0:T(8,128)S(1)} %get-tuple-element.22.mine, f32[5,32,128]{2,1,0:T(8,128)S(1)} %collective-permute-done.5.got), custom_call_target="tpu_custom_call" | custom-call | tf_op jit(solution)/shard_map/gradient/pallas_call | solution.py:247
  (1 shorter events, 0.0 us)
Async XLA Ops:
  0.6 0.9 %copy-start = (f32[1,10,32,128]{3,2,1,0:T(8,128)S(1)}, f32[1,10,32,128]{3,2,1,0:T(8,128)}, u32[]{:S(2)}) copy-start(f32[1,10,32,128]{3,2,1,0:T(8,128)} %alpha.3) | copy-start | bytes 491524
  1.5 0.9 %copy-start.1 = (f32[1,10,32,128]{3,2,1,0:T(8,128)S(1)}, f32[1,10,32,128]{3,2,1,0:T(8,128)}, u32[]{:S(2)}) copy-start(f32[1,10,32,128]{3,2,1,0:T(8,128)} %anomaly.1) | copy-start | bytes 491524
  2.5 0.9 %copy-start.2 = (f32[10,32,128]{2,1,0:T(8,128)S(1)}, f32[10,32,128]{2,1,0:T(8,128)}, u32[]{:S(2)}) copy-start(f32[10,32,128]{2,1,0:T(8,128)} %lon_faces.1) | copy-start | bytes 491524
  3.4 0.9 %copy-start.3 = (f32[10,32,128]{2,1,0:T(8,128)S(1)}, f32[10,32,128]{2,1,0:T(8,128)}, u32[]{:S(2)}) copy-start(f32[10,32,128]{2,1,0:T(8,128)} %lat_faces.1) | copy-start | bytes 491524
  4.3 0.9 %copy-start.4 = (f32[10,32,128]{2,1,0:T(8,128)S(1)}, f32[10,32,128]{2,1,0:T(8,128)}, u32[]{:S(2)}) copy-start(f32[10,32,128]{2,1,0:T(8,128)} %normalizer.1) | copy-start | bytes 491524
  5.2 0.9 %copy-start.5 = (f32[10,32,128]{2,1,0:T(8,128)S(1)}, f32[10,32,128]{2,1,0:T(8,128)}, u32[]{:S(2)}) copy-start(f32[10,32,128]{2,1,0:T(8,128)} %innovation.1) | copy-start | bytes 491524
  6.1 0.9 %copy-start.6 = (f32[10,32,128]{2,1,0:T(8,128)S(1)}, f32[10,32,128]{2,1,0:T(8,128)}, u32[]{:S(2)}) copy-start(f32[10,32,128]{2,1,0:T(8,128)} %weight.1) | copy-start | bytes 491524
  7.0 0.7 %copy-start.7 = (f32[10,10]{1,0:T(8,128)S(1)}, f32[10,10]{1,0:T(8,128)}, u32[]{:S(2)}) copy-start(f32[10,10]{1,0:T(8,128)} %vertical.3) | copy-start | bytes 1204
  8.6 4.4 %collective-permute-start = (f32[10,32,128]{2,1,0:T(8,128)S(1)}, f32[10,32,128]{2,1,0:T(8,128)S(1)}, u32[]{:S(2)}, u32[]{:S(2)}) collective-permute-start(f32[10,32,128]{2,1,0:T(8,128)S(1)} %get-tuple-element.14), channel_id=1, source_target_pairs={{0,1},{1,0},{2,3},{3,2},{4,5},{5,4},{6,7},{7,6},{8,9},{9,8},{10,11... | collective-permute-start | bytes 491528 | tf_op jit(solution)/shard_map/ppermute | solution.py:26
  13.0 12.0 %collective-permute-start.1 = (f32[440,128]{1,0:T(8,128)S(1)}, f32[440,128]{1,0:T(8,128)S(1)}, u32[]{:S(2)}, u32[]{:S(2)}) collective-permute-start(f32[440,128]{1,0:T(8,128)S(1)} %get-tuple-element.15), channel_id=1, source_target_pairs={{0,16},{16,32},{32,48},{48,64},{64,80},{80,96},{96,112},{112,128},... | collective-permute-start | bytes 675848 | tf_op jit(solution)/shard_map/ppermute | solution.py:26
  14.1 12.7 %collective-permute-start.2 = (f32[440,128]{1,0:T(8,128)S(1)}, f32[440,128]{1,0:T(8,128)S(1)}, u32[]{:S(2)}, u32[]{:S(2)}) collective-permute-start(f32[440,128]{1,0:T(8,128)S(1)} %get-tuple-element.16), channel_id=1, source_target_pairs={{0,240},{16,0},{32,16},{48,32},{64,48},{80,64},{96,80},{112,96},{1... | collective-permute-start | bytes 675848 | tf_op jit(solution)/shard_map/ppermute | solution.py:26
  27.4 6.0 %collective-permute-start.3 = (f32[4,64,128]{2,1,0:T(8,128)S(1)}, f32[4,64,128]{2,1,0:T(8,128)S(1)}, u32[]{:S(2)}, u32[]{:S(2)}) collective-permute-start(f32[4,64,128]{2,1,0:T(8,128)S(1)} %get-tuple-element.19), channel_id=1, source_target_pairs={{0,2},{2,4},{4,6},{6,8},{8,10},{10,12},{12,14},{14,0},{1,3},{3,5},... | collective-permute-start | bytes 393224 | tf_op jit(solution)/shard_map/ppermute | solution.py:26
  27.8 7.0 %collective-permute-start.4 = (f32[4,64,128]{2,1,0:T(8,128)S(1)}, f32[4,64,128]{2,1,0:T(8,128)S(1)}, u32[]{:S(2)}, u32[]{:S(2)}) collective-permute-start(f32[4,64,128]{2,1,0:T(8,128)S(1)} %get-tuple-element.20), channel_id=1, source_target_pairs={{0,14},{2,0},{4,2},{6,4},{8,6},{10,8},{12,10},{14,12},{1,15},{3,1}... | collective-permute-start | bytes 393224 | tf_op jit(solution)/shard_map/ppermute | solution.py:26
  47.4 3.4 %collective-permute-start.5 = (f32[5,32,128]{2,1,0:T(8,128)S(1)}, f32[5,32,128]{2,1,0:T(8,128)S(1)}, u32[]{:S(2)}, u32[]{:S(2)}) collective-permute-start(f32[5,32,128]{2,1,0:T(8,128)S(1)} %get-tuple-element.23), channel_id=1, source_target_pairs={{0,1},{1,0},{2,3},{3,2},{4,5},{5,4},{6,7},{7,6},{8,9},{9,8},{10,11... | collective-permute-start | bytes 245768 | tf_op jit(solution)/shard_map/ppermute | solution.py:26
where the time goes:
time: 52.5 us; the launch traced here: 52.3 us
  starting transfers between devices  16 us (30%)
  Pallas kernels  15.5 us (30%)
  waiting for transfers between devices  13 us (25%)
  local copies, waits for them, and re-layouts  7.1 us (14%)
  between operations  0.67 us (1%)
    ppermute x6, starting transfers between devices, around(): return lax.ppermute(value, axis, pairs)  16 us
    ppermute x6, waiting for transfers between devices, around(): return lax.ppermute(value, axis, pairs)  13 us
    pallas_call x1, Pallas kernels, local(): pl.pallas_call(functools.partial(diffuse_kernel, half), out_shape=(block,...  12.6 us
    unnamed x16, local copies, waits for them, and re-layouts  7.1 us
    pallas_call x1, Pallas kernels, local(): pl.pallas_call(functools.partial(gradient_kernel, half), out_shape=f32(*a...  1.47 us
  transfers between devices with their start and end apart: 6, of which 6 were waited for; matrix products, arithmetic and copies ran while one was open for 0% of the time, Pallas kernels for 0%

commit v1 on v0

v1 whole, which is shorter than its diff:
```python
import functools
import math

import jax
import jax.numpy as jnp
from jax import lax
from jax.experimental import pallas as pl
from jax.experimental.pallas import tpu as pltpu
from jax.sharding import PartitionSpec as P

STEPS = 8
DEEP = 2 * STEPS
LANES = 128
VMEM = pl.BlockSpec(memory_space=pltpu.VMEM)
SMEM = pl.BlockSpec(memory_space=pltpu.SMEM)
HBM = pl.BlockSpec(memory_space=pltpu.HBM)
PARAMS = pltpu.CompilerParams(vmem_limit_bytes=32 * 1024 * 1024)


def f32(*shape):
    return jax.ShapeDtypeStruct(shape, jnp.float32)


def around(value, axis, steps):
    count = lax.axis_size(axis)
    pairs = [(source, (source + steps) % count) for source in range(count)]
    return lax.ppermute(value, axis, pairs)


def diagonal(value, lon_steps, lat_steps):
    lons, lats = lax.axis_size("lon"), lax.axis_size("lat")
    pairs = []
    for i in range(lons):
        for j in range(lats):
            target = ((i + lon_steps) % lons) * lats + (j + lat_steps) % lats
            pairs.append((i * lats + j, target))
    return lax.ppermute(value, ("lon", "lat"), pairs)


def lane_places(count, width):
    return [(i * width // LANES, i * width % LANES) for i in range(count)]


def lane_groups(count, width):
    return -(-count * width // LANES)


def turned(value, shift):
    shift = shift % value.shape[-1]
    return pltpu.roll(value, shift, axis=value.ndim - 1) if shift else value


def mixed(vertical_ref, alpha_ref, level):
    total = vertical_ref[level, 0] * alpha_ref[0, 0]
    for k in range(1, alpha_ref.shape[1]):
        total = total + vertical_ref[level, k] * alpha_ref[0, k]
    return total


def prepare_kernel(
    half,
    vertical_hbm,
    alpha_hbm,
    anomaly_hbm,
    lon_hbm,
    lat_hbm,
    normalizer_hbm,
    innovation_hbm,
    weight_hbm,
    keep,
    give,
    vertical,
    alpha,
    anomaly,
    faces,
    normalizer,
    innovation,
    weight,
    sems,
):
    base = lax.axis_index("mem") * half
    other = half - base
    pairs = [
        (vertical_hbm, vertical),
        (alpha_hbm, alpha),
        (weight_hbm, weight),
        (normalizer_hbm, normalizer),
        (anomaly_hbm, anomaly),
        (innovation_hbm.at[pl.ds(base, half)], innovation),
        (lon_hbm.at[pl.ds(base, half)], keep.at[pl.ds(half, half)]),
        (lat_hbm.at[pl.ds(base, half)], faces),
    ]
    copies = [pltpu.make_async_copy(a, b, sems.at[n]) for n, (a, b) in enumerate(pairs)]
    for copy in copies:
        copy.start()
    copies[0].wait()
    copies[1].wait()
    for i in range(half):
        keep[i] = mixed(vertical, alpha, base + i)
        give[i] = mixed(vertical, alpha, other + i)
    for copy in copies[2:]:
        copy.wait()
    last = lax.axis_index("lat") == lax.axis_size("lat") - 1
    lane = lax.broadcasted_iota(jnp.int32, faces.shape[1:], 1)
    closed = jnp.logical_and(last, lane == faces.shape[2] - 1)
    for i in range(half):
        mine, theirs = base + i, other + i
        root = jnp.sqrt(weight[mine])
        keep[2 * half + i] = jnp.where(closed, 0.0, faces[i])
        keep[3 * half + i] = normalizer[mine] * anomaly[0, mine] * root
        keep[4 * half + i] = root * innovation[i]
        keep[5 * half + i] = 1.0 / root
        give[half + i] = normalizer[theirs] * anomaly[0, theirs] * jnp.sqrt(weight[theirs])


def field_refs(half, keep, got):
    deep = [keep.at[i] for i in range(half)]
    deep += [got.at[i] for i in range(half)]
    deep += [keep.at[half + i] for i in range(2 * half)]
    shallow = [keep.at[3 * half + i] for i in range(half)]
    shallow += [got.at[half + i] for i in range(half)]
    shallow += [keep.at[4 * half + i] for i in range(half)]
    return deep, shallow


def pack_kernel(
    half, keep, got, first, final, west, east, west_first, west_final, east_first, east_final
):
    deep, shallow = field_refs(half, keep, got)
    rows, lanes = keep.shape[1:]
    at = 0
    for width, fields in ((DEEP, deep), (STEPS, shallow)):
        for ref in fields:
            first[at : at + width] = ref[:width]
            final[at : at + width] = ref[rows - width :]
            at += width
    lane = lax.broadcasted_iota(jnp.int32, (1, lanes), 1)
    group = -1
    for width, fields in ((DEEP, deep), (STEPS, shallow)):
        per = lanes // width
        for begin in range(0, len(fields), per):
            group += 1
            heads = tails = jnp.zeros((rows, lanes), jnp.float32)
            for slot, ref in enumerate(fields[begin : begin + per]):
                place = slot * width
                inside = jnp.logical_and(lane >= place, lane < place + width)
                block = ref[...]
                heads = jnp.where(inside, turned(block, place), heads)
                tails = jnp.where(inside, turned(block, place + width), tails)
            west[group] = heads
            east[group] = tails
            at = group * DEEP
            west_first[at : at + width] = heads[:width]
            west_final[at : at + width] = heads[rows - width :]
            east_first[at : at + width] = tails[:width]
            east_final[at : at + width] = tails[rows - width :]


def diffuse_kernel(
    half,
    keep,
    got,
    below,
    above,
    left,
    right,
    left_below,
    left_above,
    right_below,
    right_above,
    increment,
    mine,
    theirs,
    deep_tiles,
    shallow_tiles,
    coef,
    work,
):
    deep, shallow = field_refs(half, keep, got)
    rows, lanes = keep.shape[1:]
    lane = lax.broadcasted_iota(jnp.int32, (1, lanes), 1)
    at = 0
    first_group = 0
    for width, fields, tiles in ((DEEP, deep, deep_tiles), (STEPS, shallow, shallow_tiles)):
        for i, (ref, (group, place)) in enumerate(zip(fields, lane_places(len(fields), width))):
            group += first_group
            corner = group * DEEP
            pieces = (
                (below[at : at + width], left_below, right_below, 0, width),
                (ref[...], left, right, width, rows),
                (above[at : at + width], left_above, right_above, width + rows, width),
            )
            at += width
            for block, lefts, rights, start, count in pieces:
                if lefts is left:
                    before, after = left[group], right[group]
                else:
                    before = lefts[corner : corner + width]
                    after = rights[corner : corner + width]
                before = turned(before, DEEP - width - place)
                after = turned(after, lanes - DEEP - place)
                out = slice(STEPS + start, STEPS + start + count)
                tiles[i, 0, out] = jnp.where(lane < DEEP, before, turned(block, DEEP))
                tiles[i, 1, out] = jnp.where(lane >= lanes - DEEP, after, turned(block, -DEEP))
        first_group += lane_groups(len(fields), width)

    high = rows + 2 * DEEP
    edge = jnp.zeros((STEPS, lanes), jnp.float32)
    for n in range(work.shape[0]):
        for t in range(2):
            work[n, t, :STEPS] = edge
            work[n, t, STEPS + high :] = edge
    for n in range(2 * half):
        for t in range(2):
            deep_tiles[2 * half + n, t, :STEPS] = edge

    def sweep(source, target, begin, count, tile, member):
        def at(shift):
            return work[source + member, tile, pl.ds(STEPS + begin + shift, count)]

        def c(n):
            return coef[n, tile, pl.ds(begin, count)]

        here = at(0)
        work[target + member, tile, pl.ds(STEPS + begin, count)] = (
            (c(0) * here + c(1) * at(1))
            + (c(2) * at(-1) + c(3) * turned(here, -1))
            + c(4) * turned(here, 1)
        )

    def sweeps(margin):
        source, target = 0, 2
        for step in range(1, STEPS + 1):
            cut = (margin + step) // 4 * 4
            for tile in range(2):
                for member in range(2):
                    sweep(source, target, cut, high - 2 * cut, tile, member)
            source, target = target, source

    def level(i, carry):
        for tile in range(2):
            body = pl.ds(STEPS, high)
            north = deep_tiles[2 * half + i, tile, body]
            south = deep_tiles[2 * half + i, tile, pl.ds(STEPS - 1, high)]
            east = deep_tiles[3 * half + i, tile, body]
            west = turned(east, 1)
            coef[0, tile] = 1.0 - ((north + south) + (east + west))
            coef[1, tile] = north
            coef[2, tile] = south
            coef[3, tile] = east
            coef[4, tile] = west
            for member in range(2):
                work[member, tile, body] = deep_tiles[member * half + i, tile, body]
        sweeps(0)
        inner = pl.ds(2 * STEPS, high - 2 * STEPS)
        shallow_rows = pl.ds(STEPS, high - 2 * STEPS)
        center = slice(STEPS, STEPS + rows)
        totals = []
        for tile in range(2):
            gains = [shallow_tiles[m * half + i, tile, shallow_rows] for m in range(2)]
            total = gains[0] * work[0, tile, inner] + gains[1] * work[1, tile, inner]
            totals.append(total[center])
            residual = total - shallow_tiles[2 * half + i, tile, shallow_rows]
            for member in range(2):
                work[member, tile, inner] = gains[member] * residual
        joined = lane < lanes // 2
        total = jnp.where(joined, turned(totals[0], -DEEP), turned(totals[1], DEEP))
        increment[i] = total * keep[5 * half + i]
        sweeps(STEPS)
        own = pl.ds(STEPS + DEEP, rows)
        for member, out in enumerate((mine, theirs)):
            parts = [work[member, tile, own] for tile in range(2)]
            out[i] = jnp.where(joined, turned(parts[0], -DEEP), turned(parts[1], DEEP))
        return carry

    lax.fori_loop(0, half, level, 0)


def gradient_kernel(half, vertical, alpha, mine, got, gradient):
    base = lax.axis_index("mem") * half
    other = half - base
    for k in range(2 * half):
        total = alpha[0, k]
        for i in range(half):
            total = total + vertical[base + i, k] * mine[i]
            total = total + vertical[other + i, k] * got[i]
        gradient[0, k] = total


def local(
    alpha_fields, anomalies, lon_faces, lat_faces, normalizer, innovation, misfit_weight, vertical
):
    levels, rows, lanes = lon_faces.shape
    half = levels // 2
    deep_count, shallow_count = 4 * half, 3 * half
    deep_groups = lane_groups(deep_count, DEEP)
    groups = deep_groups + lane_groups(shallow_count, STEPS)
    strip = f32(DEEP * deep_count + STEPS * shallow_count, lanes)
    column = f32(groups, rows, lanes)
    corner = f32(DEEP * deep_groups + STEPS * (groups - deep_groups), lanes)
    block = f32(half, rows, lanes)
    high = rows + 2 * DEEP

    keep, give = pl.pallas_call(
        functools.partial(prepare_kernel, half),
        out_shape=(f32(6 * half, rows, lanes), f32(levels, rows, lanes)),
        in_specs=[HBM] * 8,
        out_specs=(VMEM, VMEM),
        scratch_shapes=[
            pltpu.SMEM(vertical.shape, jnp.float32),
            pltpu.VMEM(alpha_fields.shape, jnp.float32),
            pltpu.VMEM(anomalies.shape, jnp.float32),
            pltpu.VMEM(block.shape, jnp.float32),
            pltpu.VMEM(normalizer.shape, jnp.float32),
            pltpu.VMEM(block.shape, jnp.float32),
            pltpu.VMEM(misfit_weight.shape, jnp.float32),
            pltpu.SemaphoreType.DMA((8,)),
        ],
        compiler_params=PARAMS,
        name="prepare",
    )(vertical, alpha_fields, anomalies, lon_faces, lat_faces, normalizer, innovation, misfit_weight)
    got = around(give, "mem", 1)

    first, final, west, east, west_first, west_final, east_first, east_final = pl.pallas_call(
        functools.partial(pack_kernel, half),
        out_shape=(strip, strip, column, column, corner, corner, corner, corner),
        in_specs=[VMEM] * 2,
        out_specs=(VMEM,) * 8,
        compiler_params=PARAMS,
        name="pack",
    )(keep, got)
    below = around(final, "lon", 1)
    above = around(first, "lon", -1)
    left = around(east, "lat", 1)
    right = around(west, "lat", -1)
    left_below = diagonal(east_final, 1, 1)
    left_above = diagonal(east_first, -1, 1)
    right_below = diagonal(west_final, 1, -1)
    right_above = diagonal(west_first, -1, -1)

    increment, mine, theirs = pl.pallas_call(
        functools.partial(diffuse_kernel, half),
        out_shape=(block, block, block),
        in_specs=[VMEM] * 10,
        out_specs=(VMEM,) * 3,
        scratch_shapes=[
            pltpu.VMEM((deep_count, 2, STEPS + high, lanes), jnp.float32),
            pltpu.VMEM((shallow_count, 2, high, lanes), jnp.float32),
            pltpu.VMEM((5, 2, high, lanes), jnp.float32),
            pltpu.VMEM((4, 2, high + 2 * STEPS, lanes), jnp.float32),
        ],
        compiler_params=PARAMS,
        name="diffuse",
    )(keep, got, below, above, left, right, left_below, left_above, right_below, right_above)
    got = around(theirs, "mem", 1)

    gradient = pl.pallas_call(
        functools.partial(gradient_kernel, half),
        out_shape=f32(*alpha_fields.shape),
        in_specs=[SMEM] + [VMEM] * 3,
        out_specs=VMEM,
        compiler_params=PARAMS,
        name="gradient",
    )(vertical, alpha_fields, mine, got)
    return (increment, gradient)


def solution(mesh):
    return jax.shard_map(
        local,
        mesh=mesh,
        in_specs=(
            P("mem", None, "lon", "lat"),
            P("mem", None, "lon", "lat"),
            P(None, "lon", "lat"),
            P(None, "lon", "lat"),
            P(None, "lon", "lat"),
            P(None, "lon", "lat"),
            P(None, "lon", "lat"),
            P(),
        ),
        out_specs=(P("mem", "lon", "lat"), P("mem", None, "lon", "lat")),
        check_vma=False,
    )
```

time: 52.5 us -> 60.3 us (1.15)
  starting transfers between devices: 16 us -> 24.8 us
  Pallas kernels: 15.5 us -> 13 us
  waiting for transfers between devices: 13 us -> 14.4 us
    ppermute x0 -> x4, waiting for transfers between devices: none -> 12.5 us  [diagonal(): return lax.ppermute(value, ('lon', 'lat'), pairs)]
    ppermute x0 -> x4, starting transfers between devices: none -> 11.3 us  [diagonal(): return lax.ppermute(value, ('lon', 'lat'), pairs)]
    ppermute x6, waiting for transfers between devices: 13 us -> 1.96 us  [around(): return lax.ppermute(value, axis, pairs)]
    pallas_call x1, Pallas kernels: 12.6 us -> 9.75 us  [local(): pl.pallas_call(functools.partial(diffuse_kernel, half), out_shape=(block,...]
    ppermute x6, starting transfers between devices: 16 us -> 13.6 us  [around(): return lax.ppermute(value, axis, pairs)]
  transfers between devices with their start and end apart: 6 -> 10, of which waited for: 6 -> 6; matrix products, arithmetic and copies ran while one was open for 0% -> 0% of each run, Pallas kernels for 0% -> 0%
where the time goes in v1:
time: 60.3 us; the launch traced here: 60 us
  starting transfers between devices  24.8 us (41%)
  waiting for transfers between devices  14.4 us (24%)
  Pallas kernels  13 us (22%)
  local copies, waits for them, and re-layouts  7.1 us (12%)
  between operations  0.69 us (1%)
    ppermute x6, starting transfers between devices, around(): return lax.ppermute(value, axis, pairs)  13.6 us
    ppermute x4, waiting for transfers between devices, diagonal(): return lax.ppermute(value, ('lon', 'lat'), pairs)  12.5 us
    ppermute x4, starting transfers between devices, diagonal(): return lax.ppermute(value, ('lon', 'lat'), pairs)  11.3 us
    pallas_call x1, Pallas kernels, local(): pl.pallas_call(functools.partial(diffuse_kernel, half), out_shape=(block,...  9.75 us
    unnamed x16, local copies, waits for them, and re-layouts  7.1 us
    ppermute x6, waiting for transfers between devices, around(): return lax.ppermute(value, axis, pairs)  1.96 us
    pallas_call x1, Pallas kernels, local(): pl.pallas_call(functools.partial(gradient_kernel, half), out_shape=f32(*a...  1.47 us
    pallas_call x1, Pallas kernels, local(): pl.pallas_call(functools.partial(prepare_kernel, half), out_shape=(f32(6...  1.4 us
  transfers between devices with their start and end apart: 10, of which 6 were waited for; matrix products, arithmetic and copies ran while one was open for 0% of the time, Pallas kernels for 0%

profile of v1, /device:TPU:1, one launch (start us, length us, event | category | flops | bytes accessed | tf_op | source)
XLA Modules:
  0.0 60.0 jit_solution(11205736790526926841)
XLA Ops:
  0.6 0.0 copy-start
  0.6 0.9 %copy-done = f32[1,10,32,128]{3,2,1,0:T(8,128)S(1)} copy-done((f32[1,10,32,128]{3,2,1,0:T(8,128)S(1)}, f32[1,10,32,128]{3,2,1,0:T(8,128)}, u32[]{:S(2)}) %copy-start) | copy-done | bytes 163864
  1.5 0.0 copy-start.1
  1.6 0.9 %copy-done.1 = f32[1,10,32,128]{3,2,1,0:T(8,128)S(1)} copy-done((f32[1,10,32,128]{3,2,1,0:T(8,128)S(1)}, f32[1,10,32,128]{3,2,1,0:T(8,128)}, u32[]{:S(2)}) %copy-start.1) | copy-done | bytes 163864
  2.5 0.0 copy-start.2
  2.5 0.9 %copy-done.2 = f32[10,32,128]{2,1,0:T(8,128)S(1)} copy-done((f32[10,32,128]{2,1,0:T(8,128)S(1)}, f32[10,32,128]{2,1,0:T(8,128)}, u32[]{:S(2)}) %copy-start.2) | copy-done | bytes 163864
  3.4 0.0 copy-start.3
  3.4 0.9 %copy-done.3 = f32[10,32,128]{2,1,0:T(8,128)S(1)} copy-done((f32[10,32,128]{2,1,0:T(8,128)S(1)}, f32[10,32,128]{2,1,0:T(8,128)}, u32[]{:S(2)}) %copy-start.3) | copy-done | bytes 163864
  4.3 0.0 copy-start.4
  4.3 0.9 %copy-done.4 = f32[10,32,128]{2,1,0:T(8,128)S(1)} copy-done((f32[10,32,128]{2,1,0:T(8,128)S(1)}, f32[10,32,128]{2,1,0:T(8,128)}, u32[]{:S(2)}) %copy-start.4) | copy-done | bytes 163864
  5.2 0.0 copy-start.5
  5.2 0.9 %copy-done.5 = f32[10,32,128]{2,1,0:T(8,128)S(1)} copy-done((f32[10,32,128]{2,1,0:T(8,128)S(1)}, f32[10,32,128]{2,1,0:T(8,128)}, u32[]{:S(2)}) %copy-start.5) | copy-done | bytes 163864
  6.1 0.0 copy-start.6
  6.1 0.9 %copy-done.6 = f32[10,32,128]{2,1,0:T(8,128)S(1)} copy-done((f32[10,32,128]{2,1,0:T(8,128)S(1)}, f32[10,32,128]{2,1,0:T(8,128)}, u32[]{:S(2)}) %copy-start.6) | copy-done | bytes 163864
  7.0 0.0 copy-start.7
  7.0 0.7 %copy-done.7 = f32[10,10]{1,0:T(8,128)S(1)} copy-done((f32[10,10]{1,0:T(8,128)S(1)}, f32[10,10]{1,0:T(8,128)}, u32[]{:S(2)}) %copy-start.7) | copy-done | bytes 424
  7.7 1.4 %prepare.1 = (f32[30,32,128]{2,1,0:T(8,128)S(1)}, f32[10,32,128]{2,1,0:T(8,128)S(1)}) custom-call(f32[10,10]{1,0:T(8,128)S(1)} %copy-done.7, f32[1,10,32,128]{3,2,1,0:T(8,128)S(1)} %copy-done, f32[1,10,32,128]{3,2,1,0:T(8,128)S(1)} %copy-done.1, f32[10,32,128]{2,1,0:T(8,128)S(1)} %copy-done.2, f32[10,32,128]{2,1,0:T(8,128)S(1)} %copy-done.3, ...), custom_call_target="tpu_custom_call" | custom-call | tf_op jit(solution)/shard_map/prepare/pallas_call | solution.py:304
  9.2 3.3 %collective-permute-start = (f32[10,32,128]{2,1,0:T(8,128)S(1)}, f32[10,32,128]{2,1,0:T(8,128)S(1)}, u32[]{:S(2)}, u32[]{:S(2)}) collective-permute-start(f32[10,32,128]{2,1,0:T(8,128)S(1)} %get-tuple-element.16), channel_id=1, source_target_pairs={{0,1},{1,0},{2,3},{3,2},{4,5},{5,4},{6,7},{7,6},{8,9},{9,8},{10,11... | collective-permute-start | bytes 491528 | tf_op jit(solution)/shard_map/ppermute | solution.py:27
  12.5 1.0 %collective-permute-done.got = f32[10,32,128]{2,1,0:T(8,128)S(1)} collective-permute-done((f32[10,32,128]{2,1,0:T(8,128)S(1)}, f32[10,32,128]{2,1,0:T(8,128)S(1)}, u32[]{:S(2)}, u32[]{:S(2)}) %collective-permute-start) | collective-permute-done | bytes 163872 | tf_op jit(solution)/shard_map/ppermute | solution.py:27
  13.5 0.3 pack.1
  13.9 1.1 %collective-permute-start.1 = (f32[440,128]{1,0:T(8,128)S(1)}, f32[440,128]{1,0:T(8,128)S(1)}, u32[]{:S(2)}, u32[]{:S(2)}) collective-permute-start(f32[440,128]{1,0:T(8,128)S(1)} %get-tuple-element.17), channel_id=1, source_target_pairs={{0,16},{16,32},{32,48},{48,64},{64,80},{80,96},{96,112},{112,128},... | collective-permute-start | bytes 675848 | tf_op jit(solution)/shard_map/ppermute | solution.py:27
  14.9 5.4 %collective-permute-start.2 = (f32[440,128]{1,0:T(8,128)S(1)}, f32[440,128]{1,0:T(8,128)S(1)}, u32[]{:S(2)}, u32[]{:S(2)}) collective-permute-start(f32[440,128]{1,0:T(8,128)S(1)} %get-tuple-element.18), channel_id=1, source_target_pairs={{0,240},{16,0},{32,16},{48,32},{64,48},{80,64},{96,80},{112,96},{1... | collective-permute-start | bytes 675848 | tf_op jit(solution)/shard_map/ppermute | solution.py:27
  20.3 0.0 collective-permute-start.5
  20.3 5.8 %collective-permute-start.6 = (f32[56,128]{1,0:T(8,128)S(1)}, f32[56,128]{1,0:T(8,128)S(1)}, u32[]{:S(2)}, u32[]{:S(2)}) collective-permute-start(f32[56,128]{1,0:T(8,128)S(1)} %get-tuple-element.22), channel_id=1, source_target_pairs={{0,242},{2,244},{4,246},{6,248},{8,250},{10,252},{12,254},{14,240}... | collective-permute-start | bytes 86024 | tf_op jit(solution)/shard_map/ppermute | solution.py:37
  26.1 0.0 collective-permute-start.3
  26.1 2.8 %collective-permute-done.5.left_below = f32[56,128]{1,0:T(8,128)S(1)} collective-permute-done((f32[56,128]{1,0:T(8,128)S(1)}, f32[56,128]{1,0:T(8,128)S(1)}, u32[]{:S(2)}, u32[]{:S(2)}) %collective-permute-start.5) | collective-permute-done | bytes 28704 | tf_op jit(solution)/shard_map/ppermute | solution.py:37
  28.9 0.8 %collective-permute-start.4 = (f32[4,32,128]{2,1,0:T(8,128)S(1)}, f32[4,32,128]{2,1,0:T(8,128)S(1)}, u32[]{:S(2)}, u32[]{:S(2)}) collective-permute-start(f32[4,32,128]{2,1,0:T(8,128)S(1)} %get-tuple-element.20), channel_id=1, source_target_pairs={{0,14},{2,0},{4,2},{6,4},{8,6},{10,8},{12,10},{14,12},{1,15},{3,1}... | collective-permute-start | bytes 196616 | tf_op jit(solution)/shard_map/ppermute | solution.py:27
  29.7 2.7 %collective-permute-done.6.left_above = f32[56,128]{1,0:T(8,128)S(1)} collective-permute-done((f32[56,128]{1,0:T(8,128)S(1)}, f32[56,128]{1,0:T(8,128)S(1)}, u32[]{:S(2)}, u32[]{:S(2)}) %collective-permute-start.6) | collective-permute-done | bytes 28704 | tf_op jit(solution)/shard_map/ppermute | solution.py:37
  32.4 0.5 collective-permute-start.7
  32.9 6.0 %collective-permute-done.7.right_below = f32[56,128]{1,0:T(8,128)S(1)} collective-permute-done((f32[56,128]{1,0:T(8,128)S(1)}, f32[56,128]{1,0:T(8,128)S(1)}, u32[]{:S(2)}, u32[]{:S(2)}) %collective-permute-start.7) | collective-permute-done | bytes 28704 | tf_op jit(solution)/shard_map/ppermute | solution.py:37
  38.9 5.0 %collective-permute-start.8 = (f32[56,128]{1,0:T(8,128)S(1)}, f32[56,128]{1,0:T(8,128)S(1)}, u32[]{:S(2)}, u32[]{:S(2)}) collective-permute-start(f32[56,128]{1,0:T(8,128)S(1)} %get-tuple-element.24), channel_id=1, source_target_pairs={{0,254},{2,240},{4,242},{6,244},{8,246},{10,248},{12,250},{14,252}... | collective-permute-start | bytes 86024 | tf_op jit(solution)/shard_map/ppermute | solution.py:37
  43.9 1.0 %collective-permute-done.8.right_above = f32[56,128]{1,0:T(8,128)S(1)} collective-permute-done((f32[56,128]{1,0:T(8,128)S(1)}, f32[56,128]{1,0:T(8,128)S(1)}, u32[]{:S(2)}, u32[]{:S(2)}) %collective-permute-start.8) | collective-permute-done | bytes 28704 | tf_op jit(solution)/shard_map/ppermute | solution.py:37
  44.9 0.0 collective-permute-done.3.left
  44.9 0.0 collective-permute-done.4.right
  44.9 0.0 collective-permute-done.1.below
  44.9 0.0 collective-permute-done.2.above
  44.9 9.7 %diffuse.1 = (f32[5,32,128]{2,1,0:T(8,128)}, f32[5,32,128]{2,1,0:T(8,128)S(1)}, f32[5,32,128]{2,1,0:T(8,128)S(1)}) custom-call(f32[30,32,128]{2,1,0:T(8,128)S(1)} %get-tuple-element.15.keep, f32[10,32,128]{2,1,0:T(8,128)S(1)} %collective-permute-done.got, f32[440,128]{1,0:T(8,128)S(1)} %collective-permute-done.1.below, ...), custom_call_target="tpu_custom_call" | custom-call | tf_op jit(solution)/shard_map/diffuse/pallas_call | solution.py:341
  54.7 3.0 %collective-permute-start.9 = (f32[5,32,128]{2,1,0:T(8,128)S(1)}, f32[5,32,128]{2,1,0:T(8,128)S(1)}, u32[]{:S(2)}, u32[]{:S(2)}) collective-permute-start(f32[5,32,128]{2,1,0:T(8,128)S(1)} %get-tuple-element.27), channel_id=1, source_target_pairs={{0,1},{1,0},{2,3},{3,2},{4,5},{5,4},{6,7},{7,6},{8,9},{9,8},{10,11... | collective-permute-start | bytes 245768 | tf_op jit(solution)/shard_map/ppermute | solution.py:27
  57.6 0.9 %collective-permute-done.9.got = f32[5,32,128]{2,1,0:T(8,128)S(1)} collective-permute-done((f32[5,32,128]{2,1,0:T(8,128)S(1)}, f32[5,32,128]{2,1,0:T(8,128)S(1)}, u32[]{:S(2)}, u32[]{:S(2)}) %collective-permute-start.9) | collective-permute-done | bytes 81952 | tf_op jit(solution)/shard_map/ppermute | solution.py:27
  58.6 1.5 %gradient.1 = f32[1,10,32,128]{3,2,1,0:T(8,128)} custom-call(f32[10,10]{1,0:T(8,128)S(1)} %copy-done.7, f32[1,10,32,128]{3,2,1,0:T(8,128)S(1)} %copy-done, f32[5,32,128]{2,1,0:T(8,128)S(1)} %get-tuple-element.26.mine, f32[5,32,128]{2,1,0:T(8,128)S(1)} %collective-permute-done.9.got), custom_call_target="tpu_custom_call" | custom-call | tf_op jit(solution)/shard_map/gradient/pallas_call | solution.py:357
Async XLA Ops:
  0.6 0.9 %copy-start = (f32[1,10,32,128]{3,2,1,0:T(8,128)S(1)}, f32[1,10,32,128]{3,2,1,0:T(8,128)}, u32[]{:S(2)}) copy-start(f32[1,10,32,128]{3,2,1,0:T(8,128)} %alpha.1) | copy-start | bytes 491524
  1.5 0.9 %copy-start.1 = (f32[1,10,32,128]{3,2,1,0:T(8,128)S(1)}, f32[1,10,32,128]{3,2,1,0:T(8,128)}, u32[]{:S(2)}) copy-start(f32[1,10,32,128]{3,2,1,0:T(8,128)} %anomaly_hbm.1) | copy-start | bytes 491524
  2.5 0.9 %copy-start.2 = (f32[10,32,128]{2,1,0:T(8,128)S(1)}, f32[10,32,128]{2,1,0:T(8,128)}, u32[]{:S(2)}) copy-start(f32[10,32,128]{2,1,0:T(8,128)} %lon_hbm.1) | copy-start | bytes 491524
  3.4 0.9 %copy-start.3 = (f32[10,32,128]{2,1,0:T(8,128)S(1)}, f32[10,32,128]{2,1,0:T(8,128)}, u32[]{:S(2)}) copy-start(f32[10,32,128]{2,1,0:T(8,128)} %lat_hbm.1) | copy-start | bytes 491524
  4.3 0.9 %copy-start.4 = (f32[10,32,128]{2,1,0:T(8,128)S(1)}, f32[10,32,128]{2,1,0:T(8,128)}, u32[]{:S(2)}) copy-start(f32[10,32,128]{2,1,0:T(8,128)} %normalizer_hbm.1) | copy-start | bytes 491524
  5.2 0.9 %copy-start.5 = (f32[10,32,128]{2,1,0:T(8,128)S(1)}, f32[10,32,128]{2,1,0:T(8,128)}, u32[]{:S(2)}) copy-start(f32[10,32,128]{2,1,0:T(8,128)} %innovation_hbm.1) | copy-start | bytes 491524
  6.1 0.9 %copy-start.6 = (f32[10,32,128]{2,1,0:T(8,128)S(1)}, f32[10,32,128]{2,1,0:T(8,128)}, u32[]{:S(2)}) copy-start(f32[10,32,128]{2,1,0:T(8,128)} %weight_hbm.1) | copy-start | bytes 491524
  7.0 0.7 %copy-start.7 = (f32[10,10]{1,0:T(8,128)S(1)}, f32[10,10]{1,0:T(8,128)}, u32[]{:S(2)}) copy-start(f32[10,10]{1,0:T(8,128)} %vertical.1) | copy-start | bytes 1204
  9.2 4.4 %collective-permute-start = (f32[10,32,128]{2,1,0:T(8,128)S(1)}, f32[10,32,128]{2,1,0:T(8,128)S(1)}, u32[]{:S(2)}, u32[]{:S(2)}) collective-permute-start(f32[10,32,128]{2,1,0:T(8,128)S(1)} %get-tuple-element.16), channel_id=1, source_target_pairs={{0,1},{1,0},{2,3},{3,2},{4,5},{5,4},{6,7},{7,6},{8,9},{9,8},{10,11... | collective-permute-start | bytes 491528 | tf_op jit(solution)/shard_map/ppermute | solution.py:27
  13.9 31.0 %collective-permute-start.1 = (f32[440,128]{1,0:T(8,128)S(1)}, f32[440,128]{1,0:T(8,128)S(1)}, u32[]{:S(2)}, u32[]{:S(2)}) collective-permute-start(f32[440,128]{1,0:T(8,128)S(1)} %get-tuple-element.17), channel_id=1, source_target_pairs={{0,16},{16,32},{32,48},{48,64},{64,80},{80,96},{96,112},{112,128},... | collective-permute-start | bytes 675848 | tf_op jit(solution)/shard_map/ppermute | solution.py:27
  14.9 30.0 %collective-permute-start.2 = (f32[440,128]{1,0:T(8,128)S(1)}, f32[440,128]{1,0:T(8,128)S(1)}, u32[]{:S(2)}, u32[]{:S(2)}) collective-permute-start(f32[440,128]{1,0:T(8,128)S(1)} %get-tuple-element.18), channel_id=1, source_target_pairs={{0,240},{16,0},{32,16},{48,32},{64,48},{80,64},{96,80},{112,96},{1... | collective-permute-start | bytes 675848 | tf_op jit(solution)/shard_map/ppermute | solution.py:27
  20.3 8.6 %collective-permute-start.5 = (f32[56,128]{1,0:T(8,128)S(1)}, f32[56,128]{1,0:T(8,128)S(1)}, u32[]{:S(2)}, u32[]{:S(2)}) collective-permute-start(f32[56,128]{1,0:T(8,128)S(1)} %get-tuple-element.21), channel_id=1, source_target_pairs={{0,18},{2,20},{4,22},{6,24},{8,26},{10,28},{12,30},{14,16},{16,34}... | collective-permute-start | bytes 86024 | tf_op jit(solution)/shard_map/ppermute | solution.py:37
  20.3 12.1 %collective-permute-start.6 = (f32[56,128]{1,0:T(8,128)S(1)}, f32[56,128]{1,0:T(8,128)S(1)}, u32[]{:S(2)}, u32[]{:S(2)}) collective-permute-start(f32[56,128]{1,0:T(8,128)S(1)} %get-tuple-element.22), channel_id=1, source_target_pairs={{0,242},{2,244},{4,246},{6,248},{8,250},{10,252},{12,254},{14,240}... | collective-permute-start | bytes 86024 | tf_op jit(solution)/shard_map/ppermute | solution.py:37
  26.1 18.8 %collective-permute-start.3 = (f32[4,32,128]{2,1,0:T(8,128)S(1)}, f32[4,32,128]{2,1,0:T(8,128)S(1)}, u32[]{:S(2)}, u32[]{:S(2)}) collective-permute-start(f32[4,32,128]{2,1,0:T(8,128)S(1)} %get-tuple-element.19), channel_id=1, source_target_pairs={{0,2},{2,4},{4,6},{6,8},{8,10},{10,12},{12,14},{14,0},{1,3},{3,5},... | collective-permute-start | bytes 196616 | tf_op jit(solution)/shard_map/ppermute | solution.py:27
  28.9 16.0 %collective-permute-start.4 = (f32[4,32,128]{2,1,0:T(8,128)S(1)}, f32[4,32,128]{2,1,0:T(8,128)S(1)}, u32[]{:S(2)}, u32[]{:S(2)}) collective-permute-start(f32[4,32,128]{2,1,0:T(8,128)S(1)} %get-tuple-element.20), channel_id=1, source_target_pairs={{0,14},{2,0},{4,2},{6,4},{8,6},{10,8},{12,10},{14,12},{1,15},{3,1}... | collective-permute-start | bytes 196616 | tf_op jit(solution)/shard_map/ppermute | solution.py:27
  32.4 6.5 %collective-permute-start.7 = (f32[56,128]{1,0:T(8,128)S(1)}, f32[56,128]{1,0:T(8,128)S(1)}, u32[]{:S(2)}, u32[]{:S(2)}) collective-permute-start(f32[56,128]{1,0:T(8,128)S(1)} %get-tuple-element.23), channel_id=1, source_target_pairs={{0,30},{2,16},{4,18},{6,20},{8,22},{10,24},{12,26},{14,28},{16,46}... | collective-permute-start | bytes 86024 | tf_op jit(solution)/shard_map/ppermute | solution.py:37
  38.9 6.0 %collective-permute-start.8 = (f32[56,128]{1,0:T(8,128)S(1)}, f32[56,128]{1,0:T(8,128)S(1)}, u32[]{:S(2)}, u32[]{:S(2)}) collective-permute-start(f32[56,128]{1,0:T(8,128)S(1)} %get-tuple-element.24), channel_id=1, source_target_pairs={{0,254},{2,240},{4,242},{6,244},{8,246},{10,248},{12,250},{14,252}... | collective-permute-start | bytes 86024 | tf_op jit(solution)/shard_map/ppermute | solution.py:37
  54.7 3.9 %collective-permute-start.9 = (f32[5,32,128]{2,1,0:T(8,128)S(1)}, f32[5,32,128]{2,1,0:T(8,128)S(1)}, u32[]{:S(2)}, u32[]{:S(2)}) collective-permute-start(f32[5,32,128]{2,1,0:T(8,128)S(1)} %get-tuple-element.27), channel_id=1, source_target_pairs={{0,1},{1,0},{2,3},{3,2},{4,5},{5,4},{6,7},{7,6},{8,9},{9,8},{10,11... | collective-permute-start | bytes 245768 | tf_op jit(solution)/shard_map/ppermute | solution.py:27

commit v2 on v1

--- a/solution.py
+++ b/solution.py
@@ -25,16 +25,6 @@
     count = lax.axis_size(axis)
     pairs = [(source, (source + steps) % count) for source in range(count)]
     return lax.ppermute(value, axis, pairs)
-
-
-def diagonal(value, lon_steps, lat_steps):
-    lons, lats = lax.axis_size("lon"), lax.axis_size("lat")
-    pairs = []
-    for i in range(lons):
-        for j in range(lats):
-            target = ((i + lon_steps) % lons) * lats + (j + lat_steps) % lats
-            pairs.append((i * lats + j, target))
-    return lax.ppermute(value, ("lon", "lat"), pairs)
 
 
 def lane_places(count, width):
@@ -69,8 +59,8 @@
     weight_hbm,
     keep,
     give,
+    alpha,
     vertical,
-    alpha,
     anomaly,
     faces,
     normalizer,
@@ -123,9 +113,7 @@
     return deep, shallow
 
 
-def pack_kernel(
-    half, keep, got, first, final, west, east, west_first, west_final, east_first, east_final
-):
+def pack_kernel(half, keep, got, first, final, west, east):
     deep, shallow = field_refs(half, keep, got)
     rows, lanes = keep.shape[1:]
     at = 0
@@ -149,11 +137,17 @@
                 tails = jnp.where(inside, turned(block, place + width), tails)
             west[group] = heads
             east[group] = tails
-            at = group * DEEP
-            west_first[at : at + width] = heads[:width]
-            west_final[at : at + width] = heads[rows - width :]
-            east_first[at : at + width] = tails[:width]
-            east_final[at : at + width] = tails[rows - width :]
+
+
+def corner_kernel(deep_groups, left, right, first, final):
+    groups, rows = left.shape[:2]
+    at = 0
+    for column in (left, right):
+        for group in range(groups):
+            width = DEEP if group < deep_groups else STEPS
+            first[at : at + width] = column[group, :width]
+            final[at : at + width] = column[group, rows - width :]
+            at += width
 
 
 def diffuse_kernel(
@@ -164,39 +158,38 @@
     above,
     left,
     right,
-    left_below,
-    left_above,
-    right_below,
-    right_above,
+    corner_below,
+    corner_above,
     increment,
     mine,
     theirs,
     deep_tiles,
     shallow_tiles,
-    coef,
     work,
+    flux,
 ):
     deep, shallow = field_refs(half, keep, got)
     rows, lanes = keep.shape[1:]
     lane = lax.broadcasted_iota(jnp.int32, (1, lanes), 1)
     at = 0
     first_group = 0
+    right_corner = corner_below.shape[0] // 2
     for width, fields, tiles in ((DEEP, deep, deep_tiles), (STEPS, shallow, shallow_tiles)):
         for i, (ref, (group, place)) in enumerate(zip(fields, lane_places(len(fields), width))):
             group += first_group
             corner = group * DEEP
             pieces = (
-                (below[at : at + width], left_below, right_below, 0, width),
-                (ref[...], left, right, width, rows),
-                (above[at : at + width], left_above, right_above, width + rows, width),
+                (below[at : at + width], corner_below, 0, width),
+                (ref[...], None, width, rows),
+                (above[at : at + width], corner_above, width + rows, width),
             )
             at += width
-            for block, lefts, rights, start, count in pieces:
-                if lefts is left:
+            for block, corners, start, count in pieces:
+                if corners is None:
                     before, after = left[group], right[group]
                 else:
-                    before = lefts[corner : corner + width]
-                    after = rights[corner : corner + width]
+                    before = corners[corner : corner + width]
+                    after = corners[right_corner + corner : right_corner + corner + width]
                 before = turned(before, DEEP - width - place)
                 after = turned(after, lanes - DEEP - place)
                 out = slice(STEPS + start, STEPS + start + count)
@@ -206,52 +199,39 @@
 
     high = rows + 2 * DEEP
     edge = jnp.zeros((STEPS, lanes), jnp.float32)
-    for n in range(work.shape[0]):
+    for n in range(2):
         for t in range(2):
             work[n, t, :STEPS] = edge
             work[n, t, STEPS + high :] = edge
-    for n in range(2 * half):
-        for t in range(2):
-            deep_tiles[2 * half + n, t, :STEPS] = edge
-
-    def sweep(source, target, begin, count, tile, member):
-        def at(shift):
-            return work[source + member, tile, pl.ds(STEPS + begin + shift, count)]
-
-        def c(n):
-            return coef[n, tile, pl.ds(begin, count)]
-
-        here = at(0)
-        work[target + member, tile, pl.ds(STEPS + begin, count)] = (
-            (c(0) * here + c(1) * at(1))
-            + (c(2) * at(-1) + c(3) * turned(here, -1))
-            + c(4) * turned(here, 1)
-        )
-
-    def sweeps(margin):
-        source, target = 0, 2
-        for step in range(1, STEPS + 1):
-            cut = (margin + step) // 4 * 4
+            flux[n, t, :STEPS] = edge
+
+    def sweeps(i, margin):
+        half_steps = STEPS // 2
+        for begin in (margin, margin + half_steps):
+            count = high - 2 * begin
+            body = pl.ds(STEPS + begin, count)
             for tile in range(2):
+                lon_coef = deep_tiles[2 * half + i, tile, body]
+                lat_coef = deep_tiles[3 * half + i, tile, body]
                 for member in range(2):
-                    sweep(source, target, cut, high - 2 * cut, tile, member)
-            source, target = target, source
+                    field = work[member, tile, body]
+                    for step in range(half_steps):
+                        if step:
+                            work[member, tile, body] = field
+                        north = work[member, tile, pl.ds(STEPS + begin + 1, count)]
+                        flux_x = lon_coef * (north - field)
+                        flux[member, tile, body] = flux_x
+                        south = flux[member, tile, pl.ds(STEPS + begin - 1, count)]
+                        flux_y = lat_coef * (turned(field, -1) - field)
+                        field = (field + (flux_x - south)) + (flux_y - turned(flux_y, 1))
+                    work[member, tile, body] = field
 
     def level(i, carry):
         for tile in range(2):
             body = pl.ds(STEPS, high)
-            north = deep_tiles[2 * half + i, tile, body]
-            south = deep_tiles[2 * half + i, tile, pl.ds(STEPS - 1, high)]
-            east = deep_tiles[3 * half + i, tile, body]
-            west = turned(east, 1)
-            coef[0, tile] = 1.0 - ((north + south) + (east + west))
-            coef[1, tile] = north
-            coef[2, tile] = south
-            coef[3, tile] = east
-            coef[4, tile] = west
             for member in range(2):
                 work[member, tile, body] = deep_tiles[member * half + i, tile, body]
-        sweeps(0)
+        sweeps(i, 0)
         inner = pl.ds(2 * STEPS, high - 2 * STEPS)
         shallow_rows = pl.ds(STEPS, high - 2 * STEPS)
         center = slice(STEPS, STEPS + rows)
@@ -266,7 +246,7 @@
         joined = lane < lanes // 2
         total = jnp.where(joined, turned(totals[0], -DEEP), turned(totals[1], DEEP))
         increment[i] = total * keep[5 * half + i]
-        sweeps(STEPS)
+        sweeps(i, STEPS)
         own = pl.ds(STEPS + DEEP, rows)
         for member, out in enumerate((mine, theirs)):
             parts = [work[member, tile, own] for tile in range(2)]
@@ -297,18 +277,27 @@
     groups = deep_groups + lane_groups(shallow_count, STEPS)
     strip = f32(DEEP * deep_count + STEPS * shallow_count, lanes)
     column = f32(groups, rows, lanes)
-    corner = f32(DEEP * deep_groups + STEPS * (groups - deep_groups), lanes)
+    corners = f32(2 * (DEEP * deep_groups + STEPS * (groups - deep_groups)), lanes)
     block = f32(half, rows, lanes)
     high = rows + 2 * DEEP
 
-    keep, give = pl.pallas_call(
+    inputs = (
+        vertical,
+        alpha_fields,
+        anomalies,
+        lon_faces,
+        lat_faces,
+        normalizer,
+        innovation,
+        misfit_weight,
+    )
+    keep, give, alpha = pl.pallas_call(
         functools.partial(prepare_kernel, half),
-        out_shape=(f32(6 * half, rows, lanes), f32(levels, rows, lanes)),
+        out_shape=(f32(6 * half, rows, lanes), f32(levels, rows, lanes), f32(*alpha_fields.shape)),
         in_specs=[HBM] * 8,
-        out_specs=(VMEM, VMEM),
+        out_specs=(VMEM, VMEM, VMEM),
         scratch_shapes=[
             pltpu.SMEM(vertical.shape, jnp.float32),
-            pltpu.VMEM(alpha_fields.shape, jnp.float32),
             pltpu.VMEM(anomalies.shape, jnp.float32),
             pltpu.VMEM(block.shape, jnp.float32),
             pltpu.VMEM(normalizer.shape, jnp.float32),
@@ -318,14 +307,14 @@
         ],
         compiler_params=PARAMS,
         name="prepare",
-    )(vertical, alpha_fields, anomalies, lon_faces, lat_faces, normalizer, innovation, misfit_weight)
+    )(*(pltpu.with_memory_space_constraint(value, pltpu.HBM) for value in inputs))
     got = around(give, "mem", 1)
 
-    first, final, west, east, west_first, west_final, east_first, east_final = pl.pallas_call(
+    first, final, west, east = pl.pallas_call(
         functools.partial(pack_kernel, half),
-        out_shape=(strip, strip, column, column, corner, corner, corner, corner),
+        out_shape=(strip, strip, column, column),
         in_specs=[VMEM] * 2,
-        out_specs=(VMEM,) * 8,
+        out_specs=(VMEM,) * 4,
         compiler_params=PARAMS,
         name="pack",
     )(keep, got)
@@ -333,25 +322,31 @@
     above = around(first, "lon", -1)
     left = around(east, "lat", 1)
     right = around(west, "lat", -1)
-    left_below = diagonal(east_final, 1, 1)
-    left_above = diagonal(east_first, -1, 1)
-    right_below = diagonal(west_final, 1, -1)
-    right_above = diagonal(west_first, -1, -1)
+    first, final = pl.pallas_call(
+        functools.partial(corner_kernel, deep_groups),
+        out_shape=(corners, corners),
+        in_specs=[VMEM] * 2,
+        out_specs=(VMEM,) * 2,
+        compiler_params=PARAMS,
+        name="corners",
+    )(left, right)
+    corner_below = around(final, "lon", 1)
+    corner_above = around(first, "lon", -1)
 
     increment, mine, theirs = pl.pallas_call(
         functools.partial(diffuse_kernel, half),
         out_shape=(block, block, block),
-        in_specs=[VMEM] * 10,
+        in_specs=[VMEM] * 8,
         out_specs=(VMEM,) * 3,
         scratch_shapes=[
             pltpu.VMEM((deep_count, 2, STEPS + high, lanes), jnp.float32),
             pltpu.VMEM((shallow_count, 2, high, lanes), jnp.float32),
-            pltpu.VMEM((5, 2, high, lanes), jnp.float32),
-            pltpu.VMEM((4, 2, high + 2 * STEPS, lanes), jnp.float32),
+            pltpu.VMEM((2, 2, high + 2 * STEPS, lanes), jnp.float32),
+            pltpu.VMEM((2, 2, high + 2 * STEPS, lanes), jnp.float32),
         ],
         compiler_params=PARAMS,
         name="diffuse",
-    )(keep, got, below, above, left, right, left_below, left_above, right_below, right_above)
+    )(keep, got, below, above, left, right, corner_below, corner_above)
     got = around(theirs, "mem", 1)
 
     gradient = pl.pallas_call(
@@ -361,7 +356,7 @@
         out_specs=VMEM,
         compiler_params=PARAMS,
         name="gradient",
-    )(vertical, alpha_fields, mine, got)
+    )(vertical, alpha, mine, got)
     return (increment, gradient)
 
 

time: 60.3 us -> 50.5 us (0.84)
  local copies, waits for them, and re-layouts: 7.1 us -> 0.01 us
  waiting for transfers between devices: 14.4 us -> 8.75 us
  Pallas kernels: 13 us -> 16.9 us
  starting transfers between devices: 24.8 us -> 24.1 us
    ppermute x4 -> x0, waiting for transfers between devices: 12.5 us -> none  [diagonal(): return lax.ppermute(value, ('lon', 'lat'), pairs)]
    ppermute x4 -> x0, starting transfers between devices: 11.3 us -> none  [diagonal(): return lax.ppermute(value, ('lon', 'lat'), pairs)]
    ppermute x6 -> x8, starting transfers between devices: 13.6 us -> 24.1 us  [around(): return lax.ppermute(value, axis, pairs)]
    unnamed x16 -> x2, local copies, waits for them, and re-layouts: 7.1 us -> 0.01 us
    ppermute x6 -> x8, waiting for transfers between devices: 1.96 us -> 8.75 us  [around(): return lax.ppermute(value, axis, pairs)]
    pallas_call x1, Pallas kernels: 9.75 us -> 13.7 us  [local(): pl.pallas_call(functools.partial(diffuse_kernel, half), out_shape=(block,...]
  transfers between devices with their start and end apart: 10 -> 8, of which waited for: 6 -> 4; matrix products, arithmetic and copies ran while one was open for 0% -> 0% of each run, Pallas kernels for 0% -> 0%
where the time goes in v2:
time: 50.5 us; the launch traced here: 50.4 us
  starting transfers between devices  24.1 us (48%)
  Pallas kernels  16.9 us (33%)
  waiting for transfers between devices  8.75 us (17%)
  between operations  0.67 us (1%)
    ppermute x8, starting transfers between devices, around(): return lax.ppermute(value, axis, pairs)  24.1 us
    pallas_call x1, Pallas kernels, local(): pl.pallas_call(functools.partial(diffuse_kernel, half), out_shape=(block,...  13.7 us
    ppermute x8, waiting for transfers between devices, around(): return lax.ppermute(value, axis, pairs)  8.75 us
    pallas_call x1, Pallas kernels, local(): pl.pallas_call(functools.partial(gradient_kernel, half), out_shape=f32(*a...  1.47 us
    pallas_call x1, Pallas kernels, local(): pl.pallas_call(functools.partial(prepare_kernel, half), out_shape=(f32(6...  1.39 us
  transfers between devices with their start and end apart: 8, of which 4 were waited for; matrix products, arithmetic and copies ran while one was open for 0% of the time, Pallas kernels for 0%

profile of v2, /device:TPU:1, one launch (start us, length us, event | category | flops | bytes accessed | tf_op | source)
XLA Modules:
  0.0 50.4 jit_solution(18186067675486105591)
XLA Ops:
  0.6 1.4 %prepare.1 = (f32[30,32,128]{2,1,0:T(8,128)S(1)}, f32[10,32,128]{2,1,0:T(8,128)S(1)}, f32[1,10,32,128]{3,2,1,0:T(8,128)S(1)}) custom-call(f32[10,10]{1,0:T(8,128)} %vertical.1, f32[1,10,32,128]{3,2,1,0:T(8,128)} %alpha_hbm.1, f32[1,10,32,128]{3,2,1,0:T(8,128)} %anomaly_hbm.1, f32[10,32,128]{2,1,0:T(8,128)} %lon_hbm.1, f32[10,32,128]{2,1,0:T(8,128)} %lat_hbm.1, ...), custom_call_target="tpu_custom_call" | custom-call | tf_op jit(solution)/shard_map/prepare/pallas_call | solution.py:294
  2.0 3.3 %collective-permute-start = (f32[10,32,128]{2,1,0:T(8,128)S(1)}, f32[10,32,128]{2,1,0:T(8,128)S(1)}, u32[]{:S(2)}, u32[]{:S(2)}) collective-permute-start(f32[10,32,128]{2,1,0:T(8,128)S(1)} %get-tuple-element.15), channel_id=1, source_target_pairs={{0,1},{1,0},{2,3},{3,2},{4,5},{5,4},{6,7},{7,6},{8,9},{9,8},{10,11... | collective-permute-start | bytes 491528 | tf_op jit(solution)/shard_map/ppermute | solution.py:27
  5.4 1.0 %collective-permute-done.got = f32[10,32,128]{2,1,0:T(8,128)S(1)} collective-permute-done((f32[10,32,128]{2,1,0:T(8,128)S(1)}, f32[10,32,128]{2,1,0:T(8,128)S(1)}, u32[]{:S(2)}, u32[]{:S(2)}) %collective-permute-start) | collective-permute-done | bytes 163872 | tf_op jit(solution)/shard_map/ppermute | solution.py:27
  6.4 0.3 pack.1
  6.7 1.1 %collective-permute-start.1 = (f32[440,128]{1,0:T(8,128)S(1)}, f32[440,128]{1,0:T(8,128)S(1)}, u32[]{:S(2)}, u32[]{:S(2)}) collective-permute-start(f32[440,128]{1,0:T(8,128)S(1)} %get-tuple-element.16), channel_id=1, source_target_pairs={{0,16},{16,32},{32,48},{48,64},{64,80},{80,96},{96,112},{112,128},... | collective-permute-start | bytes 675848 | tf_op jit(solution)/shard_map/ppermute | solution.py:27
  7.8 5.4 %collective-permute-start.2 = (f32[440,128]{1,0:T(8,128)S(1)}, f32[440,128]{1,0:T(8,128)S(1)}, u32[]{:S(2)}, u32[]{:S(2)}) collective-permute-start(f32[440,128]{1,0:T(8,128)S(1)} %get-tuple-element.17), channel_id=1, source_target_pairs={{0,240},{16,0},{32,16},{48,32},{64,48},{80,64},{96,80},{112,96},{1... | collective-permute-start | bytes 675848 | tf_op jit(solution)/shard_map/ppermute | solution.py:27
  13.2 0.3 collective-permute-start.3
  13.5 3.3 %collective-permute-start.4 = (f32[4,32,128]{2,1,0:T(8,128)S(1)}, f32[4,32,128]{2,1,0:T(8,128)S(1)}, u32[]{:S(2)}, u32[]{:S(2)}) collective-permute-start(f32[4,32,128]{2,1,0:T(8,128)S(1)} %get-tuple-element.19), channel_id=1, source_target_pairs={{0,14},{2,0},{4,2},{6,4},{8,6},{10,8},{12,10},{14,12},{1,15},{3,1}... | collective-permute-start | bytes 196616 | tf_op jit(solution)/shard_map/ppermute | solution.py:27
  16.8 5.3 %collective-permute-done.3.left = f32[4,32,128]{2,1,0:T(8,128)S(1)} collective-permute-done((f32[4,32,128]{2,1,0:T(8,128)S(1)}, f32[4,32,128]{2,1,0:T(8,128)S(1)}, u32[]{:S(2)}, u32[]{:S(2)}) %collective-permute-start.3) | collective-permute-done | bytes 65568 | tf_op jit(solution)/shard_map/ppermute | solution.py:27
  22.1 0.0 collective-permute-done.4.right
  22.1 3.0 %collective-permute-start.5 = (f32[112,128]{1,0:T(8,128)S(1)}, f32[112,128]{1,0:T(8,128)S(1)}, u32[]{:S(2)}, u32[]{:S(2)}) collective-permute-start(f32[112,128]{1,0:T(8,128)S(1)} %get-tuple-element.20), channel_id=1, source_target_pairs={{0,16},{16,32},{32,48},{48,64},{64,80},{80,96},{96,112},{112,128},... | collective-permute-start | bytes 172040 | tf_op jit(solution)/shard_map/ppermute | solution.py:27
  25.1 5.7 %collective-permute-start.6 = (f32[112,128]{1,0:T(8,128)S(1)}, f32[112,128]{1,0:T(8,128)S(1)}, u32[]{:S(2)}, u32[]{:S(2)}) collective-permute-start(f32[112,128]{1,0:T(8,128)S(1)} %get-tuple-element.21), channel_id=1, source_target_pairs={{0,240},{16,0},{32,16},{48,32},{64,48},{80,64},{96,80},{112,96},{1... | collective-permute-start | bytes 172040 | tf_op jit(solution)/shard_map/ppermute | solution.py:27
  30.9 1.5 %collective-permute-done.5.corner_below = f32[112,128]{1,0:T(8,128)S(1)} collective-permute-done((f32[112,128]{1,0:T(8,128)S(1)}, f32[112,128]{1,0:T(8,128)S(1)}, u32[]{:S(2)}, u32[]{:S(2)}) %collective-permute-start.5) | collective-permute-done | bytes 57376 | tf_op jit(solution)/shard_map/ppermute | solution.py:27
  32.4 0.0 collective-permute-done.6.corner_above
  32.4 0.0 collective-permute-done.1.below
  32.4 0.0 collective-permute-done.2.above
  32.4 0.0 copy-start
  32.4 13.7 %diffuse.1 = (f32[5,32,128]{2,1,0:T(8,128)}, f32[5,32,128]{2,1,0:T(8,128)S(1)}, f32[5,32,128]{2,1,0:T(8,128)S(1)}) custom-call(f32[30,32,128]{2,1,0:T(8,128)S(1)} %get-tuple-element.14.keep, f32[10,32,128]{2,1,0:T(8,128)S(1)} %collective-permute-done.got, f32[440,128]{1,0:T(8,128)S(1)} %collective-permute-done.1.below, ...), custom_call_target="tpu_custom_call" | custom-call | tf_op jit(solution)/shard_map/diffuse/pallas_call | solution.py:336
  46.1 1.9 %collective-permute-start.7 = (f32[5,32,128]{2,1,0:T(8,128)S(1)}, f32[5,32,128]{2,1,0:T(8,128)S(1)}, u32[]{:S(2)}, u32[]{:S(2)}) collective-permute-start(f32[5,32,128]{2,1,0:T(8,128)S(1)} %get-tuple-element.25), channel_id=1, source_target_pairs={{0,1},{1,0},{2,3},{3,2},{4,5},{5,4},{6,7},{7,6},{8,9},{9,8},{10,11... | collective-permute-start | bytes 245768 | tf_op jit(solution)/shard_map/ppermute | solution.py:27
  48.0 0.9 %collective-permute-done.7.got = f32[5,32,128]{2,1,0:T(8,128)S(1)} collective-permute-done((f32[5,32,128]{2,1,0:T(8,128)S(1)}, f32[5,32,128]{2,1,0:T(8,128)S(1)}, u32[]{:S(2)}, u32[]{:S(2)}) %collective-permute-start.7) | collective-permute-done | bytes 81952 | tf_op jit(solution)/shard_map/ppermute | solution.py:27
  48.9 0.0 copy-done
  48.9 1.5 %gradient.1 = f32[1,10,32,128]{3,2,1,0:T(8,128)} custom-call(f32[10,10]{1,0:T(8,128)S(1)} %copy-done, f32[1,10,32,128]{3,2,1,0:T(8,128)S(1)} %get-tuple-element.23.alpha, f32[5,32,128]{2,1,0:T(8,128)S(1)} %get-tuple-element.24.mine, f32[5,32,128]{2,1,0:T(8,128)S(1)} %collective-permute-done.7.got), custom_call_target="tpu_custom_call" | custom-call | tf_op jit(solution)/shard_map/gradient/pallas_call | solution.py:352
  (1 shorter events, 0.0 us)
Async XLA Ops:
  2.0 4.4 %collective-permute-start = (f32[10,32,128]{2,1,0:T(8,128)S(1)}, f32[10,32,128]{2,1,0:T(8,128)S(1)}, u32[]{:S(2)}, u32[]{:S(2)}) collective-permute-start(f32[10,32,128]{2,1,0:T(8,128)S(1)} %get-tuple-element.15), channel_id=1, source_target_pairs={{0,1},{1,0},{2,3},{3,2},{4,5},{5,4},{6,7},{7,6},{8,9},{9,8},{10,11... | collective-permute-start | bytes 491528 | tf_op jit(solution)/shard_map/ppermute | solution.py:27
  6.7 25.6 %collective-permute-start.1 = (f32[440,128]{1,0:T(8,128)S(1)}, f32[440,128]{1,0:T(8,128)S(1)}, u32[]{:S(2)}, u32[]{:S(2)}) collective-permute-start(f32[440,128]{1,0:T(8,128)S(1)} %get-tuple-element.16), channel_id=1, source_target_pairs={{0,16},{16,32},{32,48},{48,64},{64,80},{80,96},{96,112},{112,128},... | collective-permute-start | bytes 675848 | tf_op jit(solution)/shard_map/ppermute | solution.py:27
  7.8 24.6 %collective-permute-start.2 = (f32[440,128]{1,0:T(8,128)S(1)}, f32[440,128]{1,0:T(8,128)S(1)}, u32[]{:S(2)}, u32[]{:S(2)}) collective-permute-start(f32[440,128]{1,0:T(8,128)S(1)} %get-tuple-element.17), channel_id=1, source_target_pairs={{0,240},{16,0},{32,16},{48,32},{64,48},{80,64},{96,80},{112,96},{1... | collective-permute-start | bytes 675848 | tf_op jit(solution)/shard_map/ppermute | solution.py:27
  13.2 8.9 %collective-permute-start.3 = (f32[4,32,128]{2,1,0:T(8,128)S(1)}, f32[4,32,128]{2,1,0:T(8,128)S(1)}, u32[]{:S(2)}, u32[]{:S(2)}) collective-permute-start(f32[4,32,128]{2,1,0:T(8,128)S(1)} %get-tuple-element.18), channel_id=1, source_target_pairs={{0,2},{2,4},{4,6},{6,8},{8,10},{10,12},{12,14},{14,0},{1,3},{3,5},... | collective-permute-start | bytes 196616 | tf_op jit(solution)/shard_map/ppermute | solution.py:27
  13.5 8.6 %collective-permute-start.4 = (f32[4,32,128]{2,1,0:T(8,128)S(1)}, f32[4,32,128]{2,1,0:T(8,128)S(1)}, u32[]{:S(2)}, u32[]{:S(2)}) collective-permute-start(f32[4,32,128]{2,1,0:T(8,128)S(1)} %get-tuple-element.19), channel_id=1, source_target_pairs={{0,14},{2,0},{4,2},{6,4},{8,6},{10,8},{12,10},{14,12},{1,15},{3,1}... | collective-permute-start | bytes 196616 | tf_op jit(solution)/shard_map/ppermute | solution.py:27
  22.1 10.3 %collective-permute-start.5 = (f32[112,128]{1,0:T(8,128)S(1)}, f32[112,128]{1,0:T(8,128)S(1)}, u32[]{:S(2)}, u32[]{:S(2)}) collective-permute-start(f32[112,128]{1,0:T(8,128)S(1)} %get-tuple-element.20), channel_id=1, source_target_pairs={{0,16},{16,32},{32,48},{48,64},{64,80},{80,96},{96,112},{112,128},... | collective-permute-start | bytes 172040 | tf_op jit(solution)/shard_map/ppermute | solution.py:27
  25.1 7.2 %collective-permute-start.6 = (f32[112,128]{1,0:T(8,128)S(1)}, f32[112,128]{1,0:T(8,128)S(1)}, u32[]{:S(2)}, u32[]{:S(2)}) collective-permute-start(f32[112,128]{1,0:T(8,128)S(1)} %get-tuple-element.21), channel_id=1, source_target_pairs={{0,240},{16,0},{32,16},{48,32},{64,48},{80,64},{96,80},{112,96},{1... | collective-permute-start | bytes 172040 | tf_op jit(solution)/shard_map/ppermute | solution.py:27
  32.4 16.6 %copy-start = (f32[10,10]{1,0:T(8,128)S(1)}, f32[10,10]{1,0:T(8,128)}, u32[]{:S(2)}) copy-start(f32[10,10]{1,0:T(8,128)} %vertical.1) | copy-start | bytes 1204
  46.1 2.8 %collective-permute-start.7 = (f32[5,32,128]{2,1,0:T(8,128)S(1)}, f32[5,32,128]{2,1,0:T(8,128)S(1)}, u32[]{:S(2)}, u32[]{:S(2)}) collective-permute-start(f32[5,32,128]{2,1,0:T(8,128)S(1)} %get-tuple-element.25), channel_id=1, source_target_pairs={{0,1},{1,0},{2,3},{3,2},{4,5},{5,4},{6,7},{7,6},{8,9},{9,8},{10,11... | collective-permute-start | bytes 245768 | tf_op jit(solution)/shard_map/ppermute | solution.py:27

commit v3 on v2

v3 whole, which is shorter than its diff:
```python
import functools
import math

import jax
import jax.numpy as jnp
from jax import lax
from jax.experimental import pallas as pl
from jax.experimental.pallas import tpu as pltpu
from jax.sharding import PartitionSpec as P

STEPS = 8
DEEP = 2 * STEPS
LANES = 128
VMEM = pl.BlockSpec(memory_space=pltpu.VMEM)
SMEM = pl.BlockSpec(memory_space=pltpu.SMEM)
HBM = pl.BlockSpec(memory_space=pltpu.HBM)
PARAMS = pltpu.CompilerParams(vmem_limit_bytes=32 * 1024 * 1024)


def f32(*shape):
    return jax.ShapeDtypeStruct(shape, jnp.float32)


def around(value, axis, steps):
    count = lax.axis_size(axis)
    pairs = [(source, (source + steps) % count) for source in range(count)]
    return lax.ppermute(value, axis, pairs)


def lane_places(deep, shallow):
    places = []
    for width, count in ((DEEP, deep), (STEPS, shallow)):
        for i in range(count):
            group, place = divmod(i * width, LANES)
            if width == STEPS:
                group += -(-deep * DEEP // LANES)
            places.append((width, group, place, (place + 2 * DEEP - width) % LANES))
    return places


def turned(value, shift):
    shift = shift % value.shape[-1]
    return pltpu.roll(value, shift, axis=value.ndim - 1) if shift else value


def mixed(vertical_ref, alpha_ref, level):
    total = vertical_ref[level, 0] * alpha_ref[0, 0]
    for k in range(1, alpha_ref.shape[1]):
        total = total + vertical_ref[level, k] * alpha_ref[0, k]
    return total


def prepare_kernel(
    half,
    vertical_hbm,
    alpha_hbm,
    anomaly_hbm,
    lon_hbm,
    lat_hbm,
    normalizer_hbm,
    innovation_hbm,
    weight_hbm,
    keep,
    give,
    alpha,
    vertical,
    anomaly,
    faces,
    normalizer,
    innovation,
    weight,
    sems,
):
    base = lax.axis_index("mem") * half
    other = half - base
    pairs = [
        (vertical_hbm, vertical),
        (alpha_hbm, alpha),
        (weight_hbm, weight),
        (normalizer_hbm, normalizer),
        (anomaly_hbm, anomaly),
        (innovation_hbm.at[pl.ds(base, half)], innovation),
        (lon_hbm.at[pl.ds(base, half)], keep.at[pl.ds(half, half)]),
        (lat_hbm.at[pl.ds(base, half)], faces),
    ]
    copies = [pltpu.make_async_copy(a, b, sems.at[n]) for n, (a, b) in enumerate(pairs)]
    for copy in copies:
        copy.start()
    copies[0].wait()
    copies[1].wait()
    for i in range(half):
        keep[i] = mixed(vertical, alpha, base + i)
        give[i] = mixed(vertical, alpha, other + i)
    for copy in copies[2:]:
        copy.wait()
    last = lax.axis_index("lat") == lax.axis_size("lat") - 1
    lane = lax.broadcasted_iota(jnp.int32, faces.shape[1:], 1)
    closed = jnp.logical_and(last, lane == faces.shape[2] - 1)
    for i in range(half):
        mine, theirs = base + i, other + i
        root = jnp.sqrt(weight[mine])
        keep[2 * half + i] = jnp.where(closed, 0.0, faces[i])
        keep[3 * half + i] = normalizer[mine] * anomaly[0, mine] * root
        keep[4 * half + i] = root * innovation[i]
        keep[5 * half + i] = 1.0 / root
        give[half + i] = normalizer[theirs] * anomaly[0, theirs] * jnp.sqrt(weight[theirs])


def field_refs(half, keep, got):
    deep = [keep.at[i] for i in range(half)]
    deep += [got.at[i] for i in range(half)]
    deep += [keep.at[half + i] for i in range(2 * half)]
    shallow = [keep.at[3 * half + i] for i in range(half)]
    shallow += [got.at[half + i] for i in range(half)]
    shallow += [keep.at[4 * half + i] for i in range(half)]
    return deep, shallow


def strip_kernel(half, keep, got, first, final):
    deep, shallow = field_refs(half, keep, got)
    rows = keep.shape[1]
    at = 0
    for width, fields in ((DEEP, deep), (STEPS, shallow)):
        for ref in fields:
            first[at : at + width] = ref[:width]
            final[at : at + width] = ref[rows - width :]
            at += width


def in_lanes(lane, place, width):
    if place + width > LANES:
        return jnp.logical_or(lane >= place, lane < place + width - LANES)
    return jnp.logical_and(lane >= place, lane < place + width)


def column_kernel(half, keep, got, below, above, west, east):
    deep, shallow = field_refs(half, keep, got)
    rows, lanes = keep.shape[1:]
    high = rows + 2 * DEEP
    lane = lax.broadcasted_iota(jnp.int32, (1, lanes), 1)
    packs = {}
    at = 0
    for ref, (width, group, place, opposite) in zip(
        deep + shallow, lane_places(len(deep), len(shallow))
    ):
        pieces = (below[at : at + width], ref[...], above[at : at + width])
        at += width
        for n, piece in enumerate(pieces):
            heads, tails = packs.get((group, n), (0.0, 0.0))
            heads = jnp.where(in_lanes(lane, place, width), turned(piece, place), heads)
            tails = jnp.where(in_lanes(lane, opposite, width), turned(piece, place + 2 * DEEP), tails)
            packs[group, n] = heads, tails
    at = 0
    for heads, tails in packs.values():
        count = heads.shape[0]
        west[at : at + count] = heads
        east[at : at + count] = tails
        at += count


def diffusion(half, field_tiles, other_tiles, face_tiles, shallow_tiles, totals):
    high = field_tiles.shape[1] - 2 * STEPS
    rows = high - 2 * DEEP
    edge = jnp.zeros((STEPS, field_tiles.shape[2]), jnp.float32)
    for n in range(2 * half):
        face_tiles[n, :STEPS] = edge
        for ref in (field_tiles, other_tiles):
            ref[n, :STEPS] = edge
            ref[n, STEPS + high :] = edge

    def step(source, target, begin, count):
        body = pl.ds(STEPS + begin, count)
        up = pl.ds(STEPS + begin + 1, count)
        down = pl.ds(STEPS + begin - 1, count)
        for i in range(half):
            lon_coef = face_tiles[i, body]
            lon_before = face_tiles[i, down]
            lat_coef = face_tiles[half + i, body]
            for n in (i, half + i):
                field = source[n, body]
                flux_x = lon_coef * (source[n, up] - field)
                flux_x = flux_x - lon_before * (field - source[n, down])
                flux_y = lat_coef * (turned(field, -1) - field)
                target[n, body] = (field + flux_x) + (flux_y - turned(flux_y, 1))

    def root(margin):
        for begin in (margin, margin + STEPS // 2):
            count = high - 2 * begin

            def pair(_, carry):
                step(field_tiles, other_tiles, begin, count)
                step(other_tiles, field_tiles, begin, count)
                return carry

            lax.fori_loop(0, STEPS // 4, pair, 0)

    root(0)
    inner = pl.ds(2 * STEPS, rows + 2 * STEPS)
    for i in range(half):
        gains = [shallow_tiles[m * half + i] for m in range(2)]
        total = sum(gains[m] * field_tiles[m * half + i, inner] for m in range(2))
        totals[i] = total[STEPS : STEPS + rows]
        residual = total - shallow_tiles[2 * half + i]
        for m in range(2):
            field_tiles[m * half + i, inner] = gains[m] * residual
    root(STEPS)


def tile_targets(half, field_tiles, face_tiles, shallow_tiles):
    high = field_tiles.shape[1] - 2 * STEPS
    targets = [field_tiles.at[n, pl.ds(STEPS, high)] for n in range(2 * half)]
    targets += [face_tiles.at[n, pl.ds(STEPS, high)] for n in range(2 * half)]
    return targets + [shallow_tiles.at[n] for n in range(3 * half)]


def main_kernel(half, keep, got, below, above, total, mine, theirs, *tiles):
    field_tiles, other_tiles, face_tiles, shallow_tiles = tiles
    deep, shallow = field_refs(half, keep, got)
    rows = keep.shape[1]
    at = 0
    for n, (ref, out) in enumerate(
        zip(deep + shallow, tile_targets(half, field_tiles, face_tiles, shallow_tiles))
    ):
        width = DEEP if n < len(deep) else STEPS
        out[:width] = below[at : at + width]
        out[width : width + rows] = ref[...]
        out[width + rows :] = above[at : at + width]
        at += width
    diffusion(half, *tiles, total)
    own = pl.ds(STEPS + DEEP, rows)
    for i in range(half):
        mine[i] = field_tiles[i, own]
        theirs[i] = field_tiles[half + i, own]


def edge_kernel(
    half,
    keep,
    got,
    below,
    above,
    left,
    right,
    main_total,
    main_mine,
    main_theirs,
    increment,
    mine,
    theirs,
    *tiles,
):
    field_tiles, other_tiles, face_tiles, shallow_tiles, totals = tiles
    deep, shallow = field_refs(half, keep, got)
    rows, lanes = keep.shape[1:]
    lane = lax.broadcasted_iota(jnp.int32, (1, lanes), 1)
    at = 0
    group_rows = {DEEP: rows + 2 * DEEP, STEPS: rows + 2 * STEPS}
    for ref, out, (width, group, place, _) in zip(
        deep + shallow,
        tile_targets(half, field_tiles, face_tiles, shallow_tiles),
        lane_places(len(deep), len(shallow)),
    ):
        pieces = (below[at : at + width], ref[...], above[at : at + width])
        at += width
        start = group * group_rows[DEEP]
        offset = 0
        for piece in pieces:
            count = piece.shape[0]
            here = pl.ds(start + offset, count)
            sides = jnp.where(in_lanes(lane, place, width), right[here], left[here])
            own = jnp.where(lane < lanes - 3 * DEEP, turned(piece, 2 * DEEP), piece)
            out[offset : offset + count] = jnp.where(lane < 2 * DEEP, turned(sides, -place), own)
            offset += count
    diffusion(half, field_tiles, other_tiles, face_tiles, shallow_tiles, totals)
    body = pl.ds(STEPS + DEEP, rows)

    def joined(main, sides):
        sides = jnp.where(lane < DEEP, turned(sides, -2 * DEEP), sides)
        return jnp.where(in_lanes(lane, DEEP, lanes - 2 * DEEP), main, sides)

    for i in range(half):
        increment[i] = joined(main_total[i], totals[i]) * keep[5 * half + i]
        mine[i] = joined(main_mine[i], field_tiles[i, body])
        theirs[i] = joined(main_theirs[i], field_tiles[half + i, body])


def gradient_kernel(half, vertical, alpha, mine, got, gradient):
    base = lax.axis_index("mem") * half
    other = half - base
    for k in range(2 * half):
        total = alpha[0, k]
        for i in range(half):
            total = total + vertical[base + i, k] * mine[i]
            total = total + vertical[other + i, k] * got[i]
        gradient[0, k] = total


def local(
    alpha_fields, anomalies, lon_faces, lat_faces, normalizer, innovation, misfit_weight, vertical
):
    levels, rows, lanes = lon_faces.shape
    half = levels // 2
    high = rows + 2 * DEEP
    strip = f32(DEEP * 4 * half + STEPS * 3 * half, lanes)
    deep_groups = -(-4 * half * DEEP // lanes)
    shallow_groups = -(-3 * half * STEPS // lanes)
    column = f32(deep_groups * high + shallow_groups * (rows + 2 * STEPS), lanes)
    block = f32(half, rows, lanes)
    tiles = [
        pltpu.VMEM((levels, high + 2 * STEPS, lanes), jnp.float32),
        pltpu.VMEM((levels, high + 2 * STEPS, lanes), jnp.float32),
        pltpu.VMEM((levels, high + STEPS, lanes), jnp.float32),
        pltpu.VMEM((3 * half, rows + 2 * STEPS, lanes), jnp.float32),
    ]

    inputs = (
        vertical,
        alpha_fields,
        anomalies,
        lon_faces,
        lat_faces,
        normalizer,
        innovation,
        misfit_weight,
    )
    keep, give, alpha = pl.pallas_call(
        functools.partial(prepare_kernel, half),
        out_shape=(f32(6 * half, rows, lanes), f32(levels, rows, lanes), f32(*alpha_fields.shape)),
        in_specs=[HBM] * 8,
        out_specs=(VMEM, VMEM, VMEM),
        scratch_shapes=[
            pltpu.SMEM(vertical.shape, jnp.float32),
            pltpu.VMEM(anomalies.shape, jnp.float32),
            pltpu.VMEM(block.shape, jnp.float32),
            pltpu.VMEM(normalizer.shape, jnp.float32),
            pltpu.VMEM(block.shape, jnp.float32),
            pltpu.VMEM(misfit_weight.shape, jnp.float32),
            pltpu.SemaphoreType.DMA((8,)),
        ],
        compiler_params=PARAMS,
        name="prepare",
    )(*(pltpu.with_memory_space_constraint(value, pltpu.HBM) for value in inputs))
    got = around(give, "mem", 1)

    first, final = pl.pallas_call(
        functools.partial(strip_kernel, half),
        out_shape=(strip, strip),
        in_specs=[VMEM] * 2,
        out_specs=(VMEM,) * 2,
        compiler_params=PARAMS,
        name="strips",
    )(keep, got)
    below = around(final, "lon", 1)
    above = around(first, "lon", -1)
    west, east = pl.pallas_call(
        functools.partial(column_kernel, half),
        out_shape=(column, column),
        in_specs=[VMEM] * 4,
        out_specs=(VMEM,) * 2,
        compiler_params=PARAMS,
        name="columns",
    )(keep, got, below, above)
    left = around(east, "lat", 1)
    right = around(west, "lat", -1)
    main = pl.pallas_call(
        functools.partial(main_kernel, half),
        out_shape=(block, block, block),
        in_specs=[VMEM] * 4,
        out_specs=(VMEM,) * 3,
        scratch_shapes=tiles,
        compiler_params=PARAMS,
        name="main",
    )(keep, got, below, above)
    increment, mine, theirs = pl.pallas_call(
        functools.partial(edge_kernel, half),
        out_shape=(block, block, block),
        in_specs=[VMEM] * 9,
        out_specs=(VMEM,) * 3,
        scratch_shapes=tiles + [pltpu.VMEM(block.shape, jnp.float32)],
        compiler_params=PARAMS,
        name="edge",
    )(keep, got, below, above, left, right, *main)
    got = around(theirs, "mem", 1)

    gradient = pl.pallas_call(
        functools.partial(gradient_kernel, half),
        out_shape=f32(*alpha_fields.shape),
        in_specs=[SMEM] + [VMEM] * 3,
        out_specs=VMEM,
        compiler_params=PARAMS,
        name="gradient",
    )(vertical, alpha, mine, got)
    return (increment, gradient)


def solution(mesh):
    return jax.shard_map(
        local,
        mesh=mesh,
        in_specs=(
            P("mem", None, "lon", "lat"),
            P("mem", None, "lon", "lat"),
            P(None, "lon", "lat"),
            P(None, "lon", "lat"),
            P(None, "lon", "lat"),
            P(None, "lon", "lat"),
            P(None, "lon", "lat"),
            P(),
        ),
        out_specs=(P("mem", "lon", "lat"), P("mem", None, "lon", "lat")),
        check_vma=False,
    )
```

time: 50.5 us -> 41.7 us (0.83)
  starting transfers between devices: 24.1 us -> 15.5 us
  Pallas kernels: 16.9 us -> 16.1 us
  waiting for transfers between devices: 8.75 us -> 9.32 us
    ppermute x8 -> x6, starting transfers between devices: 24.1 us -> 15.5 us  [around(): return lax.ppermute(value, axis, pairs)]
    pallas_call x3 -> x4, Pallas kernels: 14.1 us -> 13.2 us  [the longest x1 6.92 us: local(): pl.pallas_call(functools.partial(edge_kernel, half), out_shape=(block, bl...]
    ppermute x8 -> x6, waiting for transfers between devices: 8.75 us -> 9.32 us  [around(): return lax.ppermute(value, axis, pairs)]
  transfers between devices with their start and end apart: 8 -> 6, of which waited for: 4 -> 4; matrix products, arithmetic and copies ran while one was open for 0% -> 0% of each run, Pallas kernels for 0% -> 14%
where the time goes in v3:
time: 41.7 us; the launch traced here: 41.6 us
  Pallas kernels  16.1 us (39%)
  starting transfers between devices  15.5 us (37%)
  waiting for transfers between devices  9.32 us (22%)
  between operations  0.68 us (2%)
    ppermute x6, starting transfers between devices, around(): return lax.ppermute(value, axis, pairs)  15.5 us
    ppermute x6, waiting for transfers between devices, around(): return lax.ppermute(value, axis, pairs)  9.32 us
    pallas_call x1, Pallas kernels, local(): pl.pallas_call(functools.partial(edge_kernel, half), out_shape=(block, bl...  6.92 us
    pallas_call x1, Pallas kernels, local(): pl.pallas_call(functools.partial(main_kernel, half), out_shape=(block, bl...  5.69 us
    pallas_call x1, Pallas kernels, local(): pl.pallas_call(functools.partial(gradient_kernel, half), out_shape=f32(*a...  1.47 us
    pallas_call x1, Pallas kernels, local(): pl.pallas_call(functools.partial(prepare_kernel, half), out_shape=(f32(6...  1.39 us
  transfers between devices with their start and end apart: 6, of which 4 were waited for; matrix products, arithmetic and copies ran while one was open for 0% of the time, Pallas kernels for 14%

profile of v3, /device:TPU:1, one launch (start us, length us, event | category | flops | bytes accessed | tf_op | source)
XLA Modules:
  0.0 41.6 jit_solution(6306769399086477330)
XLA Ops:
  0.6 1.4 %prepare.1 = (f32[30,32,128]{2,1,0:T(8,128)S(1)}, f32[10,32,128]{2,1,0:T(8,128)S(1)}, f32[1,10,32,128]{3,2,1,0:T(8,128)S(1)}) custom-call(f32[10,10]{1,0:T(8,128)} %vertical.1, f32[1,10,32,128]{3,2,1,0:T(8,128)} %alpha_hbm.1, f32[1,10,32,128]{3,2,1,0:T(8,128)} %anomaly_hbm.1, f32[10,32,128]{2,1,0:T(8,128)} %lon_hbm.1, f32[10,32,128]{2,1,0:T(8,128)} %lat_hbm.1, ...), custom_call_target="tpu_custom_call" | custom-call | tf_op jit(solution)/shard_map/prepare/pallas_call | solution.py:326
  2.0 3.3 %collective-permute-start = (f32[10,32,128]{2,1,0:T(8,128)S(1)}, f32[10,32,128]{2,1,0:T(8,128)S(1)}, u32[]{:S(2)}, u32[]{:S(2)}) collective-permute-start(f32[10,32,128]{2,1,0:T(8,128)S(1)} %get-tuple-element.16), channel_id=1, source_target_pairs={{0,1},{1,0},{2,3},{3,2},{4,5},{5,4},{6,7},{7,6},{8,9},{9,8},{10,11... | collective-permute-start | bytes 491528 | tf_op jit(solution)/shard_map/ppermute | solution.py:27
  5.4 1.0 %collective-permute-done.got = f32[10,32,128]{2,1,0:T(8,128)S(1)} collective-permute-done((f32[10,32,128]{2,1,0:T(8,128)S(1)}, f32[10,32,128]{2,1,0:T(8,128)S(1)}, u32[]{:S(2)}, u32[]{:S(2)}) %collective-permute-start) | collective-permute-done | bytes 163872 | tf_op jit(solution)/shard_map/ppermute | solution.py:27
  6.4 1.1 %collective-permute-start.1 = (f32[440,128]{1,0:T(8,128)S(1)}, f32[440,128]{1,0:T(8,128)S(1)}, u32[]{:S(2)}, u32[]{:S(2)}) collective-permute-start(f32[440,128]{1,0:T(8,128)S(1)} %get-tuple-element.17), channel_id=1, source_target_pairs={{0,16},{16,32},{32,48},{48,64},{64,80},{80,96},{96,112},{112,128},... | collective-permute-start | bytes 675848 | tf_op jit(solution)/shard_map/ppermute | solution.py:27
  7.5 5.4 %collective-permute-start.2 = (f32[440,128]{1,0:T(8,128)S(1)}, f32[440,128]{1,0:T(8,128)S(1)}, u32[]{:S(2)}, u32[]{:S(2)}) collective-permute-start(f32[440,128]{1,0:T(8,128)S(1)} %get-tuple-element.18), channel_id=1, source_target_pairs={{0,240},{16,0},{32,16},{48,32},{64,48},{80,64},{96,80},{112,96},{1... | collective-permute-start | bytes 675848 | tf_op jit(solution)/shard_map/ppermute | solution.py:27
  12.9 5.5 %collective-permute-done.1.below = f32[440,128]{1,0:T(8,128)S(1)} collective-permute-done((f32[440,128]{1,0:T(8,128)S(1)}, f32[440,128]{1,0:T(8,128)S(1)}, u32[]{:S(2)}, u32[]{:S(2)}) %collective-permute-start.1) | collective-permute-done | bytes 225312 | tf_op jit(solution)/shard_map/ppermute | solution.py:27
  18.4 1.8 %collective-permute-done.2.above = f32[440,128]{1,0:T(8,128)S(1)} collective-permute-done((f32[440,128]{1,0:T(8,128)S(1)}, f32[440,128]{1,0:T(8,128)S(1)}, u32[]{:S(2)}, u32[]{:S(2)}) %collective-permute-start.2) | collective-permute-done | bytes 225312 | tf_op jit(solution)/shard_map/ppermute | solution.py:27
  20.3 0.5 %columns.1 = (f32[240,128]{1,0:T(8,128)S(1)}, f32[240,128]{1,0:T(8,128)S(1)}) custom-call(f32[30,32,128]{2,1,0:T(8,128)S(1)} %get-tuple-element.15.keep, f32[10,32,128]{2,1,0:T(8,128)S(1)} %collective-permute-done.got, f32[440,128]{1,0:T(8,128)S(1)} %collective-permute-done.1.below, f32[440,128]{1,0:T(8,128)S(1)} %collective-permute-done.2.above), custom_call_target="tpu_custom_call" | custom-call | tf_op jit(solution)/shard_map/columns/pallas_call | solution.py:355
  20.8 0.4 collective-permute-start.3
  21.2 3.3 %collective-permute-start.4 = (f32[240,128]{1,0:T(8,128)S(1)}, f32[240,128]{1,0:T(8,128)S(1)}, u32[]{:S(2)}, u32[]{:S(2)}) collective-permute-start(f32[240,128]{1,0:T(8,128)S(1)} %get-tuple-element.20), channel_id=1, source_target_pairs={{0,14},{2,0},{4,2},{6,4},{8,6},{10,8},{12,10},{14,12},{1,15},{3,1}... | collective-permute-start | bytes 368648 | tf_op jit(solution)/shard_map/ppermute | solution.py:27
  24.5 5.7 %main.1 = (f32[5,32,128]{2,1,0:T(8,128)S(1)}, f32[5,32,128]{2,1,0:T(8,128)S(1)}, f32[5,32,128]{2,1,0:T(8,128)S(1)}) custom-call(f32[30,32,128]{2,1,0:T(8,128)S(1)} %get-tuple-element.15.keep, f32[10,32,128]{2,1,0:T(8,128)S(1)} %collective-permute-done.got, f32[440,128]{1,0:T(8,128)S(1)} %collective-permute-done.1.below, ...), custom_call_target="tpu_custom_call" | custom-call | tf_op jit(solution)/shard_map/main/pallas_call | solution.py:365
  30.2 0.0 collective-permute-done.3.left
  30.2 0.0 collective-permute-done.4.right
  30.2 0.0 copy-start
  30.2 6.9 %edge.1 = (f32[5,32,128]{2,1,0:T(8,128)}, f32[5,32,128]{2,1,0:T(8,128)S(1)}, f32[5,32,128]{2,1,0:T(8,128)S(1)}) custom-call(f32[30,32,128]{2,1,0:T(8,128)S(1)} %get-tuple-element.15.keep, f32[10,32,128]{2,1,0:T(8,128)S(1)} %collective-permute-done.got, f32[440,128]{1,0:T(8,128)S(1)} %collective-permute-done.1.below, ...), custom_call_target="tpu_custom_call" | custom-call | tf_op jit(solution)/shard_map/edge/pallas_call | solution.py:374
  37.1 2.1 %collective-permute-start.5 = (f32[5,32,128]{2,1,0:T(8,128)S(1)}, f32[5,32,128]{2,1,0:T(8,128)S(1)}, u32[]{:S(2)}, u32[]{:S(2)}) collective-permute-start(f32[5,32,128]{2,1,0:T(8,128)S(1)} %get-tuple-element.27), channel_id=1, source_target_pairs={{0,1},{1,0},{2,3},{3,2},{4,5},{5,4},{6,7},{7,6},{8,9},{9,8},{10,11... | collective-permute-start | bytes 245768 | tf_op jit(solution)/shard_map/ppermute | solution.py:27
  39.2 0.9 %collective-permute-done.5.got = f32[5,32,128]{2,1,0:T(8,128)S(1)} collective-permute-done((f32[5,32,128]{2,1,0:T(8,128)S(1)}, f32[5,32,128]{2,1,0:T(8,128)S(1)}, u32[]{:S(2)}, u32[]{:S(2)}) %collective-permute-start.5) | collective-permute-done | bytes 81952 | tf_op jit(solution)/shard_map/ppermute | solution.py:27
  40.1 0.0 copy-done
  40.1 1.5 %gradient.1 = f32[1,10,32,128]{3,2,1,0:T(8,128)} custom-call(f32[10,10]{1,0:T(8,128)S(1)} %copy-done, f32[1,10,32,128]{3,2,1,0:T(8,128)S(1)} %get-tuple-element.25.alpha, f32[5,32,128]{2,1,0:T(8,128)S(1)} %get-tuple-element.26.mine, f32[5,32,128]{2,1,0:T(8,128)S(1)} %collective-permute-done.5.got), custom_call_target="tpu_custom_call" | custom-call | tf_op jit(solution)/shard_map/gradient/pallas_call | solution.py:385
  (1 shorter events, 0.0 us)
Async XLA Ops:
  2.0 4.4 %collective-permute-start = (f32[10,32,128]{2,1,0:T(8,128)S(1)}, f32[10,32,128]{2,1,0:T(8,128)S(1)}, u32[]{:S(2)}, u32[]{:S(2)}) collective-permute-start(f32[10,32,128]{2,1,0:T(8,128)S(1)} %get-tuple-element.16), channel_id=1, source_target_pairs={{0,1},{1,0},{2,3},{3,2},{4,5},{5,4},{6,7},{7,6},{8,9},{9,8},{10,11... | collective-permute-start | bytes 491528 | tf_op jit(solution)/shard_map/ppermute | solution.py:27
  6.4 12.0 %collective-permute-start.1 = (f32[440,128]{1,0:T(8,128)S(1)}, f32[440,128]{1,0:T(8,128)S(1)}, u32[]{:S(2)}, u32[]{:S(2)}) collective-permute-start(f32[440,128]{1,0:T(8,128)S(1)} %get-tuple-element.17), channel_id=1, source_target_pairs={{0,16},{16,32},{32,48},{48,64},{64,80},{80,96},{96,112},{112,128},... | collective-permute-start | bytes 675848 | tf_op jit(solution)/shard_map/ppermute | solution.py:27
  7.5 12.7 %collective-permute-start.2 = (f32[440,128]{1,0:T(8,128)S(1)}, f32[440,128]{1,0:T(8,128)S(1)}, u32[]{:S(2)}, u32[]{:S(2)}) collective-permute-start(f32[440,128]{1,0:T(8,128)S(1)} %get-tuple-element.18), channel_id=1, source_target_pairs={{0,240},{16,0},{32,16},{48,32},{64,48},{80,64},{96,80},{112,96},{1... | collective-permute-start | bytes 675848 | tf_op jit(solution)/shard_map/ppermute | solution.py:27
  20.8 9.4 %collective-permute-start.3 = (f32[240,128]{1,0:T(8,128)S(1)}, f32[240,128]{1,0:T(8,128)S(1)}, u32[]{:S(2)}, u32[]{:S(2)}) collective-permute-start(f32[240,128]{1,0:T(8,128)S(1)} %get-tuple-element.19), channel_id=1, source_target_pairs={{0,2},{2,4},{4,6},{6,8},{8,10},{10,12},{12,14},{14,0},{1,3},{3,5},... | collective-permute-start | bytes 368648 | tf_op jit(solution)/shard_map/ppermute | solution.py:27
  21.2 9.0 %collective-permute-start.4 = (f32[240,128]{1,0:T(8,128)S(1)}, f32[240,128]{1,0:T(8,128)S(1)}, u32[]{:S(2)}, u32[]{:S(2)}) collective-permute-start(f32[240,128]{1,0:T(8,128)S(1)} %get-tuple-element.20), channel_id=1, source_target_pairs={{0,14},{2,0},{4,2},{6,4},{8,6},{10,8},{12,10},{14,12},{1,15},{3,1}... | collective-permute-start | bytes 368648 | tf_op jit(solution)/shard_map/ppermute | solution.py:27
  30.2 9.9 %copy-start = (f32[10,10]{1,0:T(8,128)S(1)}, f32[10,10]{1,0:T(8,128)}, u32[]{:S(2)}) copy-start(f32[10,10]{1,0:T(8,128)} %vertical.1) | copy-start | bytes 1204
  37.1 3.0 %collective-permute-start.5 = (f32[5,32,128]{2,1,0:T(8,128)S(1)}, f32[5,32,128]{2,1,0:T(8,128)S(1)}, u32[]{:S(2)}, u32[]{:S(2)}) collective-permute-start(f32[5,32,128]{2,1,0:T(8,128)S(1)} %get-tuple-element.27), channel_id=1, source_target_pairs={{0,1},{1,0},{2,3},{3,2},{4,5},{5,4},{6,7},{7,6},{8,9},{9,8},{10,11... | collective-permute-start | bytes 245768 | tf_op jit(solution)/shard_map/ppermute | solution.py:27

commit v4 on v3

--- a/solution.py
+++ b/solution.py
@@ -168,7 +168,10 @@
             ref[n, :STEPS] = edge
             ref[n, STEPS + high :] = edge
 
+    zero = lax.axis_index("mem") // 2
+
     def step(source, target, begin, count):
+        begin = begin + zero
         body = pl.ds(STEPS + begin, count)
         up = pl.ds(STEPS + begin + 1, count)
         down = pl.ds(STEPS + begin - 1, count)
@@ -213,18 +216,25 @@
     return targets + [shallow_tiles.at[n] for n in range(3 * half)]
 
 
-def main_kernel(half, keep, got, below, above, total, mine, theirs, *tiles):
+def main_kernel(half, keep, got, below, above, total, mine, theirs, edge_own, *tiles):
     field_tiles, other_tiles, face_tiles, shallow_tiles = tiles
     deep, shallow = field_refs(half, keep, got)
-    rows = keep.shape[1]
+    rows, lanes = keep.shape[1:]
+    lane = lax.broadcasted_iota(jnp.int32, (1, lanes), 1)
     at = 0
+    edge_at = 0
     for n, (ref, out) in enumerate(
         zip(deep + shallow, tile_targets(half, field_tiles, face_tiles, shallow_tiles))
     ):
         width = DEEP if n < len(deep) else STEPS
-        out[:width] = below[at : at + width]
-        out[width : width + rows] = ref[...]
-        out[width + rows :] = above[at : at + width]
+        offset = 0
+        for piece in (below[at : at + width], ref[...], above[at : at + width]):
+            count = piece.shape[0]
+            out[offset : offset + count] = piece
+            own = jnp.where(lane < lanes - 3 * DEEP, turned(piece, 2 * DEEP), piece)
+            edge_own[edge_at : edge_at + count] = own
+            offset += count
+            edge_at += count
         at += width
     diffusion(half, *tiles, total)
     own = pl.ds(STEPS + DEEP, rows)
@@ -236,41 +246,31 @@
 def edge_kernel(
     half,
     keep,
-    got,
-    below,
-    above,
     left,
     right,
     main_total,
     main_mine,
     main_theirs,
+    edge_own,
     increment,
     mine,
     theirs,
     *tiles,
 ):
     field_tiles, other_tiles, face_tiles, shallow_tiles, totals = tiles
-    deep, shallow = field_refs(half, keep, got)
     rows, lanes = keep.shape[1:]
     lane = lax.broadcasted_iota(jnp.int32, (1, lanes), 1)
+    high = rows + 2 * DEEP
     at = 0
-    group_rows = {DEEP: rows + 2 * DEEP, STEPS: rows + 2 * STEPS}
-    for ref, out, (width, group, place, _) in zip(
-        deep + shallow,
+    for out, (width, group, place, _) in zip(
         tile_targets(half, field_tiles, face_tiles, shallow_tiles),
-        lane_places(len(deep), len(shallow)),
+        lane_places(4 * half, 3 * half),
     ):
-        pieces = (below[at : at + width], ref[...], above[at : at + width])
-        at += width
-        start = group * group_rows[DEEP]
-        offset = 0
-        for piece in pieces:
-            count = piece.shape[0]
-            here = pl.ds(start + offset, count)
-            sides = jnp.where(in_lanes(lane, place, width), right[here], left[here])
-            own = jnp.where(lane < lanes - 3 * DEEP, turned(piece, 2 * DEEP), piece)
-            out[offset : offset + count] = jnp.where(lane < 2 * DEEP, turned(sides, -place), own)
-            offset += count
+        count = rows + 2 * width
+        here = pl.ds(group * high, count)
+        sides = jnp.where(in_lanes(lane, place, width), right[here], left[here])
+        out[...] = jnp.where(lane < 2 * DEEP, turned(sides, -place), edge_own[at : at + count])
+        at += count
     diffusion(half, field_tiles, other_tiles, face_tiles, shallow_tiles, totals)
     body = pl.ds(STEPS + DEEP, rows)
 
@@ -284,14 +284,22 @@
         theirs[i] = joined(main_theirs[i], field_tiles[half + i, body])
 
 
-def gradient_kernel(half, vertical, alpha, mine, got, gradient):
+def partial_kernel(half, vertical, alpha, mine, partial, splat):
     base = lax.axis_index("mem") * half
     other = half - base
     for k in range(2 * half):
         total = alpha[0, k]
         for i in range(half):
             total = total + vertical[base + i, k] * mine[i]
-            total = total + vertical[other + i, k] * got[i]
+            splat[i, k : k + 1] = jnp.full((1, splat.shape[2]), vertical[other + i, k])
+        partial[k] = total
+
+
+def gradient_kernel(half, partial, splat, got, gradient):
+    for k in range(2 * half):
+        total = partial[k]
+        for i in range(half):
+            total = total + splat[i, k : k + 1] * got[i]
         gradient[0, k] = total
 
 
@@ -362,11 +370,12 @@
     )(keep, got, below, above)
     left = around(east, "lat", 1)
     right = around(west, "lat", -1)
+    edge_own = f32(high * 4 * half + (rows + 2 * STEPS) * 3 * half, lanes)
     main = pl.pallas_call(
         functools.partial(main_kernel, half),
-        out_shape=(block, block, block),
+        out_shape=(block, block, block, edge_own),
         in_specs=[VMEM] * 4,
-        out_specs=(VMEM,) * 3,
+        out_specs=(VMEM,) * 4,
         scratch_shapes=tiles,
         compiler_params=PARAMS,
         name="main",
@@ -374,22 +383,30 @@
     increment, mine, theirs = pl.pallas_call(
         functools.partial(edge_kernel, half),
         out_shape=(block, block, block),
-        in_specs=[VMEM] * 9,
+        in_specs=[VMEM] * 7,
         out_specs=(VMEM,) * 3,
         scratch_shapes=tiles + [pltpu.VMEM(block.shape, jnp.float32)],
         compiler_params=PARAMS,
         name="edge",
-    )(keep, got, below, above, left, right, *main)
+    )(keep, left, right, *main)
     got = around(theirs, "mem", 1)
 
+    partial, splat = pl.pallas_call(
+        functools.partial(partial_kernel, half),
+        out_shape=(f32(levels, rows, lanes), f32(half, levels, lanes)),
+        in_specs=[SMEM] + [VMEM] * 2,
+        out_specs=(VMEM, VMEM),
+        compiler_params=PARAMS,
+        name="partial",
+    )(vertical, alpha, mine)
     gradient = pl.pallas_call(
         functools.partial(gradient_kernel, half),
         out_shape=f32(*alpha_fields.shape),
-        in_specs=[SMEM] + [VMEM] * 3,
+        in_specs=[VMEM] * 3,
         out_specs=VMEM,
         compiler_params=PARAMS,
         name="gradient",
-    )(vertical, alpha, mine, got)
+    )(partial, splat, got)
     return (increment, gradient)
 
 

time: 41.7 us -> 41 us (0.983)
  waiting for transfers between devices: 9.32 us -> 8.56 us
    ppermute x6, waiting for transfers between devices: 9.32 us -> 8.56 us  [around(): return lax.ppermute(value, axis, pairs)]
    pallas_call x0 -> x1, Pallas kernels: none -> 0.75 us  [local(): pl.pallas_call(functools.partial(partial_kernel, half), out_shape=(f32(le...]
    pallas_call x1, Pallas kernels: 1.47 us -> 0.73 us  [local(): pl.pallas_call(functools.partial(gradient_kernel, half), out_shape=f32(*a...]
  transfers between devices with their start and end apart: 6 -> 6, of which waited for: 4 -> 4; matrix products, arithmetic and copies ran while one was open for 0% -> 0% of each run, Pallas kernels for 14% -> 16%
where the time goes in v4:
time: 41 us; the launch traced here: 40.9 us
  Pallas kernels  16.1 us (39%)
  starting transfers between devices  15.5 us (38%)
  waiting for transfers between devices  8.56 us (21%)
  between operations  0.7 us (2%)
    ppermute x6, starting transfers between devices, around(): return lax.ppermute(value, axis, pairs)  15.5 us
    ppermute x6, waiting for transfers between devices, around(): return lax.ppermute(value, axis, pairs)  8.56 us
    pallas_call x1, Pallas kernels, local(): pl.pallas_call(functools.partial(edge_kernel, half), out_shape=(block, bl...  6.66 us
    pallas_call x1, Pallas kernels, local(): pl.pallas_call(functools.partial(main_kernel, half), out_shape=(block, bl...  5.96 us
    pallas_call x1, Pallas kernels, local(): pl.pallas_call(functools.partial(prepare_kernel, half), out_shape=(f32(6...  1.39 us
  transfers between devices with their start and end apart: 6, of which 4 were waited for; matrix products, arithmetic and copies ran while one was open for 0% of the time, Pallas kernels for 16%

profile of v4, /device:TPU:1, one launch (start us, length us, event | category | flops | bytes accessed | tf_op | source)
XLA Modules:
  0.0 40.9 jit_solution(11973063689251646240)
XLA Ops:
  0.6 1.4 %prepare.1 = (f32[30,32,128]{2,1,0:T(8,128)S(1)}, f32[10,32,128]{2,1,0:T(8,128)S(1)}, f32[1,10,32,128]{3,2,1,0:T(8,128)S(1)}) custom-call(f32[10,10]{1,0:T(8,128)} %vertical.1, f32[1,10,32,128]{3,2,1,0:T(8,128)} %alpha_hbm.1, f32[1,10,32,128]{3,2,1,0:T(8,128)} %anomaly_hbm.1, f32[10,32,128]{2,1,0:T(8,128)} %lon_hbm.1, f32[10,32,128]{2,1,0:T(8,128)} %lat_hbm.1, ...), custom_call_target="tpu_custom_call" | custom-call | tf_op jit(solution)/shard_map/prepare/pallas_call | solution.py:334
  2.0 3.3 %collective-permute-start = (f32[10,32,128]{2,1,0:T(8,128)S(1)}, f32[10,32,128]{2,1,0:T(8,128)S(1)}, u32[]{:S(2)}, u32[]{:S(2)}) collective-permute-start(f32[10,32,128]{2,1,0:T(8,128)S(1)} %get-tuple-element.19), channel_id=1, source_target_pairs={{0,1},{1,0},{2,3},{3,2},{4,5},{5,4},{6,7},{7,6},{8,9},{9,8},{10,11... | collective-permute-start | bytes 491528 | tf_op jit(solution)/shard_map/ppermute | solution.py:27
  5.4 1.0 %collective-permute-done.got = f32[10,32,128]{2,1,0:T(8,128)S(1)} collective-permute-done((f32[10,32,128]{2,1,0:T(8,128)S(1)}, f32[10,32,128]{2,1,0:T(8,128)S(1)}, u32[]{:S(2)}, u32[]{:S(2)}) %collective-permute-start) | collective-permute-done | bytes 163872 | tf_op jit(solution)/shard_map/ppermute | solution.py:27
  6.4 1.1 %collective-permute-start.1 = (f32[440,128]{1,0:T(8,128)S(1)}, f32[440,128]{1,0:T(8,128)S(1)}, u32[]{:S(2)}, u32[]{:S(2)}) collective-permute-start(f32[440,128]{1,0:T(8,128)S(1)} %get-tuple-element.20), channel_id=1, source_target_pairs={{0,16},{16,32},{32,48},{48,64},{64,80},{80,96},{96,112},{112,128},... | collective-permute-start | bytes 675848 | tf_op jit(solution)/shard_map/ppermute | solution.py:27
  7.5 5.4 %collective-permute-start.2 = (f32[440,128]{1,0:T(8,128)S(1)}, f32[440,128]{1,0:T(8,128)S(1)}, u32[]{:S(2)}, u32[]{:S(2)}) collective-permute-start(f32[440,128]{1,0:T(8,128)S(1)} %get-tuple-element.21), channel_id=1, source_target_pairs={{0,240},{16,0},{32,16},{48,32},{64,48},{80,64},{96,80},{112,96},{1... | collective-permute-start | bytes 675848 | tf_op jit(solution)/shard_map/ppermute | solution.py:27
  12.9 5.5 %collective-permute-done.1.below = f32[440,128]{1,0:T(8,128)S(1)} collective-permute-done((f32[440,128]{1,0:T(8,128)S(1)}, f32[440,128]{1,0:T(8,128)S(1)}, u32[]{:S(2)}, u32[]{:S(2)}) %collective-permute-start.1) | collective-permute-done | bytes 225312 | tf_op jit(solution)/shard_map/ppermute | solution.py:27
  18.4 1.8 %collective-permute-done.2.above = f32[440,128]{1,0:T(8,128)S(1)} collective-permute-done((f32[440,128]{1,0:T(8,128)S(1)}, f32[440,128]{1,0:T(8,128)S(1)}, u32[]{:S(2)}, u32[]{:S(2)}) %collective-permute-start.2) | collective-permute-done | bytes 225312 | tf_op jit(solution)/shard_map/ppermute | solution.py:27
  20.3 0.5 %columns.1 = (f32[240,128]{1,0:T(8,128)S(1)}, f32[240,128]{1,0:T(8,128)S(1)}) custom-call(f32[30,32,128]{2,1,0:T(8,128)S(1)} %get-tuple-element.18.keep, f32[10,32,128]{2,1,0:T(8,128)S(1)} %collective-permute-done.got, f32[440,128]{1,0:T(8,128)S(1)} %collective-permute-done.1.below, f32[440,128]{1,0:T(8,128)S(1)} %collective-permute-done.2.above), custom_call_target="tpu_custom_call" | custom-call | tf_op jit(solution)/shard_map/columns/pallas_call | solution.py:363
  20.8 0.4 collective-permute-start.3
  21.2 3.3 %collective-permute-start.4 = (f32[240,128]{1,0:T(8,128)S(1)}, f32[240,128]{1,0:T(8,128)S(1)}, u32[]{:S(2)}, u32[]{:S(2)}) collective-permute-start(f32[240,128]{1,0:T(8,128)S(1)} %get-tuple-element.23), channel_id=1, source_target_pairs={{0,14},{2,0},{4,2},{6,4},{8,6},{10,8},{12,10},{14,12},{1,15},{3,1}... | collective-permute-start | bytes 368648 | tf_op jit(solution)/shard_map/ppermute | solution.py:27
  24.5 6.0 %main.1 = (f32[5,32,128]{2,1,0:T(8,128)S(1)}, f32[5,32,128]{2,1,0:T(8,128)S(1)}, f32[5,32,128]{2,1,0:T(8,128)S(1)}, f32[2000,128]{1,0:T(8,128)S(1)}) custom-call(f32[30,32,128]{2,1,0:T(8,128)S(1)} %get-tuple-element.18.keep, f32[10,32,128]{2,1,0:T(8,128)S(1)} %collective-permute-done.got, f32[440,128]{1,0:T(8,128)S(1)} %collective-permute-done.1.below, ...), custom_call_target="tpu_custom_call" | custom-call | tf_op jit(solution)/shard_map/main/pallas_call | solution.py:374
  30.4 0.0 collective-permute-done.3.left
  30.4 0.0 collective-permute-done.4.right
  30.4 0.0 copy-start
  30.5 6.7 %edge.1 = (f32[5,32,128]{2,1,0:T(8,128)}, f32[5,32,128]{2,1,0:T(8,128)S(1)}, f32[5,32,128]{2,1,0:T(8,128)S(1)}) custom-call(f32[30,32,128]{2,1,0:T(8,128)S(1)} %get-tuple-element.18.keep, f32[240,128]{1,0:T(8,128)S(1)} %collective-permute-done.3.left, f32[240,128]{1,0:T(8,128)S(1)} %collective-permute-done.4.right, ...), custom_call_target="tpu_custom_call" | custom-call | tf_op jit(solution)/shard_map/edge/pallas_call | solution.py:383
  37.1 2.1 %collective-permute-start.5 = (f32[5,32,128]{2,1,0:T(8,128)S(1)}, f32[5,32,128]{2,1,0:T(8,128)S(1)}, u32[]{:S(2)}, u32[]{:S(2)}) collective-permute-start(f32[5,32,128]{2,1,0:T(8,128)S(1)} %get-tuple-element.33), channel_id=1, source_target_pairs={{0,1},{1,0},{2,3},{3,2},{4,5},{5,4},{6,7},{7,6},{8,9},{9,8},{10,11... | collective-permute-start | bytes 245768 | tf_op jit(solution)/shard_map/ppermute | solution.py:27
  39.2 0.0 copy-done
  39.2 0.8 %partial.1 = (f32[10,32,128]{2,1,0:T(8,128)S(1)}, f32[5,10,128]{2,1,0:T(8,128)S(1)}) custom-call(f32[10,10]{1,0:T(8,128)S(1)} %copy-done, f32[1,10,32,128]{3,2,1,0:T(8,128)S(1)} %get-tuple-element.29.alpha, f32[5,32,128]{2,1,0:T(8,128)S(1)} %get-tuple-element.30.mine), custom_call_target="tpu_custom_call" | custom-call | tf_op jit(solution)/shard_map/partial/pallas_call | solution.py:394
  40.0 0.2 collective-permute-done.5.got
  40.1 0.7 %gradient.1 = f32[1,10,32,128]{3,2,1,0:T(8,128)} custom-call(f32[10,32,128]{2,1,0:T(8,128)S(1)} %get-tuple-element.31.partial, f32[5,10,128]{2,1,0:T(8,128)S(1)} %get-tuple-element.32.splat, f32[5,32,128]{2,1,0:T(8,128)S(1)} %collective-permute-done.5.got), custom_call_target="tpu_custom_call" | custom-call | tf_op jit(solution)/shard_map/gradient/pallas_call | solution.py:402
  (1 shorter events, 0.0 us)
Async XLA Ops:
  2.0 4.4 %collective-permute-start = (f32[10,32,128]{2,1,0:T(8,128)S(1)}, f32[10,32,128]{2,1,0:T(8,128)S(1)}, u32[]{:S(2)}, u32[]{:S(2)}) collective-permute-start(f32[10,32,128]{2,1,0:T(8,128)S(1)} %get-tuple-element.19), channel_id=1, source_target_pairs={{0,1},{1,0},{2,3},{3,2},{4,5},{5,4},{6,7},{7,6},{8,9},{9,8},{10,11... | collective-permute-start | bytes 491528 | tf_op jit(solution)/shard_map/ppermute | solution.py:27
  6.4 12.0 %collective-permute-start.1 = (f32[440,128]{1,0:T(8,128)S(1)}, f32[440,128]{1,0:T(8,128)S(1)}, u32[]{:S(2)}, u32[]{:S(2)}) collective-permute-start(f32[440,128]{1,0:T(8,128)S(1)} %get-tuple-element.20), channel_id=1, source_target_pairs={{0,16},{16,32},{32,48},{48,64},{64,80},{80,96},{96,112},{112,128},... | collective-permute-start | bytes 675848 | tf_op jit(solution)/shard_map/ppermute | solution.py:27
  7.5 12.7 %collective-permute-start.2 = (f32[440,128]{1,0:T(8,128)S(1)}, f32[440,128]{1,0:T(8,128)S(1)}, u32[]{:S(2)}, u32[]{:S(2)}) collective-permute-start(f32[440,128]{1,0:T(8,128)S(1)} %get-tuple-element.21), channel_id=1, source_target_pairs={{0,240},{16,0},{32,16},{48,32},{64,48},{80,64},{96,80},{112,96},{1... | collective-permute-start | bytes 675848 | tf_op jit(solution)/shard_map/ppermute | solution.py:27
  20.8 9.6 %collective-permute-start.3 = (f32[240,128]{1,0:T(8,128)S(1)}, f32[240,128]{1,0:T(8,128)S(1)}, u32[]{:S(2)}, u32[]{:S(2)}) collective-permute-start(f32[240,128]{1,0:T(8,128)S(1)} %get-tuple-element.22), channel_id=1, source_target_pairs={{0,2},{2,4},{4,6},{6,8},{8,10},{10,12},{12,14},{14,0},{1,3},{3,5},... | collective-permute-start | bytes 368648 | tf_op jit(solution)/shard_map/ppermute | solution.py:27
  21.2 9.2 %collective-permute-start.4 = (f32[240,128]{1,0:T(8,128)S(1)}, f32[240,128]{1,0:T(8,128)S(1)}, u32[]{:S(2)}, u32[]{:S(2)}) collective-permute-start(f32[240,128]{1,0:T(8,128)S(1)} %get-tuple-element.23), channel_id=1, source_target_pairs={{0,14},{2,0},{4,2},{6,4},{8,6},{10,8},{12,10},{14,12},{1,15},{3,1}... | collective-permute-start | bytes 368648 | tf_op jit(solution)/shard_map/ppermute | solution.py:27
  30.4 8.8 %copy-start = (f32[10,10]{1,0:T(8,128)S(1)}, f32[10,10]{1,0:T(8,128)}, u32[]{:S(2)}) copy-start(f32[10,10]{1,0:T(8,128)} %vertical.1) | copy-start | bytes 1204
  37.1 3.0 %collective-permute-start.5 = (f32[5,32,128]{2,1,0:T(8,128)S(1)}, f32[5,32,128]{2,1,0:T(8,128)S(1)}, u32[]{:S(2)}, u32[]{:S(2)}) collective-permute-start(f32[5,32,128]{2,1,0:T(8,128)S(1)} %get-tuple-element.33), channel_id=1, source_target_pairs={{0,1},{1,0},{2,3},{3,2},{4,5},{5,4},{6,7},{7,6},{8,9},{9,8},{10,11... | collective-permute-start | bytes 245768 | tf_op jit(solution)/shard_map/ppermute | solution.py:27

commit v5 on v4

--- a/solution.py
+++ b/solution.py
@@ -11,6 +11,7 @@
 STEPS = 8
 DEEP = 2 * STEPS
 LANES = 128
+TILE = 8
 VMEM = pl.BlockSpec(memory_space=pltpu.VMEM)
 SMEM = pl.BlockSpec(memory_space=pltpu.SMEM)
 HBM = pl.BlockSpec(memory_space=pltpu.HBM)
@@ -170,32 +171,31 @@
 
     zero = lax.axis_index("mem") // 2
 
-    def step(source, target, begin, count):
-        begin = begin + zero
-        body = pl.ds(STEPS + begin, count)
-        up = pl.ds(STEPS + begin + 1, count)
-        down = pl.ds(STEPS + begin - 1, count)
+    def step(source, target, begin, end):
         for i in range(half):
-            lon_coef = face_tiles[i, body]
-            lon_before = face_tiles[i, down]
-            lat_coef = face_tiles[half + i, body]
-            for n in (i, half + i):
-                field = source[n, body]
-                flux_x = lon_coef * (source[n, up] - field)
-                flux_x = flux_x - lon_before * (field - source[n, down])
-                flux_y = lat_coef * (turned(field, -1) - field)
-                target[n, body] = (field + flux_x) + (flux_y - turned(flux_y, 1))
+            for at in range(begin, end, TILE):
+                here = pl.ds(at, TILE)
+                up = pl.ds(at + 1 + zero, TILE)
+                down = pl.ds(at - 1 + zero, TILE)
+                lon_coef = face_tiles[i, here]
+                lon_before = face_tiles[i, down]
+                lat_coef = face_tiles[half + i, here]
+                for n in (i, half + i):
+                    field = source[n, here]
+                    flux_x = lon_coef * (source[n, up] - field)
+                    flux_x = flux_x - lon_before * (field - source[n, down])
+                    flux_y = lat_coef * (turned(field, -1) - field)
+                    target[n, here] = (field + flux_x) + (flux_y - turned(flux_y, 1))
 
     def root(margin):
-        for begin in (margin, margin + STEPS // 2):
-            count = high - 2 * begin
-
-            def pair(_, carry):
-                step(field_tiles, other_tiles, begin, count)
-                step(other_tiles, field_tiles, begin, count)
-                return carry
-
-            lax.fori_loop(0, STEPS // 4, pair, 0)
+        begin, end = STEPS + margin, STEPS + high - margin
+
+        def pair(_, carry):
+            step(field_tiles, other_tiles, begin, end)
+            step(other_tiles, field_tiles, begin, end)
+            return carry
+
+        lax.fori_loop(0, STEPS // 2, pair, 0)
 
     root(0)
     inner = pl.ds(2 * STEPS, rows + 2 * STEPS)

time: 41 us -> 37.7 us (0.920)
  Pallas kernels: 16.1 us -> 12.8 us
    pallas_call x1, Pallas kernels: 5.96 us -> 4.32 us  [local(): pl.pallas_call(functools.partial(main_kernel, half), out_shape=(block, bl...]
    pallas_call x1, Pallas kernels: 6.66 us -> 5.03 us  [local(): pl.pallas_call(functools.partial(edge_kernel, half), out_shape=(block, bl...]
  transfers between devices with their start and end apart: 6 -> 6, of which waited for: 4 -> 4; matrix products, arithmetic and copies ran while one was open for 0% -> 0% of each run, Pallas kernels for 16% -> 13%
where the time goes in v5:
time: 37.7 us; the launch traced here: 37.6 us
  starting transfers between devices  15.5 us (41%)
  Pallas kernels  12.8 us (34%)
  waiting for transfers between devices  8.56 us (23%)
  between operations  0.69 us (2%)
    ppermute x6, starting transfers between devices, around(): return lax.ppermute(value, axis, pairs)  15.5 us
    ppermute x6, waiting for transfers between devices, around(): return lax.ppermute(value, axis, pairs)  8.56 us
    pallas_call x1, Pallas kernels, local(): pl.pallas_call(functools.partial(edge_kernel, half), out_shape=(block, bl...  5.03 us
    pallas_call x1, Pallas kernels, local(): pl.pallas_call(functools.partial(main_kernel, half), out_shape=(block, bl...  4.32 us
    pallas_call x1, Pallas kernels, local(): pl.pallas_call(functools.partial(prepare_kernel, half), out_shape=(f32(6...  1.39 us
  transfers between devices with their start and end apart: 6, of which 4 were waited for; matrix products, arithmetic and copies ran while one was open for 0% of the time, Pallas kernels for 13%

profile of v5, /device:TPU:1, one launch (start us, length us, event | category | flops | bytes accessed | tf_op | source)
XLA Modules:
  0.0 37.6 jit_solution(366500461360968271)
XLA Ops:
  0.6 1.4 %prepare.1 = (f32[30,32,128]{2,1,0:T(8,128)S(1)}, f32[10,32,128]{2,1,0:T(8,128)S(1)}, f32[1,10,32,128]{3,2,1,0:T(8,128)S(1)}) custom-call(f32[10,10]{1,0:T(8,128)} %vertical.1, f32[1,10,32,128]{3,2,1,0:T(8,128)} %alpha_hbm.1, f32[1,10,32,128]{3,2,1,0:T(8,128)} %anomaly_hbm.1, f32[10,32,128]{2,1,0:T(8,128)} %lon_hbm.1, f32[10,32,128]{2,1,0:T(8,128)} %lat_hbm.1, ...), custom_call_target="tpu_custom_call" | custom-call | tf_op jit(solution)/shard_map/prepare/pallas_call | solution.py:334
  2.0 3.3 %collective-permute-start = (f32[10,32,128]{2,1,0:T(8,128)S(1)}, f32[10,32,128]{2,1,0:T(8,128)S(1)}, u32[]{:S(2)}, u32[]{:S(2)}) collective-permute-start(f32[10,32,128]{2,1,0:T(8,128)S(1)} %get-tuple-element.19), channel_id=1, source_target_pairs={{0,1},{1,0},{2,3},{3,2},{4,5},{5,4},{6,7},{7,6},{8,9},{9,8},{10,11... | collective-permute-start | bytes 491528 | tf_op jit(solution)/shard_map/ppermute | solution.py:28
  5.4 1.0 %collective-permute-done.got = f32[10,32,128]{2,1,0:T(8,128)S(1)} collective-permute-done((f32[10,32,128]{2,1,0:T(8,128)S(1)}, f32[10,32,128]{2,1,0:T(8,128)S(1)}, u32[]{:S(2)}, u32[]{:S(2)}) %collective-permute-start) | collective-permute-done | bytes 163872 | tf_op jit(solution)/shard_map/ppermute | solution.py:28
  6.4 1.1 %collective-permute-start.1 = (f32[440,128]{1,0:T(8,128)S(1)}, f32[440,128]{1,0:T(8,128)S(1)}, u32[]{:S(2)}, u32[]{:S(2)}) collective-permute-start(f32[440,128]{1,0:T(8,128)S(1)} %get-tuple-element.20), channel_id=1, source_target_pairs={{0,16},{16,32},{32,48},{48,64},{64,80},{80,96},{96,112},{112,128},... | collective-permute-start | bytes 675848 | tf_op jit(solution)/shard_map/ppermute | solution.py:28
  7.5 5.4 %collective-permute-start.2 = (f32[440,128]{1,0:T(8,128)S(1)}, f32[440,128]{1,0:T(8,128)S(1)}, u32[]{:S(2)}, u32[]{:S(2)}) collective-permute-start(f32[440,128]{1,0:T(8,128)S(1)} %get-tuple-element.21), channel_id=1, source_target_pairs={{0,240},{16,0},{32,16},{48,32},{64,48},{80,64},{96,80},{112,96},{1... | collective-permute-start | bytes 675848 | tf_op jit(solution)/shard_map/ppermute | solution.py:28
  12.9 5.5 %collective-permute-done.1.below = f32[440,128]{1,0:T(8,128)S(1)} collective-permute-done((f32[440,128]{1,0:T(8,128)S(1)}, f32[440,128]{1,0:T(8,128)S(1)}, u32[]{:S(2)}, u32[]{:S(2)}) %collective-permute-start.1) | collective-permute-done | bytes 225312 | tf_op jit(solution)/shard_map/ppermute | solution.py:28
  18.4 1.8 %collective-permute-done.2.above = f32[440,128]{1,0:T(8,128)S(1)} collective-permute-done((f32[440,128]{1,0:T(8,128)S(1)}, f32[440,128]{1,0:T(8,128)S(1)}, u32[]{:S(2)}, u32[]{:S(2)}) %collective-permute-start.2) | collective-permute-done | bytes 225312 | tf_op jit(solution)/shard_map/ppermute | solution.py:28
  20.3 0.5 %columns.1 = (f32[240,128]{1,0:T(8,128)S(1)}, f32[240,128]{1,0:T(8,128)S(1)}) custom-call(f32[30,32,128]{2,1,0:T(8,128)S(1)} %get-tuple-element.18.keep, f32[10,32,128]{2,1,0:T(8,128)S(1)} %collective-permute-done.got, f32[440,128]{1,0:T(8,128)S(1)} %collective-permute-done.1.below, f32[440,128]{1,0:T(8,128)S(1)} %collective-permute-done.2.above), custom_call_target="tpu_custom_call" | custom-call | tf_op jit(solution)/shard_map/columns/pallas_call | solution.py:363
  20.8 0.4 %collective-permute-start.3 = (f32[240,128]{1,0:T(8,128)S(1)}, f32[240,128]{1,0:T(8,128)S(1)}, u32[]{:S(2)}, u32[]{:S(2)}) collective-permute-start(f32[240,128]{1,0:T(8,128)S(1)} %get-tuple-element.22), channel_id=1, source_target_pairs={{0,2},{2,4},{4,6},{6,8},{8,10},{10,12},{12,14},{14,0},{1,3},{3,5},... | collective-permute-start | bytes 368648 | tf_op jit(solution)/shard_map/ppermute | solution.py:28
  21.2 3.3 %collective-permute-start.4 = (f32[240,128]{1,0:T(8,128)S(1)}, f32[240,128]{1,0:T(8,128)S(1)}, u32[]{:S(2)}, u32[]{:S(2)}) collective-permute-start(f32[240,128]{1,0:T(8,128)S(1)} %get-tuple-element.23), channel_id=1, source_target_pairs={{0,14},{2,0},{4,2},{6,4},{8,6},{10,8},{12,10},{14,12},{1,15},{3,1}... | collective-permute-start | bytes 368648 | tf_op jit(solution)/shard_map/ppermute | solution.py:28
  24.5 4.3 %main.1 = (f32[5,32,128]{2,1,0:T(8,128)S(1)}, f32[5,32,128]{2,1,0:T(8,128)S(1)}, f32[5,32,128]{2,1,0:T(8,128)S(1)}, f32[2000,128]{1,0:T(8,128)S(1)}) custom-call(f32[30,32,128]{2,1,0:T(8,128)S(1)} %get-tuple-element.18.keep, f32[10,32,128]{2,1,0:T(8,128)S(1)} %collective-permute-done.got, f32[440,128]{1,0:T(8,128)S(1)} %collective-permute-done.1.below, ...), custom_call_target="tpu_custom_call" | custom-call | tf_op jit(solution)/shard_map/main/pallas_call | solution.py:374
  28.8 0.0 collective-permute-done.3.left
  28.8 0.0 collective-permute-done.4.right
  28.8 0.0 copy-start
  28.8 5.0 %edge.1 = (f32[5,32,128]{2,1,0:T(8,128)}, f32[5,32,128]{2,1,0:T(8,128)S(1)}, f32[5,32,128]{2,1,0:T(8,128)S(1)}) custom-call(f32[30,32,128]{2,1,0:T(8,128)S(1)} %get-tuple-element.18.keep, f32[240,128]{1,0:T(8,128)S(1)} %collective-permute-done.3.left, f32[240,128]{1,0:T(8,128)S(1)} %collective-permute-done.4.right, ...), custom_call_target="tpu_custom_call" | custom-call | tf_op jit(solution)/shard_map/edge/pallas_call | solution.py:383
  33.9 2.1 %collective-permute-start.5 = (f32[5,32,128]{2,1,0:T(8,128)S(1)}, f32[5,32,128]{2,1,0:T(8,128)S(1)}, u32[]{:S(2)}, u32[]{:S(2)}) collective-permute-start(f32[5,32,128]{2,1,0:T(8,128)S(1)} %get-tuple-element.33), channel_id=1, source_target_pairs={{0,1},{1,0},{2,3},{3,2},{4,5},{5,4},{6,7},{7,6},{8,9},{9,8},{10,11... | collective-permute-start | bytes 245768 | tf_op jit(solution)/shard_map/ppermute | solution.py:28
  35.9 0.0 copy-done
  35.9 0.8 %partial.1 = (f32[10,32,128]{2,1,0:T(8,128)S(1)}, f32[5,10,128]{2,1,0:T(8,128)S(1)}) custom-call(f32[10,10]{1,0:T(8,128)S(1)} %copy-done, f32[1,10,32,128]{3,2,1,0:T(8,128)S(1)} %get-tuple-element.29.alpha, f32[5,32,128]{2,1,0:T(8,128)S(1)} %get-tuple-element.30.mine), custom_call_target="tpu_custom_call" | custom-call | tf_op jit(solution)/shard_map/partial/pallas_call | solution.py:394
  36.7 0.2 collective-permute-done.5.got
  36.9 0.7 %gradient.1 = f32[1,10,32,128]{3,2,1,0:T(8,128)} custom-call(f32[10,32,128]{2,1,0:T(8,128)S(1)} %get-tuple-element.31.partial, f32[5,10,128]{2,1,0:T(8,128)S(1)} %get-tuple-element.32.splat, f32[5,32,128]{2,1,0:T(8,128)S(1)} %collective-permute-done.5.got), custom_call_target="tpu_custom_call" | custom-call | tf_op jit(solution)/shard_map/gradient/pallas_call | solution.py:402
  (1 shorter events, 0.0 us)
Async XLA Ops:
  2.0 4.4 %collective-permute-start = (f32[10,32,128]{2,1,0:T(8,128)S(1)}, f32[10,32,128]{2,1,0:T(8,128)S(1)}, u32[]{:S(2)}, u32[]{:S(2)}) collective-permute-start(f32[10,32,128]{2,1,0:T(8,128)S(1)} %get-tuple-element.19), channel_id=1, source_target_pairs={{0,1},{1,0},{2,3},{3,2},{4,5},{5,4},{6,7},{7,6},{8,9},{9,8},{10,11... | collective-permute-start | bytes 491528 | tf_op jit(solution)/shard_map/ppermute | solution.py:28
  6.4 12.0 %collective-permute-start.1 = (f32[440,128]{1,0:T(8,128)S(1)}, f32[440,128]{1,0:T(8,128)S(1)}, u32[]{:S(2)}, u32[]{:S(2)}) collective-permute-start(f32[440,128]{1,0:T(8,128)S(1)} %get-tuple-element.20), channel_id=1, source_target_pairs={{0,16},{16,32},{32,48},{48,64},{64,80},{80,96},{96,112},{112,128},... | collective-permute-start | bytes 675848 | tf_op jit(solution)/shard_map/ppermute | solution.py:28
  7.5 12.7 %collective-permute-start.2 = (f32[440,128]{1,0:T(8,128)S(1)}, f32[440,128]{1,0:T(8,128)S(1)}, u32[]{:S(2)}, u32[]{:S(2)}) collective-permute-start(f32[440,128]{1,0:T(8,128)S(1)} %get-tuple-element.21), channel_id=1, source_target_pairs={{0,240},{16,0},{32,16},{48,32},{64,48},{80,64},{96,80},{112,96},{1... | collective-permute-start | bytes 675848 | tf_op jit(solution)/shard_map/ppermute | solution.py:28
  20.8 8.0 %collective-permute-start.3 = (f32[240,128]{1,0:T(8,128)S(1)}, f32[240,128]{1,0:T(8,128)S(1)}, u32[]{:S(2)}, u32[]{:S(2)}) collective-permute-start(f32[240,128]{1,0:T(8,128)S(1)} %get-tuple-element.22), channel_id=1, source_target_pairs={{0,2},{2,4},{4,6},{6,8},{8,10},{10,12},{12,14},{14,0},{1,3},{3,5},... | collective-permute-start | bytes 368648 | tf_op jit(solution)/shard_map/ppermute | solution.py:28
  21.2 7.6 %collective-permute-start.4 = (f32[240,128]{1,0:T(8,128)S(1)}, f32[240,128]{1,0:T(8,128)S(1)}, u32[]{:S(2)}, u32[]{:S(2)}) collective-permute-start(f32[240,128]{1,0:T(8,128)S(1)} %get-tuple-element.23), channel_id=1, source_target_pairs={{0,14},{2,0},{4,2},{6,4},{8,6},{10,8},{12,10},{14,12},{1,15},{3,1}... | collective-permute-start | bytes 368648 | tf_op jit(solution)/shard_map/ppermute | solution.py:28
  28.8 7.1 %copy-start = (f32[10,10]{1,0:T(8,128)S(1)}, f32[10,10]{1,0:T(8,128)}, u32[]{:S(2)}) copy-start(f32[10,10]{1,0:T(8,128)} %vertical.1) | copy-start | bytes 1204
  33.9 3.0 %collective-permute-start.5 = (f32[5,32,128]{2,1,0:T(8,128)S(1)}, f32[5,32,128]{2,1,0:T(8,128)S(1)}, u32[]{:S(2)}, u32[]{:S(2)}) collective-permute-start(f32[5,32,128]{2,1,0:T(8,128)S(1)} %get-tuple-element.33), channel_id=1, source_target_pairs={{0,1},{1,0},{2,3},{3,2},{4,5},{5,4},{6,7},{7,6},{8,9},{9,8},{10,11... | collective-permute-start | bytes 245768 | tf_op jit(solution)/shard_map/ppermute | solution.py:28

commit v6 on v5

--- a/solution.py
+++ b/solution.py
@@ -28,13 +28,13 @@
     return lax.ppermute(value, axis, pairs)
 
 
-def lane_places(deep, shallow):
+def lane_places(half):
     places = []
-    for width, count in ((DEEP, deep), (STEPS, shallow)):
+    for width, count in ((DEEP, 4 * half), (STEPS, 3 * half)):
         for i in range(count):
             group, place = divmod(i * width, LANES)
             if width == STEPS:
-                group += -(-deep * DEEP // LANES)
+                group += -(-4 * half * DEEP // LANES)
             places.append((width, group, place, (place + 2 * DEEP - width) % LANES))
     return places
 
@@ -108,24 +108,36 @@
 
 
 def field_refs(half, keep, got):
-    deep = [keep.at[i] for i in range(half)]
-    deep += [got.at[i] for i in range(half)]
-    deep += [keep.at[half + i] for i in range(2 * half)]
-    shallow = [keep.at[3 * half + i] for i in range(half)]
-    shallow += [got.at[half + i] for i in range(half)]
-    shallow += [keep.at[4 * half + i] for i in range(half)]
-    return deep, shallow
-
-
-def strip_kernel(half, keep, got, first, final):
-    deep, shallow = field_refs(half, keep, got)
-    rows = keep.shape[1]
+    deep = [keep.at[i] for i in range(3 * half)] + [got.at[i] for i in range(half)]
+    shallow = [keep.at[3 * half + i] for i in range(2 * half)]
+    return deep + shallow + [got.at[half + i] for i in range(half)]
+
+
+def widths(half):
+    return [DEEP] * (4 * half) + [STEPS] * (3 * half)
+
+
+def halo_refs(half, kept, gotten):
+    refs = []
+    ends = {False: 0, True: 0}
+    for n, width in enumerate(widths(half)):
+        late = 3 * half <= n < 4 * half or n >= 6 * half
+        pack = gotten if late else kept
+        refs.append(pack.at[pl.ds(ends[late], width)])
+        ends[late] += width
+    return refs
+
+
+def strip_kernel(counts, source, first, final):
+    rows = source.shape[1]
     at = 0
-    for width, fields in ((DEEP, deep), (STEPS, shallow)):
-        for ref in fields:
-            first[at : at + width] = ref[:width]
-            final[at : at + width] = ref[rows - width :]
+    n = 0
+    for count, width in counts:
+        for _ in range(count):
+            first[at : at + width] = source[n, :width]
+            final[at : at + width] = source[n, rows - width :]
             at += width
+            n += 1
 
 
 def in_lanes(lane, place, width):
@@ -134,19 +146,17 @@
     return jnp.logical_and(lane >= place, lane < place + width)
 
 
-def column_kernel(half, keep, got, below, above, west, east):
-    deep, shallow = field_refs(half, keep, got)
-    rows, lanes = keep.shape[1:]
-    high = rows + 2 * DEEP
+def column_kernel(half, keep, got, kept_below, got_below, kept_above, got_above, west, east):
+    lanes = keep.shape[2]
     lane = lax.broadcasted_iota(jnp.int32, (1, lanes), 1)
     packs = {}
-    at = 0
-    for ref, (width, group, place, opposite) in zip(
-        deep + shallow, lane_places(len(deep), len(shallow))
+    for below, ref, above, (width, group, place, opposite) in zip(
+        halo_refs(half, kept_below, got_below),
+        field_refs(half, keep, got),
+        halo_refs(half, kept_above, got_above),
+        lane_places(half),
     ):
-        pieces = (below[at : at + width], ref[...], above[at : at + width])
-        at += width
-        for n, piece in enumerate(pieces):
+        for n, piece in enumerate((below[...], ref[...], above[...])):
             heads, tails = packs.get((group, n), (0.0, 0.0))
             heads = jnp.where(in_lanes(lane, place, width), turned(piece, place), heads)
             tails = jnp.where(in_lanes(lane, opposite, width), turned(piece, place + 2 * DEEP), tails)
@@ -159,19 +169,25 @@
         at += count
 
 
-def diffusion(half, field_tiles, other_tiles, face_tiles, shallow_tiles, totals):
-    high = field_tiles.shape[1] - 2 * STEPS
+def split_tiles(half, tiles):
+    return tiles[:half], tiles[half : 2 * half], tiles[2 * half], tiles[2 * half + 1]
+
+
+def diffusion(half, tiles, totals):
+    fields, others, face_tiles, shallow_tiles = split_tiles(half, tiles)
+    high = fields[0].shape[1] - 2 * STEPS
     rows = high - 2 * DEEP
-    edge = jnp.zeros((STEPS, field_tiles.shape[2]), jnp.float32)
+    edge = jnp.zeros((STEPS, fields[0].shape[2]), jnp.float32)
     for n in range(2 * half):
         face_tiles[n, :STEPS] = edge
-        for ref in (field_tiles, other_tiles):
-            ref[n, :STEPS] = edge
-            ref[n, STEPS + high :] = edge
+    for ref in (*fields, *others):
+        for m in range(2):
+            ref[m, :STEPS] = edge
+            ref[m, STEPS + high :] = edge
 
     zero = lax.axis_index("mem") // 2
 
-    def step(source, target, begin, end):
+    def step(sources, targets, begin, end):
         for i in range(half):
             for at in range(begin, end, TILE):
                 here = pl.ds(at, TILE)
@@ -180,67 +196,83 @@
                 lon_coef = face_tiles[i, here]
                 lon_before = face_tiles[i, down]
                 lat_coef = face_tiles[half + i, here]
-                for n in (i, half + i):
-                    field = source[n, here]
-                    flux_x = lon_coef * (source[n, up] - field)
-                    flux_x = flux_x - lon_before * (field - source[n, down])
+                lat_before = turned(lat_coef, 1)
+                for m in range(2):
+                    field = sources[i][m, here]
+                    flux_x = lon_coef * (sources[i][m, up] - field)
+                    flux_x = flux_x - lon_before * (field - sources[i][m, down])
                     flux_y = lat_coef * (turned(field, -1) - field)
-                    target[n, here] = (field + flux_x) + (flux_y - turned(flux_y, 1))
+                    flux_y = flux_y - lat_before * (field - turned(field, 1))
+                    targets[i][m, here] = field + (flux_x + flux_y)
 
     def root(margin):
         begin, end = STEPS + margin, STEPS + high - margin
 
-        def pair(_, carry):
-            step(field_tiles, other_tiles, begin, end)
-            step(other_tiles, field_tiles, begin, end)
+        def steps(_, carry):
+            for _ in range(STEPS // 4):
+                step(fields, others, begin, end)
+                step(others, fields, begin, end)
             return carry
 
-        lax.fori_loop(0, STEPS // 2, pair, 0)
+        lax.fori_loop(0, 2, steps, 0)
 
     root(0)
     inner = pl.ds(2 * STEPS, rows + 2 * STEPS)
     for i in range(half):
-        gains = [shallow_tiles[m * half + i] for m in range(2)]
-        total = sum(gains[m] * field_tiles[m * half + i, inner] for m in range(2))
+        gains = [shallow_tiles[i], shallow_tiles[2 * half + i]]
+        total = gains[0] * fields[i][0, inner] + gains[1] * fields[i][1, inner]
         totals[i] = total[STEPS : STEPS + rows]
-        residual = total - shallow_tiles[2 * half + i]
+        residual = total - shallow_tiles[half + i]
         for m in range(2):
-            field_tiles[m * half + i, inner] = gains[m] * residual
+            fields[i][m, inner] = gains[m] * residual
     root(STEPS)
 
 
-def tile_targets(half, field_tiles, face_tiles, shallow_tiles):
-    high = field_tiles.shape[1] - 2 * STEPS
-    targets = [field_tiles.at[n, pl.ds(STEPS, high)] for n in range(2 * half)]
-    targets += [face_tiles.at[n, pl.ds(STEPS, high)] for n in range(2 * half)]
+def tile_targets(half, tiles):
+    fields, _, face_tiles, shallow_tiles = split_tiles(half, tiles)
+    body = pl.ds(STEPS, fields[0].shape[1] - 2 * STEPS)
+    targets = [fields[i].at[0, body] for i in range(half)]
+    targets += [face_tiles.at[n, body] for n in range(2 * half)]
+    targets += [fields[i].at[1, body] for i in range(half)]
     return targets + [shallow_tiles.at[n] for n in range(3 * half)]
 
 
-def main_kernel(half, keep, got, below, above, total, mine, theirs, edge_own, *tiles):
-    field_tiles, other_tiles, face_tiles, shallow_tiles = tiles
-    deep, shallow = field_refs(half, keep, got)
+def main_kernel(
+    half,
+    keep,
+    got,
+    kept_below,
+    got_below,
+    kept_above,
+    got_above,
+    total,
+    mine,
+    theirs,
+    edge_own,
+    *tiles,
+):
     rows, lanes = keep.shape[1:]
     lane = lax.broadcasted_iota(jnp.int32, (1, lanes), 1)
-    at = 0
     edge_at = 0
-    for n, (ref, out) in enumerate(
-        zip(deep + shallow, tile_targets(half, field_tiles, face_tiles, shallow_tiles))
+    for below, ref, above, out in zip(
+        halo_refs(half, kept_below, got_below),
+        field_refs(half, keep, got),
+        halo_refs(half, kept_above, got_above),
+        tile_targets(half, tiles),
     ):
-        width = DEEP if n < len(deep) else STEPS
         offset = 0
-        for piece in (below[at : at + width], ref[...], above[at : at + width]):
+        for piece in (below[...], ref[...], above[...]):
             count = piece.shape[0]
             out[offset : offset + count] = piece
             own = jnp.where(lane < lanes - 3 * DEEP, turned(piece, 2 * DEEP), piece)
             edge_own[edge_at : edge_at + count] = own
             offset += count
             edge_at += count
-        at += width
-    diffusion(half, *tiles, total)
+    diffusion(half, tiles, total)
     own = pl.ds(STEPS + DEEP, rows)
     for i in range(half):
-        mine[i] = field_tiles[i, own]
-        theirs[i] = field_tiles[half + i, own]
+        mine[i] = tiles[i][0, own]
+        theirs[i] = tiles[i][1, own]
 
 
 def edge_kernel(
@@ -255,23 +287,20 @@
     increment,
     mine,
     theirs,
+    totals,
     *tiles,
 ):
-    field_tiles, other_tiles, face_tiles, shallow_tiles, totals = tiles
     rows, lanes = keep.shape[1:]
     lane = lax.broadcasted_iota(jnp.int32, (1, lanes), 1)
     high = rows + 2 * DEEP
     at = 0
-    for out, (width, group, place, _) in zip(
-        tile_targets(half, field_tiles, face_tiles, shallow_tiles),
-        lane_places(4 * half, 3 * half),
-    ):
+    for out, (width, group, place, _) in zip(tile_targets(half, tiles), lane_places(half)):
         count = rows + 2 * width
         here = pl.ds(group * high, count)
         sides = jnp.where(in_lanes(lane, place, width), right[here], left[here])
         out[...] = jnp.where(lane < 2 * DEEP, turned(sides, -place), edge_own[at : at + count])
         at += count
-    diffusion(half, field_tiles, other_tiles, face_tiles, shallow_tiles, totals)
+    diffusion(half, tiles, totals)
     body = pl.ds(STEPS + DEEP, rows)
 
     def joined(main, sides):
@@ -280,8 +309,8 @@
 
     for i in range(half):
         increment[i] = joined(main_total[i], totals[i]) * keep[5 * half + i]
-        mine[i] = joined(main_mine[i], field_tiles[i, body])
-        theirs[i] = joined(main_theirs[i], field_tiles[half + i, body])
+        mine[i] = joined(main_mine[i], tiles[i][0, body])
+        theirs[i] = joined(main_theirs[i], tiles[i][1, body])
 
 
 def partial_kernel(half, vertical, alpha, mine, partial, splat):
@@ -309,17 +338,25 @@
     levels, rows, lanes = lon_faces.shape
     half = levels // 2
     high = rows + 2 * DEEP
-    strip = f32(DEEP * 4 * half + STEPS * 3 * half, lanes)
     deep_groups = -(-4 * half * DEEP // lanes)
     shallow_groups = -(-3 * half * STEPS // lanes)
     column = f32(deep_groups * high + shallow_groups * (rows + 2 * STEPS), lanes)
     block = f32(half, rows, lanes)
-    tiles = [
-        pltpu.VMEM((levels, high + 2 * STEPS, lanes), jnp.float32),
-        pltpu.VMEM((levels, high + 2 * STEPS, lanes), jnp.float32),
-        pltpu.VMEM((levels, high + STEPS, lanes), jnp.float32),
-        pltpu.VMEM((3 * half, rows + 2 * STEPS, lanes), jnp.float32),
-    ]
+    tiles = [pltpu.VMEM((2, high + 2 * STEPS, lanes), jnp.float32) for _ in range(2 * half)]
+    tiles.append(pltpu.VMEM((levels, high + STEPS, lanes), jnp.float32))
+    tiles.append(pltpu.VMEM((3 * half, rows + 2 * STEPS, lanes), jnp.float32))
+
+    def strips(source, counts, name):
+        strip = f32(sum(count * width for count, width in counts), lanes)
+        first, final = pl.pallas_call(
+            functools.partial(strip_kernel, counts),
+            out_shape=(strip, strip),
+            in_specs=[VMEM],
+            out_specs=(VMEM,) * 2,
+            compiler_params=PARAMS,
+            name=name,
+        )(source)
+        return around(final, "lon", 1), around(first, "lon", -1)
 
     inputs = (
         vertical,
@@ -349,43 +386,35 @@
         name="prepare",
     )(*(pltpu.with_memory_space_constraint(value, pltpu.HBM) for value in inputs))
     got = around(give, "mem", 1)
-
-    first, final = pl.pallas_call(
-        functools.partial(strip_kernel, half),
-        out_shape=(strip, strip),
-        in_specs=[VMEM] * 2,
-        out_specs=(VMEM,) * 2,
-        compiler_params=PARAMS,
-        name="strips",
-    )(keep, got)
-    below = around(final, "lon", 1)
-    above = around(first, "lon", -1)
+    kept_below, kept_above = strips(keep, ((3 * half, DEEP), (2 * half, STEPS)), "kept_strips")
+    got_below, got_above = strips(got, ((half, DEEP), (half, STEPS)), "got_strips")
+    blocks = (keep, got, kept_below, got_below, kept_above, got_above)
     west, east = pl.pallas_call(
         functools.partial(column_kernel, half),
         out_shape=(column, column),
-        in_specs=[VMEM] * 4,
+        in_specs=[VMEM] * 6,
         out_specs=(VMEM,) * 2,
         compiler_params=PARAMS,
         name="columns",
-    )(keep, got, below, above)
+    )(*blocks)
     left = around(east, "lat", 1)
     right = around(west, "lat", -1)
     edge_own = f32(high * 4 * half + (rows + 2 * STEPS) * 3 * half, lanes)
     main = pl.pallas_call(
         functools.partial(main_kernel, half),
         out_shape=(block, block, block, edge_own),
-        in_specs=[VMEM] * 4,
+        in_specs=[VMEM] * 6,
         out_specs=(VMEM,) * 4,
         scratch_shapes=tiles,
         compiler_params=PARAMS,
         name="main",
-    )(keep, got, below, above)
+    )(*blocks)
     increment, mine, theirs = pl.pallas_call(
         functools.partial(edge_kernel, half),
         out_shape=(block, block, block),
         in_specs=[VMEM] * 7,
         out_specs=(VMEM,) * 3,
-        scratch_shapes=tiles + [pltpu.VMEM(block.shape, jnp.float32)],
+        scratch_shapes=[pltpu.VMEM(block.shape, jnp.float32)] + tiles,
         compiler_params=PARAMS,
         name="edge",
     )(keep, left, right, *main)

time: 37.7 us -> 35.2 us (0.934)
  waiting for transfers between devices: 8.56 us -> 1.88 us
  starting transfers between devices: 15.5 us -> 21.2 us
  Pallas kernels: 12.8 us -> 11.4 us
    ppermute x6 -> x8, waiting for transfers between devices: 8.56 us -> 1.88 us  [around(): return lax.ppermute(value, axis, pairs)]
    ppermute x6 -> x8, starting transfers between devices: 15.5 us -> 21.2 us  [around(): return lax.ppermute(value, axis, pairs)]
    pallas_call x1, Pallas kernels: 5.03 us -> 4.32 us  [local(): pl.pallas_call(functools.partial(edge_kernel, half), out_shape=(block, bl...]
    pallas_call x1, Pallas kernels: 4.32 us -> 3.62 us  [local(): pl.pallas_call(functools.partial(main_kernel, half), out_shape=(block, bl...]
  transfers between devices with their start and end apart: 6 -> 8, of which waited for: 4 -> 2; matrix products, arithmetic and copies ran while one was open for 0% -> 0% of each run, Pallas kernels for 13% -> 13%
where the time goes in v6:
time: 35.2 us; the launch traced here: 35.1 us
  starting transfers between devices  21.2 us (60%)
  Pallas kernels  11.4 us (32%)
  waiting for transfers between devices  1.88 us (5%)
  between operations  0.71 us (2%)
    ppermute x8, starting transfers between devices, around(): return lax.ppermute(value, axis, pairs)  21.2 us
    pallas_call x1, Pallas kernels, local(): pl.pallas_call(functools.partial(edge_kernel, half), out_shape=(block, bl...  4.32 us
    pallas_call x1, Pallas kernels, local(): pl.pallas_call(functools.partial(main_kernel, half), out_shape=(block, bl...  3.62 us
    ppermute x8, waiting for transfers between devices, around(): return lax.ppermute(value, axis, pairs)  1.88 us
    pallas_call x1, Pallas kernels, local(): pl.pallas_call(functools.partial(prepare_kernel, half), out_shape=(f32(6...  1.39 us
    pallas_call x1, Pallas kernels, local(): pl.pallas_call(functools.partial(partial_kernel, half), out_shape=(f32(le...  0.75 us
    pallas_call x1, Pallas kernels, local(): pl.pallas_call(functools.partial(gradient_kernel, half), out_shape=f32(*a...  0.73 us
  transfers between devices with their start and end apart: 8, of which 2 were waited for; matrix products, arithmetic and copies ran while one was open for 0% of the time, Pallas kernels for 13%

profile of v6, /device:TPU:1, one launch (start us, length us, event | category | flops | bytes accessed | tf_op | source)
XLA Modules:
  0.0 35.1 jit_solution(15217115305506116687)
XLA Ops:
  0.6 1.4 %prepare.1 = (f32[30,32,128]{2,1,0:T(8,128)S(1)}, f32[10,32,128]{2,1,0:T(8,128)S(1)}, f32[1,10,32,128]{3,2,1,0:T(8,128)S(1)}) custom-call(f32[10,10]{1,0:T(8,128)} %vertical.1, f32[1,10,32,128]{3,2,1,0:T(8,128)} %alpha_hbm.1, f32[1,10,32,128]{3,2,1,0:T(8,128)} %anomaly_hbm.1, f32[10,32,128]{2,1,0:T(8,128)} %lon_hbm.1, f32[10,32,128]{2,1,0:T(8,128)} %lat_hbm.1, ...), custom_call_target="tpu_custom_call" | custom-call | tf_op jit(solution)/shard_map/prepare/pallas_call | solution.py:371
  2.0 3.3 %collective-permute-start = (f32[10,32,128]{2,1,0:T(8,128)S(1)}, f32[10,32,128]{2,1,0:T(8,128)S(1)}, u32[]{:S(2)}, u32[]{:S(2)}) collective-permute-start(f32[10,32,128]{2,1,0:T(8,128)S(1)} %get-tuple-element.21), channel_id=1, source_target_pairs={{0,1},{1,0},{2,3},{3,2},{4,5},{5,4},{6,7},{7,6},{8,9},{9,8},{10,11... | collective-permute-start | bytes 491528 | tf_op jit(solution)/shard_map/ppermute | solution.py:28
  5.4 1.1 %collective-permute-start.1 = (f32[320,128]{1,0:T(8,128)S(1)}, f32[320,128]{1,0:T(8,128)S(1)}, u32[]{:S(2)}, u32[]{:S(2)}) collective-permute-start(f32[320,128]{1,0:T(8,128)S(1)} %get-tuple-element.22), channel_id=1, source_target_pairs={{0,16},{16,32},{32,48},{48,64},{64,80},{80,96},{96,112},{112,128},... | collective-permute-start | bytes 491528 | tf_op jit(solution)/shard_map/ppermute | solution.py:28
  6.5 5.4 %collective-permute-start.3 = (f32[320,128]{1,0:T(8,128)S(1)}, f32[320,128]{1,0:T(8,128)S(1)}, u32[]{:S(2)}, u32[]{:S(2)}) collective-permute-start(f32[320,128]{1,0:T(8,128)S(1)} %get-tuple-element.24), channel_id=1, source_target_pairs={{0,240},{16,0},{32,16},{48,32},{64,48},{80,64},{96,80},{112,96},{1... | collective-permute-start | bytes 491528 | tf_op jit(solution)/shard_map/ppermute | solution.py:28
  11.9 0.0 collective-permute-done.source.got
  11.9 0.1 collective-permute-start.2
  12.0 5.1 %collective-permute-start.4 = (f32[120,128]{1,0:T(8,128)S(1)}, f32[120,128]{1,0:T(8,128)S(1)}, u32[]{:S(2)}, u32[]{:S(2)}) collective-permute-start(f32[120,128]{1,0:T(8,128)S(1)} %get-tuple-element.25), channel_id=1, source_target_pairs={{0,240},{16,0},{32,16},{48,32},{64,48},{80,64},{96,80},{112,96},{1... | collective-permute-start | bytes 184328 | tf_op jit(solution)/shard_map/ppermute | solution.py:28
  17.0 0.0 collective-permute-done.1.kept_below
  17.0 0.0 collective-permute-done.3.kept_above
  17.0 1.7 %collective-permute-done.2.got_below = f32[120,128]{1,0:T(8,128)S(1)} collective-permute-done((f32[120,128]{1,0:T(8,128)S(1)}, f32[120,128]{1,0:T(8,128)S(1)}, u32[]{:S(2)}, u32[]{:S(2)}) %collective-permute-start.2) | collective-permute-done | bytes 61472 | tf_op jit(solution)/shard_map/ppermute | solution.py:28
  18.7 0.0 collective-permute-done.4.got_above
  18.7 0.5 %columns.1 = (f32[240,128]{1,0:T(8,128)S(1)}, f32[240,128]{1,0:T(8,128)S(1)}) custom-call(f32[30,32,128]{2,1,0:T(8,128)S(1)} %get-tuple-element.20.source.keep, f32[10,32,128]{2,1,0:T(8,128)S(1)} %collective-permute-done.source.got, f32[320,128]{1,0:T(8,128)S(1)} %collective-permute-done.1.kept_below, f32[120,128]{1,0:T(8,128)S(1)} %collective-permute-done.2.got_below, ...), custom_call_target="tpu_custom_call" | custom-call | tf_op jit(solution)/shard_map/columns/pallas_call | solution.py:392
  19.3 0.4 %collective-permute-start.5 = (f32[240,128]{1,0:T(8,128)S(1)}, f32[240,128]{1,0:T(8,128)S(1)}, u32[]{:S(2)}, u32[]{:S(2)}) collective-permute-start(f32[240,128]{1,0:T(8,128)S(1)} %get-tuple-element.26), channel_id=1, source_target_pairs={{0,2},{2,4},{4,6},{6,8},{8,10},{10,12},{12,14},{14,0},{1,3},{3,5},... | collective-permute-start | bytes 368648 | tf_op jit(solution)/shard_map/ppermute | solution.py:28
  19.7 3.3 %collective-permute-start.6 = (f32[240,128]{1,0:T(8,128)S(1)}, f32[240,128]{1,0:T(8,128)S(1)}, u32[]{:S(2)}, u32[]{:S(2)}) collective-permute-start(f32[240,128]{1,0:T(8,128)S(1)} %get-tuple-element.27), channel_id=1, source_target_pairs={{0,14},{2,0},{4,2},{6,4},{8,6},{10,8},{12,10},{14,12},{1,15},{3,1}... | collective-permute-start | bytes 368648 | tf_op jit(solution)/shard_map/ppermute | solution.py:28
  22.9 3.6 %main.1 = (f32[5,32,128]{2,1,0:T(8,128)S(1)}, f32[5,32,128]{2,1,0:T(8,128)S(1)}, f32[5,32,128]{2,1,0:T(8,128)S(1)}, f32[2000,128]{1,0:T(8,128)S(1)}) custom-call(f32[30,32,128]{2,1,0:T(8,128)S(1)} %get-tuple-element.20.source.keep, f32[10,32,128]{2,1,0:T(8,128)S(1)} %collective-permute-done.source.got, f32[320,128]{1,0:T(8,128)S(1)} %collective-permute-done.1.kept_below, ...), custom_call_target="tpu_custom_call" | custom-call | tf_op jit(solution)/shard_map/main/pallas_call | solution.py:403
  26.6 0.0 collective-permute-done.5.left
  26.6 0.0 collective-permute-done.6.right
  26.6 0.0 copy-start
  26.6 4.3 %edge.1 = (f32[5,32,128]{2,1,0:T(8,128)}, f32[5,32,128]{2,1,0:T(8,128)S(1)}, f32[5,32,128]{2,1,0:T(8,128)S(1)}) custom-call(f32[30,32,128]{2,1,0:T(8,128)S(1)} %get-tuple-element.20.source.keep, f32[240,128]{1,0:T(8,128)S(1)} %collective-permute-done.5.left, f32[240,128]{1,0:T(8,128)S(1)} %collective-permute-done.6.right, ...), custom_call_target="tpu_custom_call" | custom-call | tf_op jit(solution)/shard_map/edge/pallas_call | solution.py:412
  30.9 2.6 %collective-permute-start.7 = (f32[5,32,128]{2,1,0:T(8,128)S(1)}, f32[5,32,128]{2,1,0:T(8,128)S(1)}, u32[]{:S(2)}, u32[]{:S(2)}) collective-permute-start(f32[5,32,128]{2,1,0:T(8,128)S(1)} %get-tuple-element.37), channel_id=1, source_target_pairs={{0,1},{1,0},{2,3},{3,2},{4,5},{5,4},{6,7},{7,6},{8,9},{9,8},{10,11... | collective-permute-start | bytes 245768 | tf_op jit(solution)/shard_map/ppermute | solution.py:28
  33.5 0.0 copy-done
  33.5 0.8 %partial.1 = (f32[10,32,128]{2,1,0:T(8,128)S(1)}, f32[5,10,128]{2,1,0:T(8,128)S(1)}) custom-call(f32[10,10]{1,0:T(8,128)S(1)} %copy-done, f32[1,10,32,128]{3,2,1,0:T(8,128)S(1)} %get-tuple-element.33.alpha, f32[5,32,128]{2,1,0:T(8,128)S(1)} %get-tuple-element.34.mine), custom_call_target="tpu_custom_call" | custom-call | tf_op jit(solution)/shard_map/partial/pallas_call | solution.py:423
  34.2 0.2 collective-permute-done.7.got
  34.4 0.7 %gradient.1 = f32[1,10,32,128]{3,2,1,0:T(8,128)} custom-call(f32[10,32,128]{2,1,0:T(8,128)S(1)} %get-tuple-element.35.partial, f32[5,10,128]{2,1,0:T(8,128)S(1)} %get-tuple-element.36.splat, f32[5,32,128]{2,1,0:T(8,128)S(1)} %collective-permute-done.7.got), custom_call_target="tpu_custom_call" | custom-call | tf_op jit(solution)/shard_map/gradient/pallas_call | solution.py:431
  (2 shorter events, 0.0 us)
Async XLA Ops:
  2.0 9.8 %collective-permute-start = (f32[10,32,128]{2,1,0:T(8,128)S(1)}, f32[10,32,128]{2,1,0:T(8,128)S(1)}, u32[]{:S(2)}, u32[]{:S(2)}) collective-permute-start(f32[10,32,128]{2,1,0:T(8,128)S(1)} %get-tuple-element.21), channel_id=1, source_target_pairs={{0,1},{1,0},{2,3},{3,2},{4,5},{5,4},{6,7},{7,6},{8,9},{9,8},{10,11... | collective-permute-start | bytes 491528 | tf_op jit(solution)/shard_map/ppermute | solution.py:28
  5.4 11.6 %collective-permute-start.1 = (f32[320,128]{1,0:T(8,128)S(1)}, f32[320,128]{1,0:T(8,128)S(1)}, u32[]{:S(2)}, u32[]{:S(2)}) collective-permute-start(f32[320,128]{1,0:T(8,128)S(1)} %get-tuple-element.22), channel_id=1, source_target_pairs={{0,16},{16,32},{32,48},{48,64},{64,80},{80,96},{96,112},{112,128},... | collective-permute-start | bytes 491528 | tf_op jit(solution)/shard_map/ppermute | solution.py:28
  6.5 10.6 %collective-permute-start.3 = (f32[320,128]{1,0:T(8,128)S(1)}, f32[320,128]{1,0:T(8,128)S(1)}, u32[]{:S(2)}, u32[]{:S(2)}) collective-permute-start(f32[320,128]{1,0:T(8,128)S(1)} %get-tuple-element.24), channel_id=1, source_target_pairs={{0,240},{16,0},{32,16},{48,32},{64,48},{80,64},{96,80},{112,96},{1... | collective-permute-start | bytes 491528 | tf_op jit(solution)/shard_map/ppermute | solution.py:28
  11.9 6.9 %collective-permute-start.2 = (f32[120,128]{1,0:T(8,128)S(1)}, f32[120,128]{1,0:T(8,128)S(1)}, u32[]{:S(2)}, u32[]{:S(2)}) collective-permute-start(f32[120,128]{1,0:T(8,128)S(1)} %get-tuple-element.23), channel_id=1, source_target_pairs={{0,16},{16,32},{32,48},{48,64},{64,80},{80,96},{96,112},{112,128},... | collective-permute-start | bytes 184328 | tf_op jit(solution)/shard_map/ppermute | solution.py:28
  12.0 6.8 %collective-permute-start.4 = (f32[120,128]{1,0:T(8,128)S(1)}, f32[120,128]{1,0:T(8,128)S(1)}, u32[]{:S(2)}, u32[]{:S(2)}) collective-permute-start(f32[120,128]{1,0:T(8,128)S(1)} %get-tuple-element.25), channel_id=1, source_target_pairs={{0,240},{16,0},{32,16},{48,32},{64,48},{80,64},{96,80},{112,96},{1... | collective-permute-start | bytes 184328 | tf_op jit(solution)/shard_map/ppermute | solution.py:28
  19.3 7.3 %collective-permute-start.5 = (f32[240,128]{1,0:T(8,128)S(1)}, f32[240,128]{1,0:T(8,128)S(1)}, u32[]{:S(2)}, u32[]{:S(2)}) collective-permute-start(f32[240,128]{1,0:T(8,128)S(1)} %get-tuple-element.26), channel_id=1, source_target_pairs={{0,2},{2,4},{4,6},{6,8},{8,10},{10,12},{12,14},{14,0},{1,3},{3,5},... | collective-permute-start | bytes 368648 | tf_op jit(solution)/shard_map/ppermute | solution.py:28
  19.7 6.9 %collective-permute-start.6 = (f32[240,128]{1,0:T(8,128)S(1)}, f32[240,128]{1,0:T(8,128)S(1)}, u32[]{:S(2)}, u32[]{:S(2)}) collective-permute-start(f32[240,128]{1,0:T(8,128)S(1)} %get-tuple-element.27), channel_id=1, source_target_pairs={{0,14},{2,0},{4,2},{6,4},{8,6},{10,8},{12,10},{14,12},{1,15},{3,1}... | collective-permute-start | bytes 368648 | tf_op jit(solution)/shard_map/ppermute | solution.py:28
  26.6 6.9 %copy-start = (f32[10,10]{1,0:T(8,128)S(1)}, f32[10,10]{1,0:T(8,128)}, u32[]{:S(2)}) copy-start(f32[10,10]{1,0:T(8,128)} %vertical.1) | copy-start | bytes 1204
  30.9 3.5 %collective-permute-start.7 = (f32[5,32,128]{2,1,0:T(8,128)S(1)}, f32[5,32,128]{2,1,0:T(8,128)S(1)}, u32[]{:S(2)}, u32[]{:S(2)}) collective-permute-start(f32[5,32,128]{2,1,0:T(8,128)S(1)} %get-tuple-element.37), channel_id=1, source_target_pairs={{0,1},{1,0},{2,3},{3,2},{4,5},{5,4},{6,7},{7,6},{8,9},{9,8},{10,11... | collective-permute-start | bytes 245768 | tf_op jit(solution)/shard_map/ppermute | solution.py:28

commit v7 on v6

--- a/solution.py
+++ b/solution.py
@@ -29,14 +29,17 @@
 
 
 def lane_places(half):
-    places = []
-    for width, count in ((DEEP, 4 * half), (STEPS, 3 * half)):
-        for i in range(count):
-            group, place = divmod(i * width, LANES)
-            if width == STEPS:
-                group += -(-4 * half * DEEP // LANES)
-            places.append((width, group, place, (place + 2 * DEEP - width) % LANES))
-    return places
+    per = LANES // DEEP
+    late = -(-3 * half // per)
+    slots = [(DEEP, i // per, i % per * DEEP) for i in range(3 * half)]
+    slots += [(DEEP, late, i * DEEP) for i in range(half)]
+    slots += [(STEPS, late + 1, i * STEPS) for i in range(2 * half)]
+    slots += [(STEPS, late, half * DEEP + i * STEPS) for i in range(half)]
+    return [(width, n, at, (at + 2 * DEEP - width) % LANES) for width, n, at in slots]
+
+
+def is_late(half, n):
+    return 3 * half <= n < 4 * half or n >= 6 * half
 
 
 def turned(value, shift):
@@ -121,9 +124,9 @@
     refs = []
     ends = {False: 0, True: 0}
     for n, width in enumerate(widths(half)):
-        late = 3 * half <= n < 4 * half or n >= 6 * half
+        late = is_late(half, n)
         pack = gotten if late else kept
-        refs.append(pack.at[pl.ds(ends[late], width)])
+        refs.append(None if pack is None else pack.at[pl.ds(ends[late], width)])
         ends[late] += width
     return refs
 
@@ -146,27 +149,63 @@
     return jnp.logical_and(lane >= place, lane < place + width)
 
 
-def column_kernel(half, keep, got, kept_below, got_below, kept_above, got_above, west, east):
-    lanes = keep.shape[2]
+def packed(half, lane, fields):
+    packs = {}
+    for n, rows in fields.items():
+        width, group, place, opposite = lane_places(half)[n]
+        heads, tails = packs.get(group, (jnp.zeros_like(rows), jnp.zeros_like(rows)))
+        top = DEEP - width if rows.shape[0] < heads.shape[0] else 0
+        if top:
+            margin = jnp.zeros((top, rows.shape[1]), rows.dtype)
+            rows = jnp.concatenate([margin, rows] if fields.low else [rows, margin], axis=0)
+        heads = jnp.where(in_lanes(lane, place, width), turned(rows, place), heads)
+        tails = jnp.where(in_lanes(lane, opposite, width), turned(rows, place + 2 * DEEP), tails)
+        packs[group] = heads, tails
+    return packs
+
+
+class Side(dict):
+    def __init__(self, items, low):
+        super().__init__(items)
+        self.low = low
+
+
+def own_column_kernel(half, keep, got, west, east):
+    lane = lax.broadcasted_iota(jnp.int32, (1, keep.shape[2]), 1)
+    fields = {n: ref[...] for n, ref in enumerate(field_refs(half, keep, got))}
+    for group, (heads, tails) in packed(half, lane, fields).items():
+        west[group], east[group] = heads, tails
+
+
+def halo_columns(half, lane, kept, gotten, low):
+    refs = halo_refs(half, kept, gotten)
+    chosen = {n: ref[...] for n, ref in enumerate(refs) if ref is not None}
+    return packed(half, lane, Side(chosen, low))
+
+
+def early_column_kernel(half, below, above, west, east):
+    lane = lax.broadcasted_iota(jnp.int32, (1, below.shape[1]), 1)
+    for side, ref in enumerate((below, above)):
+        for group, (heads, tails) in halo_columns(half, lane, ref, None, side == 0).items():
+            count = heads.shape[0]
+            west[group, side, :count], east[group, side, :count] = heads, tails
+
+
+def column_kernel(half, own_west, own_east, early_west, early_east, below, above, west, east):
+    rows, lanes = own_west.shape[1:]
     lane = lax.broadcasted_iota(jnp.int32, (1, lanes), 1)
-    packs = {}
-    for below, ref, above, (width, group, place, opposite) in zip(
-        halo_refs(half, kept_below, got_below),
-        field_refs(half, keep, got),
-        halo_refs(half, kept_above, got_above),
-        lane_places(half),
-    ):
-        for n, piece in enumerate((below[...], ref[...], above[...])):
-            heads, tails = packs.get((group, n), (0.0, 0.0))
-            heads = jnp.where(in_lanes(lane, place, width), turned(piece, place), heads)
-            tails = jnp.where(in_lanes(lane, opposite, width), turned(piece, place + 2 * DEEP), tails)
-            packs[group, n] = heads, tails
-    at = 0
-    for heads, tails in packs.values():
-        count = heads.shape[0]
-        west[at : at + count] = heads
-        east[at : at + count] = tails
-        at += count
+    late = [halo_columns(half, lane, None, ref, n == 0) for n, ref in enumerate((below, above))]
+    groups = own_west.shape[0]
+    for n, (own, early, out) in enumerate(((own_west, early_west, west), (own_east, early_east, east))):
+        at = 0
+        for group in range(groups):
+            width = STEPS if group == groups - 1 else DEEP
+            for side in range(2):
+                place = at + side * (width + rows)
+                ends = late[side][group][n] if group in late[side] else early[group, side, :width]
+                out[place : place + width] = ends
+            out[at + width : at + width + rows] = own[group]
+            at += rows + 2 * width
 
 
 def split_tiles(half, tiles):
@@ -185,6 +224,9 @@
             ref[m, :STEPS] = edge
             ref[m, STEPS + high :] = edge
 
+    for i in range(half):
+        face_tiles[2 * half + i, STEPS:] = turned(face_tiles[half + i, STEPS:], 1)
+
     zero = lax.axis_index("mem") // 2
 
     def step(sources, targets, begin, end):
@@ -196,7 +238,7 @@
                 lon_coef = face_tiles[i, here]
                 lon_before = face_tiles[i, down]
                 lat_coef = face_tiles[half + i, here]
-                lat_before = turned(lat_coef, 1)
+                lat_before = face_tiles[2 * half + i, here]
                 for m in range(2):
                     field = sources[i][m, here]
                     flux_x = lon_coef * (sources[i][m, up] - field)
@@ -293,10 +335,12 @@
     rows, lanes = keep.shape[1:]
     lane = lax.broadcasted_iota(jnp.int32, (1, lanes), 1)
     high = rows + 2 * DEEP
+    groups = 1 + max(group for _, group, _, _ in lane_places(half))
     at = 0
     for out, (width, group, place, _) in zip(tile_targets(half, tiles), lane_places(half)):
         count = rows + 2 * width
-        here = pl.ds(group * high, count)
+        inset = DEEP - width if group < groups - 1 else 0
+        here = pl.ds(group * high + inset, count)
         sides = jnp.where(in_lanes(lane, place, width), right[here], left[here])
         out[...] = jnp.where(lane < 2 * DEEP, turned(sides, -place), edge_own[at : at + count])
         at += count
@@ -338,12 +382,11 @@
     levels, rows, lanes = lon_faces.shape
     half = levels // 2
     high = rows + 2 * DEEP
-    deep_groups = -(-4 * half * DEEP // lanes)
-    shallow_groups = -(-3 * half * STEPS // lanes)
-    column = f32(deep_groups * high + shallow_groups * (rows + 2 * STEPS), lanes)
+    groups = 1 + max(group for _, group, _, _ in lane_places(half))
+    column = f32((groups - 1) * high + rows + 2 * STEPS, lanes)
     block = f32(half, rows, lanes)
     tiles = [pltpu.VMEM((2, high + 2 * STEPS, lanes), jnp.float32) for _ in range(2 * half)]
-    tiles.append(pltpu.VMEM((levels, high + STEPS, lanes), jnp.float32))
+    tiles.append(pltpu.VMEM((3 * half, high + STEPS, lanes), jnp.float32))
     tiles.append(pltpu.VMEM((3 * half, rows + 2 * STEPS, lanes), jnp.float32))
 
     def strips(source, counts, name):
@@ -389,6 +432,22 @@
     kept_below, kept_above = strips(keep, ((3 * half, DEEP), (2 * half, STEPS)), "kept_strips")
     got_below, got_above = strips(got, ((half, DEEP), (half, STEPS)), "got_strips")
     blocks = (keep, got, kept_below, got_below, kept_above, got_above)
+    own_columns = pl.pallas_call(
+        functools.partial(own_column_kernel, half),
+        out_shape=(f32(groups, rows, lanes),) * 2,
+        in_specs=[VMEM] * 2,
+        out_specs=(VMEM,) * 2,
+        compiler_params=PARAMS,
+        name="own_columns",
+    )(keep, got)
+    early_columns = pl.pallas_call(
+        functools.partial(early_column_kernel, half),
+        out_shape=(f32(groups, 2, DEEP, lanes),) * 2,
+        in_specs=[VMEM] * 2,
+        out_specs=(VMEM,) * 2,
+        compiler_params=PARAMS,
+        name="early_columns",
+    )(kept_below, kept_above)
     west, east = pl.pallas_call(
         functools.partial(column_kernel, half),
         out_shape=(column, column),
@@ -396,7 +455,7 @@
         out_specs=(VMEM,) * 2,
         compiler_params=PARAMS,
         name="columns",
-    )(*blocks)
+    )(*own_columns, *early_columns, got_below, got_above)
     left = around(east, "lat", 1)
     right = around(west, "lat", -1)
     edge_own = f32(high * 4 * half + (rows + 2 * STEPS) * 3 * half, lanes)

time: 35.2 us -> 33.9 us (0.963)
  Pallas kernels: 11.4 us -> 10.4 us
  waiting for transfers between devices: 1.88 us -> 1.31 us
    pallas_call x1, Pallas kernels: 3.62 us -> 3.05 us  [local(): pl.pallas_call(functools.partial(main_kernel, half), out_shape=(block, bl...]
    ppermute x8, waiting for transfers between devices: 1.88 us -> 1.31 us  [around(): return lax.ppermute(value, axis, pairs)]
    pallas_call x1, Pallas kernels: 4.32 us -> 3.76 us  [local(): pl.pallas_call(functools.partial(edge_kernel, half), out_shape=(block, bl...]
    pallas_call x0 -> x2, Pallas kernels: none -> 0.54 us  [the longest x1 0.33 us: local(): pl.pallas_call(functools.partial(own_column_kernel, half), out_shape=(f32...]
    pallas_call x1, Pallas kernels: 0.55 us -> 0.13 us  [local(): pl.pallas_call(functools.partial(column_kernel, half), out_shape=(column,...]
where the time goes in v7:
time: 33.9 us; the launch traced here: 33.8 us
  starting transfers between devices  21.3 us (63%)
  Pallas kernels  10.4 us (31%)
  waiting for transfers between devices  1.31 us (4%)
  between operations  0.74 us (2%)
    ppermute x8, starting transfers between devices, around(): return lax.ppermute(value, axis, pairs)  21.3 us
    pallas_call x1, Pallas kernels, local(): pl.pallas_call(functools.partial(edge_kernel, half), out_shape=(block, bl...  3.76 us
    pallas_call x1, Pallas kernels, local(): pl.pallas_call(functools.partial(main_kernel, half), out_shape=(block, bl...  3.05 us
    pallas_call x1, Pallas kernels, local(): pl.pallas_call(functools.partial(prepare_kernel, half), out_shape=(f32(6...  1.39 us
    ppermute x8, waiting for transfers between devices, around(): return lax.ppermute(value, axis, pairs)  1.31 us
    pallas_call x1, Pallas kernels, local(): pl.pallas_call(functools.partial(partial_kernel, half), out_shape=(f32(le...  0.75 us
    pallas_call x1, Pallas kernels, local(): pl.pallas_call(functools.partial(gradient_kernel, half), out_shape=f32(*a...  0.73 us
  transfers between devices with their start and end apart: 8, of which 2 were waited for; matrix products, arithmetic and copies ran while one was open for 0% of the time, Pallas kernels for 13%

profile of v7, /device:TPU:1, one launch (start us, length us, event | category | flops | bytes accessed | tf_op | source)
XLA Modules:
  0.0 33.8 jit_solution(16041416471499784951)
XLA Ops:
  0.6 1.4 %prepare.1 = (f32[30,32,128]{2,1,0:T(8,128)S(1)}, f32[10,32,128]{2,1,0:T(8,128)S(1)}, f32[1,10,32,128]{3,2,1,0:T(8,128)S(1)}) custom-call(f32[10,10]{1,0:T(8,128)} %vertical.1, f32[1,10,32,128]{3,2,1,0:T(8,128)} %alpha_hbm.1, f32[1,10,32,128]{3,2,1,0:T(8,128)} %anomaly_hbm.1, f32[10,32,128]{2,1,0:T(8,128)} %lon_hbm.1, f32[10,32,128]{2,1,0:T(8,128)} %lat_hbm.1, ...), custom_call_target="tpu_custom_call" | custom-call | tf_op jit(solution)/shard_map/prepare/pallas_call | solution.py:414
  2.0 3.3 %collective-permute-start = (f32[10,32,128]{2,1,0:T(8,128)S(1)}, f32[10,32,128]{2,1,0:T(8,128)S(1)}, u32[]{:S(2)}, u32[]{:S(2)}) collective-permute-start(f32[10,32,128]{2,1,0:T(8,128)S(1)} %get-tuple-element.25), channel_id=1, source_target_pairs={{0,1},{1,0},{2,3},{3,2},{4,5},{5,4},{6,7},{7,6},{8,9},{9,8},{10,11... | collective-permute-start | bytes 491528 | tf_op jit(solution)/shard_map/ppermute | solution.py:28
  5.4 1.1 %collective-permute-start.1 = (f32[320,128]{1,0:T(8,128)S(1)}, f32[320,128]{1,0:T(8,128)S(1)}, u32[]{:S(2)}, u32[]{:S(2)}) collective-permute-start(f32[320,128]{1,0:T(8,128)S(1)} %get-tuple-element.28), channel_id=1, source_target_pairs={{0,16},{16,32},{32,48},{48,64},{64,80},{80,96},{96,112},{112,128},... | collective-permute-start | bytes 491528 | tf_op jit(solution)/shard_map/ppermute | solution.py:28
  6.5 5.4 %collective-permute-start.2 = (f32[320,128]{1,0:T(8,128)S(1)}, f32[320,128]{1,0:T(8,128)S(1)}, u32[]{:S(2)}, u32[]{:S(2)}) collective-permute-start(f32[320,128]{1,0:T(8,128)S(1)} %get-tuple-element.29), channel_id=1, source_target_pairs={{0,240},{16,0},{32,16},{48,32},{64,48},{80,64},{96,80},{112,96},{1... | collective-permute-start | bytes 491528 | tf_op jit(solution)/shard_map/ppermute | solution.py:28
  11.9 0.0 collective-permute-done.got.source
  11.9 0.1 collective-permute-start.3
  12.0 5.1 %collective-permute-start.4 = (f32[120,128]{1,0:T(8,128)S(1)}, f32[120,128]{1,0:T(8,128)S(1)}, u32[]{:S(2)}, u32[]{:S(2)}) collective-permute-start(f32[120,128]{1,0:T(8,128)S(1)} %get-tuple-element.33), channel_id=1, source_target_pairs={{0,240},{16,0},{32,16},{48,32},{64,48},{80,64},{96,80},{112,96},{1... | collective-permute-start | bytes 184328 | tf_op jit(solution)/shard_map/ppermute | solution.py:28
  17.0 0.3 own_columns.1
  17.4 0.0 collective-permute-done.1.below.kept_below
  17.4 0.0 collective-permute-done.2.above.kept_above
  17.4 0.2 early_columns.1
  17.6 1.1 %collective-permute-done.3.below.got_below = f32[120,128]{1,0:T(8,128)S(1)} collective-permute-done((f32[120,128]{1,0:T(8,128)S(1)}, f32[120,128]{1,0:T(8,128)S(1)}, u32[]{:S(2)}, u32[]{:S(2)}) %collective-permute-start.3) | collective-permute-done | bytes 61472 | tf_op jit(solution)/shard_map/ppermute | solution.py:28
  18.7 0.0 collective-permute-done.4.above.got_above
  18.7 0.1 columns.1
  18.9 0.4 %collective-permute-start.5 = (f32[240,128]{1,0:T(8,128)S(1)}, f32[240,128]{1,0:T(8,128)S(1)}, u32[]{:S(2)}, u32[]{:S(2)}) collective-permute-start(f32[240,128]{1,0:T(8,128)S(1)} %get-tuple-element.34), channel_id=1, source_target_pairs={{0,2},{2,4},{4,6},{6,8},{8,10},{10,12},{12,14},{14,0},{1,3},{3,5},... | collective-permute-start | bytes 368648 | tf_op jit(solution)/shard_map/ppermute | solution.py:28
  19.3 3.3 %collective-permute-start.6 = (f32[240,128]{1,0:T(8,128)S(1)}, f32[240,128]{1,0:T(8,128)S(1)}, u32[]{:S(2)}, u32[]{:S(2)}) collective-permute-start(f32[240,128]{1,0:T(8,128)S(1)} %get-tuple-element.35), channel_id=1, source_target_pairs={{0,14},{2,0},{4,2},{6,4},{8,6},{10,8},{12,10},{14,12},{1,15},{3,1}... | collective-permute-start | bytes 368648 | tf_op jit(solution)/shard_map/ppermute | solution.py:28
  22.5 3.0 %main.1 = (f32[5,32,128]{2,1,0:T(8,128)S(1)}, f32[5,32,128]{2,1,0:T(8,128)S(1)}, f32[5,32,128]{2,1,0:T(8,128)S(1)}, f32[2000,128]{1,0:T(8,128)S(1)}) custom-call(f32[30,32,128]{2,1,0:T(8,128)S(1)} %get-tuple-element.24.keep.source, f32[10,32,128]{2,1,0:T(8,128)S(1)} %collective-permute-done.got.source, ...), custom_call_target="tpu_custom_call" | custom-call | tf_op jit(solution)/shard_map/main/pallas_call | solution.py:462
  25.6 0.0 collective-permute-done.5.left
  25.6 0.0 collective-permute-done.6.right
  25.6 0.0 copy-start
  25.6 3.8 %edge.1 = (f32[5,32,128]{2,1,0:T(8,128)}, f32[5,32,128]{2,1,0:T(8,128)S(1)}, f32[5,32,128]{2,1,0:T(8,128)S(1)}) custom-call(f32[30,32,128]{2,1,0:T(8,128)S(1)} %get-tuple-element.24.keep.source, f32[240,128]{1,0:T(8,128)S(1)} %collective-permute-done.5.left, f32[240,128]{1,0:T(8,128)S(1)} %collective-permute-done.6.right, ...), custom_call_target="tpu_custom_call" | custom-call | tf_op jit(solution)/shard_map/edge/pallas_call | solution.py:471
  29.4 2.7 %collective-permute-start.7 = (f32[5,32,128]{2,1,0:T(8,128)S(1)}, f32[5,32,128]{2,1,0:T(8,128)S(1)}, u32[]{:S(2)}, u32[]{:S(2)}) collective-permute-start(f32[5,32,128]{2,1,0:T(8,128)S(1)} %get-tuple-element.45), channel_id=1, source_target_pairs={{0,1},{1,0},{2,3},{3,2},{4,5},{5,4},{6,7},{7,6},{8,9},{9,8},{10,11... | collective-permute-start | bytes 245768 | tf_op jit(solution)/shard_map/ppermute | solution.py:28
  32.1 0.0 copy-done
  32.1 0.8 %partial.1 = (f32[10,32,128]{2,1,0:T(8,128)S(1)}, f32[5,10,128]{2,1,0:T(8,128)S(1)}) custom-call(f32[10,10]{1,0:T(8,128)S(1)} %copy-done, f32[1,10,32,128]{3,2,1,0:T(8,128)S(1)} %get-tuple-element.41.alpha, f32[5,32,128]{2,1,0:T(8,128)S(1)} %get-tuple-element.42.mine), custom_call_target="tpu_custom_call" | custom-call | tf_op jit(solution)/shard_map/partial/pallas_call | solution.py:482
  32.9 0.2 collective-permute-done.7.got
  33.0 0.7 %gradient.1 = f32[1,10,32,128]{3,2,1,0:T(8,128)} custom-call(f32[10,32,128]{2,1,0:T(8,128)S(1)} %get-tuple-element.43.partial, f32[5,10,128]{2,1,0:T(8,128)S(1)} %get-tuple-element.44.splat, f32[5,32,128]{2,1,0:T(8,128)S(1)} %collective-permute-done.7.got), custom_call_target="tpu_custom_call" | custom-call | tf_op jit(solution)/shard_map/gradient/pallas_call | solution.py:490
  (2 shorter events, 0.0 us)
Async XLA Ops:
  2.0 9.8 %collective-permute-start = (f32[10,32,128]{2,1,0:T(8,128)S(1)}, f32[10,32,128]{2,1,0:T(8,128)S(1)}, u32[]{:S(2)}, u32[]{:S(2)}) collective-permute-start(f32[10,32,128]{2,1,0:T(8,128)S(1)} %get-tuple-element.25), channel_id=1, source_target_pairs={{0,1},{1,0},{2,3},{3,2},{4,5},{5,4},{6,7},{7,6},{8,9},{9,8},{10,11... | collective-permute-start | bytes 491528 | tf_op jit(solution)/shard_map/ppermute | solution.py:28
  5.4 12.0 %collective-permute-start.1 = (f32[320,128]{1,0:T(8,128)S(1)}, f32[320,128]{1,0:T(8,128)S(1)}, u32[]{:S(2)}, u32[]{:S(2)}) collective-permute-start(f32[320,128]{1,0:T(8,128)S(1)} %get-tuple-element.28), channel_id=1, source_target_pairs={{0,16},{16,32},{32,48},{48,64},{64,80},{80,96},{96,112},{112,128},... | collective-permute-start | bytes 491528 | tf_op jit(solution)/shard_map/ppermute | solution.py:28
  6.5 10.9 %collective-permute-start.2 = (f32[320,128]{1,0:T(8,128)S(1)}, f32[320,128]{1,0:T(8,128)S(1)}, u32[]{:S(2)}, u32[]{:S(2)}) collective-permute-start(f32[320,128]{1,0:T(8,128)S(1)} %get-tuple-element.29), channel_id=1, source_target_pairs={{0,240},{16,0},{32,16},{48,32},{64,48},{80,64},{96,80},{112,96},{1... | collective-permute-start | bytes 491528 | tf_op jit(solution)/shard_map/ppermute | solution.py:28
  11.9 6.9 %collective-permute-start.3 = (f32[120,128]{1,0:T(8,128)S(1)}, f32[120,128]{1,0:T(8,128)S(1)}, u32[]{:S(2)}, u32[]{:S(2)}) collective-permute-start(f32[120,128]{1,0:T(8,128)S(1)} %get-tuple-element.32), channel_id=1, source_target_pairs={{0,16},{16,32},{32,48},{48,64},{64,80},{80,96},{96,112},{112,128},... | collective-permute-start | bytes 184328 | tf_op jit(solution)/shard_map/ppermute | solution.py:28
  12.0 6.8 %collective-permute-start.4 = (f32[120,128]{1,0:T(8,128)S(1)}, f32[120,128]{1,0:T(8,128)S(1)}, u32[]{:S(2)}, u32[]{:S(2)}) collective-permute-start(f32[120,128]{1,0:T(8,128)S(1)} %get-tuple-element.33), channel_id=1, source_target_pairs={{0,240},{16,0},{32,16},{48,32},{64,48},{80,64},{96,80},{112,96},{1... | collective-permute-start | bytes 184328 | tf_op jit(solution)/shard_map/ppermute | solution.py:28
  18.9 6.7 %collective-permute-start.5 = (f32[240,128]{1,0:T(8,128)S(1)}, f32[240,128]{1,0:T(8,128)S(1)}, u32[]{:S(2)}, u32[]{:S(2)}) collective-permute-start(f32[240,128]{1,0:T(8,128)S(1)} %get-tuple-element.34), channel_id=1, source_target_pairs={{0,2},{2,4},{4,6},{6,8},{8,10},{10,12},{12,14},{14,0},{1,3},{3,5},... | collective-permute-start | bytes 368648 | tf_op jit(solution)/shard_map/ppermute | solution.py:28
  19.3 6.3 %collective-permute-start.6 = (f32[240,128]{1,0:T(8,128)S(1)}, f32[240,128]{1,0:T(8,128)S(1)}, u32[]{:S(2)}, u32[]{:S(2)}) collective-permute-start(f32[240,128]{1,0:T(8,128)S(1)} %get-tuple-element.35), channel_id=1, source_target_pairs={{0,14},{2,0},{4,2},{6,4},{8,6},{10,8},{12,10},{14,12},{1,15},{3,1}... | collective-permute-start | bytes 368648 | tf_op jit(solution)/shard_map/ppermute | solution.py:28
  25.6 6.5 %copy-start = (f32[10,10]{1,0:T(8,128)S(1)}, f32[10,10]{1,0:T(8,128)}, u32[]{:S(2)}) copy-start(f32[10,10]{1,0:T(8,128)} %vertical.1) | copy-start | bytes 1204
  29.4 3.6 %collective-permute-start.7 = (f32[5,32,128]{2,1,0:T(8,128)S(1)}, f32[5,32,128]{2,1,0:T(8,128)S(1)}, u32[]{:S(2)}, u32[]{:S(2)}) collective-permute-start(f32[5,32,128]{2,1,0:T(8,128)S(1)} %get-tuple-element.45), channel_id=1, source_target_pairs={{0,1},{1,0},{2,3},{3,2},{4,5},{5,4},{6,7},{7,6},{8,9},{9,8},{10,11... | collective-permute-start | bytes 245768 | tf_op jit(solution)/shard_map/ppermute | solution.py:28

commit v8 on v7

--- a/solution.py
+++ b/solution.py
@@ -29,13 +29,19 @@
 
 
 def lane_places(half):
-    per = LANES // DEEP
-    late = -(-3 * half // per)
-    slots = [(DEEP, i // per, i % per * DEEP) for i in range(3 * half)]
-    slots += [(DEEP, late, i * DEEP) for i in range(half)]
-    slots += [(STEPS, late + 1, i * STEPS) for i in range(2 * half)]
-    slots += [(STEPS, late, half * DEEP + i * STEPS) for i in range(half)]
-    return [(width, n, at, (at + 2 * DEEP - width) % LANES) for width, n, at in slots]
+    halfway = LANES // 2
+    places = [None] * (7 * half)
+    pairs = [(i, 3 * half + i) for i in range(half)] + [(half + i, 2 * half + i) for i in range(half)]
+    for k, pair in enumerate(pairs):
+        group, at = divmod(k * DEEP, halfway)
+        for side, n in enumerate(pair):
+            places[n] = (DEEP, group, at + side * halfway)
+    last = -(-len(pairs) * DEEP // halfway)
+    for i in range(half):
+        places[4 * half + i] = (STEPS, last, i * STEPS)
+        places[6 * half + i] = (STEPS, last, i * STEPS + halfway)
+        places[5 * half + i] = (STEPS, last, (half + i // 2) * STEPS + i % 2 * halfway)
+    return places
 
 
 def is_late(half, n):
@@ -144,68 +150,58 @@
 
 
 def in_lanes(lane, place, width):
-    if place + width > LANES:
-        return jnp.logical_or(lane >= place, lane < place + width - LANES)
     return jnp.logical_and(lane >= place, lane < place + width)
 
 
-def packed(half, lane, fields):
-    packs = {}
+def packed(half, lane, fields, packs):
     for n, rows in fields.items():
-        width, group, place, opposite = lane_places(half)[n]
+        width, group, place = lane_places(half)[n]
         heads, tails = packs.get(group, (jnp.zeros_like(rows), jnp.zeros_like(rows)))
-        top = DEEP - width if rows.shape[0] < heads.shape[0] else 0
-        if top:
-            margin = jnp.zeros((top, rows.shape[1]), rows.dtype)
-            rows = jnp.concatenate([margin, rows] if fields.low else [rows, margin], axis=0)
-        heads = jnp.where(in_lanes(lane, place, width), turned(rows, place), heads)
-        tails = jnp.where(in_lanes(lane, opposite, width), turned(rows, place + 2 * DEEP), tails)
+        inside = in_lanes(lane, place, width)
+        heads = jnp.where(inside, turned(rows, place), heads)
+        tails = jnp.where(inside, turned(rows, place + width), tails)
         packs[group] = heads, tails
     return packs
-
-
-class Side(dict):
-    def __init__(self, items, low):
-        super().__init__(items)
-        self.low = low
 
 
 def own_column_kernel(half, keep, got, west, east):
     lane = lax.broadcasted_iota(jnp.int32, (1, keep.shape[2]), 1)
     fields = {n: ref[...] for n, ref in enumerate(field_refs(half, keep, got))}
-    for group, (heads, tails) in packed(half, lane, fields).items():
+    for group, (heads, tails) in packed(half, lane, fields, {}).items():
         west[group], east[group] = heads, tails
 
 
-def halo_columns(half, lane, kept, gotten, low):
+def halo_columns(half, lane, kept, gotten, packs):
     refs = halo_refs(half, kept, gotten)
-    chosen = {n: ref[...] for n, ref in enumerate(refs) if ref is not None}
-    return packed(half, lane, Side(chosen, low))
+    fields = {n: ref[...] for n, ref in enumerate(refs) if ref is not None}
+    return packed(half, lane, fields, packs)
 
 
 def early_column_kernel(half, below, above, west, east):
     lane = lax.broadcasted_iota(jnp.int32, (1, below.shape[1]), 1)
     for side, ref in enumerate((below, above)):
-        for group, (heads, tails) in halo_columns(half, lane, ref, None, side == 0).items():
+        for group, (heads, tails) in halo_columns(half, lane, ref, None, {}).items():
             count = heads.shape[0]
             west[group, side, :count], east[group, side, :count] = heads, tails
 
 
 def column_kernel(half, own_west, own_east, early_west, early_east, below, above, west, east):
-    rows, lanes = own_west.shape[1:]
+    groups, rows, lanes = own_west.shape
     lane = lax.broadcasted_iota(jnp.int32, (1, lanes), 1)
-    late = [halo_columns(half, lane, None, ref, n == 0) for n, ref in enumerate((below, above))]
-    groups = own_west.shape[0]
-    for n, (own, early, out) in enumerate(((own_west, early_west, west), (own_east, early_east, east))):
+    ends = []
+    for side, ref in enumerate((below, above)):
+        packs = {}
+        for group in range(groups):
+            here = pl.ds(0, STEPS if group == groups - 1 else DEEP)
+            packs[group] = early_west[group, side, here], early_east[group, side, here]
+        ends.append(halo_columns(half, lane, None, ref, packs))
+    for n, (own, out) in enumerate(((own_west, west), (own_east, east))):
         at = 0
         for group in range(groups):
-            width = STEPS if group == groups - 1 else DEEP
-            for side in range(2):
-                place = at + side * (width + rows)
-                ends = late[side][group][n] if group in late[side] else early[group, side, :width]
-                out[place : place + width] = ends
-            out[at + width : at + width + rows] = own[group]
-            at += rows + 2 * width
+            for piece in (ends[0][group][n], own[group], ends[1][group][n]):
+                count = piece.shape[0]
+                out[at : at + count] = piece
+                at += count
 
 
 def split_tiles(half, tiles):
@@ -214,13 +210,14 @@
 
 def diffusion(half, tiles, totals):
     fields, others, face_tiles, shallow_tiles = split_tiles(half, tiles)
+    copies = fields[0].shape[0]
     high = fields[0].shape[1] - 2 * STEPS
     rows = high - 2 * DEEP
     edge = jnp.zeros((STEPS, fields[0].shape[2]), jnp.float32)
     for n in range(2 * half):
         face_tiles[n, :STEPS] = edge
     for ref in (*fields, *others):
-        for m in range(2):
+        for m in range(copies):
             ref[m, :STEPS] = edge
             ref[m, STEPS + high :] = edge
 
@@ -239,7 +236,7 @@
                 lon_before = face_tiles[i, down]
                 lat_coef = face_tiles[half + i, here]
                 lat_before = face_tiles[2 * half + i, here]
-                for m in range(2):
+                for m in range(copies):
                     field = sources[i][m, here]
                     flux_x = lon_coef * (sources[i][m, up] - field)
                     flux_x = flux_x - lon_before * (field - sources[i][m, down])
@@ -261,11 +258,12 @@
     root(0)
     inner = pl.ds(2 * STEPS, rows + 2 * STEPS)
     for i in range(half):
-        gains = [shallow_tiles[i], shallow_tiles[2 * half + i]]
-        total = gains[0] * fields[i][0, inner] + gains[1] * fields[i][1, inner]
+        gains = [shallow_tiles[2 * m * half + i] for m in range(copies)]
+        parts = [gains[m] * fields[i][m, inner] for m in range(copies)]
+        total = parts[0] + (parts[1] if copies == 2 else turned(parts[0], LANES // 2))
         totals[i] = total[STEPS : STEPS + rows]
         residual = total - shallow_tiles[half + i]
-        for m in range(2):
+        for m in range(copies):
             fields[i][m, inner] = gains[m] * residual
     root(STEPS)
 
@@ -275,8 +273,9 @@
     body = pl.ds(STEPS, fields[0].shape[1] - 2 * STEPS)
     targets = [fields[i].at[0, body] for i in range(half)]
     targets += [face_tiles.at[n, body] for n in range(2 * half)]
-    targets += [fields[i].at[1, body] for i in range(half)]
-    return targets + [shallow_tiles.at[n] for n in range(3 * half)]
+    if fields[0].shape[0] == 2:
+        targets += [fields[i].at[1, body] for i in range(half)]
+    return targets + [shallow_tiles.at[n] for n in range(shallow_tiles.shape[0])]
 
 
 def main_kernel(
@@ -290,26 +289,36 @@
     total,
     mine,
     theirs,
-    edge_own,
+    left_own,
+    right_own,
     *tiles,
 ):
     rows, lanes = keep.shape[1:]
     lane = lax.broadcasted_iota(jnp.int32, (1, lanes), 1)
-    edge_at = 0
+    targets = tile_targets(half, tiles)
     for below, ref, above, out in zip(
         halo_refs(half, kept_below, got_below),
         field_refs(half, keep, got),
         halo_refs(half, kept_above, got_above),
-        tile_targets(half, tiles),
+        targets,
     ):
         offset = 0
         for piece in (below[...], ref[...], above[...]):
             count = piece.shape[0]
             out[offset : offset + count] = piece
-            own = jnp.where(lane < lanes - 3 * DEEP, turned(piece, 2 * DEEP), piece)
-            edge_own[edge_at : edge_at + count] = own
             offset += count
-            edge_at += count
+    pairs = [(n, 3 * half + n if n < half else n) for n in range(3 * half)]
+    pairs += [(4 * half + i, 6 * half + i) for i in range(half)]
+    pairs += [(5 * half + i, 5 * half + i) for i in range(half)]
+    halfway = lanes // 2
+    at = 0
+    for one, two in pairs:
+        a, b = targets[one][...], targets[two][...]
+        count = a.shape[0]
+        here = pl.ds(at, count)
+        left_own[here] = jnp.where(lane < halfway, turned(a, DEEP), turned(b, DEEP + halfway))
+        right_own[here] = jnp.where(lane < halfway, turned(a, halfway - DEEP), turned(b, -DEEP))
+        at += count
     diffusion(half, tiles, total)
     own = pl.ds(STEPS + DEEP, rows)
     for i in range(half):
@@ -318,43 +327,55 @@
 
 
 def edge_kernel(
-    half,
-    keep,
-    left,
-    right,
-    main_total,
-    main_mine,
-    main_theirs,
-    edge_own,
-    increment,
-    mine,
-    theirs,
-    totals,
-    *tiles,
+    half, after, pack, own, total_in, mine_in, theirs_in, total_out, mine, theirs, totals, *tiles
 ):
-    rows, lanes = keep.shape[1:]
+    rows, lanes = mine.shape[1:]
+    high = rows + 2 * DEEP
+    halfway = lanes // 2
     lane = lax.broadcasted_iota(jnp.int32, (1, lanes), 1)
-    high = rows + 2 * DEEP
-    groups = 1 + max(group for _, group, _, _ in lane_places(half))
+    begin = halfway - DEEP if after else 0
+    inside = jnp.logical_or(
+        in_lanes(lane, begin, DEEP), in_lanes(lane, begin + halfway, DEEP)
+    )
+    low = lane < halfway
+    places = lane_places(half)
+    targets = tile_targets(half, tiles)
+
+    def sides(n):
+        width, group, place = places[n]
+        shift = begin + (0 if after else DEEP - width) - place % halfway
+        return turned(pack[pl.ds(group * high, rows + 2 * width)], shift)
+
+    blocks = [sides(i) for i in range(half)]
+    faces = [sides(half + i) for i in range(half)]
+    swapped = [turned(block, halfway) for block in faces]
+    blocks += [jnp.where(low, a, b) for a, b in zip(faces, swapped)]
+    blocks += [jnp.where(low, b, a) for a, b in zip(faces, swapped)]
+    blocks += [sides(4 * half + i) for i in range(half)]
+    for i in range(half):
+        a = sides(5 * half + i)
+        b = turned(a, halfway)
+        blocks.append(jnp.where(low, b, a) if i % 2 else jnp.where(low, a, b))
     at = 0
-    for out, (width, group, place, _) in zip(tile_targets(half, tiles), lane_places(half)):
-        count = rows + 2 * width
-        inset = DEEP - width if group < groups - 1 else 0
-        here = pl.ds(group * high + inset, count)
-        sides = jnp.where(in_lanes(lane, place, width), right[here], left[here])
-        out[...] = jnp.where(lane < 2 * DEEP, turned(sides, -place), edge_own[at : at + count])
+    for block, out in zip(blocks, targets):
+        count = block.shape[0]
+        out[...] = jnp.where(inside, block, own[at : at + count])
         at += count
     diffusion(half, tiles, totals)
     body = pl.ds(STEPS + DEEP, rows)
-
-    def joined(main, sides):
-        sides = jnp.where(lane < DEEP, turned(sides, -2 * DEEP), sides)
-        return jnp.where(in_lanes(lane, DEEP, lanes - 2 * DEEP), main, sides)
-
-    for i in range(half):
-        increment[i] = joined(main_total[i], totals[i]) * keep[5 * half + i]
-        mine[i] = joined(main_mine[i], tiles[i][0, body])
-        theirs[i] = joined(main_theirs[i], tiles[i][1, body])
+    shift = halfway + DEEP if after else -DEEP
+    chosen = lane >= lanes - DEEP if after else lane < DEEP
+    for i in range(half):
+        field = tiles[i][0, body]
+        total_out[i] = jnp.where(chosen, turned(totals[i], shift), total_in[i])
+        mine[i] = jnp.where(chosen, turned(field, shift), mine_in[i])
+        theirs[i] = jnp.where(chosen, turned(field, shift + halfway), theirs_in[i])
+
+
+def last_edge_kernel(half, keep, pack, own, total_in, mine_in, theirs_in, increment, *rest):
+    edge_kernel(half, True, pack, own, total_in, mine_in, theirs_in, increment, *rest)
+    for i in range(half):
+        increment[i] = increment[i] * keep[5 * half + i]
 
 
 def partial_kernel(half, vertical, alpha, mine, partial, splat):
@@ -382,12 +403,15 @@
     levels, rows, lanes = lon_faces.shape
     half = levels // 2
     high = rows + 2 * DEEP
-    groups = 1 + max(group for _, group, _, _ in lane_places(half))
+    groups = 1 + max(group for _, group, _ in lane_places(half))
     column = f32((groups - 1) * high + rows + 2 * STEPS, lanes)
     block = f32(half, rows, lanes)
-    tiles = [pltpu.VMEM((2, high + 2 * STEPS, lanes), jnp.float32) for _ in range(2 * half)]
-    tiles.append(pltpu.VMEM((3 * half, high + STEPS, lanes), jnp.float32))
-    tiles.append(pltpu.VMEM((3 * half, rows + 2 * STEPS, lanes), jnp.float32))
+
+    def tiles(copies):
+        shapes = [(copies, high + 2 * STEPS, lanes)] * (2 * half)
+        shapes.append((3 * half, high + STEPS, lanes))
+        shapes.append(((1 + copies) * half, rows + 2 * STEPS, lanes))
+        return [pltpu.VMEM(shape, jnp.float32) for shape in shapes]
 
     def strips(source, counts, name):
         strip = f32(sum(count * width for count, width in counts), lanes)
@@ -458,25 +482,35 @@
     )(*own_columns, *early_columns, got_below, got_above)
     left = around(east, "lat", 1)
     right = around(west, "lat", -1)
-    edge_own = f32(high * 4 * half + (rows + 2 * STEPS) * 3 * half, lanes)
-    main = pl.pallas_call(
+    edge_own = f32(high * 3 * half + (rows + 2 * STEPS) * 2 * half, lanes)
+    *main, left_own, right_own = pl.pallas_call(
         functools.partial(main_kernel, half),
-        out_shape=(block, block, block, edge_own),
+        out_shape=(block, block, block, edge_own, edge_own),
         in_specs=[VMEM] * 6,
-        out_specs=(VMEM,) * 4,
-        scratch_shapes=tiles,
+        out_specs=(VMEM,) * 5,
+        scratch_shapes=tiles(2),
         compiler_params=PARAMS,
         name="main",
     )(*blocks)
+    edge_tiles = [pltpu.VMEM(block.shape, jnp.float32)] + tiles(1)
+    joined = pl.pallas_call(
+        functools.partial(edge_kernel, half, False),
+        out_shape=(block, block, block),
+        in_specs=[VMEM] * 5,
+        out_specs=(VMEM,) * 3,
+        scratch_shapes=edge_tiles,
+        compiler_params=PARAMS,
+        name="left_edge",
+    )(left, left_own, *main)
     increment, mine, theirs = pl.pallas_call(
-        functools.partial(edge_kernel, half),
+        functools.partial(last_edge_kernel, half),
         out_shape=(block, block, block),
-        in_specs=[VMEM] * 7,
+        in_specs=[VMEM] * 6,
         out_specs=(VMEM,) * 3,
-        scratch_shapes=[pltpu.VMEM(block.shape, jnp.float32)] + tiles,
-        compiler_params=PARAMS,
-        name="edge",
-    )(keep, left, right, *main)
+        scratch_shapes=edge_tiles,
+        compiler_params=PARAMS,
+        name="right_edge",
+    )(keep, right, right_own, *joined)
     got = around(theirs, "mem", 1)
 
     partial, splat = pl.pallas_call(

time: 33.9 us -> 35.6 us (1.050)
  Pallas kernels: 10.4 us -> 12.3 us
    pallas_call x1 -> x2, Pallas kernels: 3.76 us -> 5.14 us  [the longest x1 2.85 us: local(): pl.pallas_call(functools.partial(last_edge_kernel, half), out_shape=(bloc...]
    pallas_call x1, Pallas kernels: 3.05 us -> 3.54 us  [local(): pl.pallas_call(functools.partial(main_kernel, half), out_shape=(block, bl...]
  transfers between devices with their start and end apart: 8 -> 8, of which waited for: 2 -> 2; matrix products, arithmetic and copies ran while one was open for 0% -> 0% of each run, Pallas kernels for 13% -> 20%
where the time goes in v8:
time: 35.6 us; the launch traced here: 35.5 us
  starting transfers between devices  21.2 us (60%)
  Pallas kernels  12.3 us (35%)
  waiting for transfers between devices  1.3 us (4%)
  between operations  0.75 us (2%)
    ppermute x8, starting transfers between devices, around(): return lax.ppermute(value, axis, pairs)  21.2 us
    pallas_call x1, Pallas kernels, local(): pl.pallas_call(functools.partial(main_kernel, half), out_shape=(block, bl...  3.54 us
    pallas_call x1, Pallas kernels, local(): pl.pallas_call(functools.partial(last_edge_kernel, half), out_shape=(bloc...  2.85 us
    pallas_call x1, Pallas kernels, local(): pl.pallas_call(functools.partial(edge_kernel, half, False), out_shape=(bl...  2.29 us
    pallas_call x1, Pallas kernels, local(): pl.pallas_call(functools.partial(prepare_kernel, half), out_shape=(f32(6...  1.39 us
    ppermute x8, waiting for transfers between devices, around(): return lax.ppermute(value, axis, pairs)  1.3 us
    pallas_call x1, Pallas kernels, local(): pl.pallas_call(functools.partial(partial_kernel, half), out_shape=(f32(le...  0.75 us
    pallas_call x1, Pallas kernels, local(): pl.pallas_call(functools.partial(gradient_kernel, half), out_shape=f32(*a...  0.73 us
  transfers between devices with their start and end apart: 8, of which 2 were waited for; matrix products, arithmetic and copies ran while one was open for 0% of the time, Pallas kernels for 20%

profile of v8, /device:TPU:1, one launch (start us, length us, event | category | flops | bytes accessed | tf_op | source)
XLA Modules:
  0.0 35.5 jit_solution(16596431305506027725)
XLA Ops:
  0.6 1.4 %prepare.1 = (f32[30,32,128]{2,1,0:T(8,128)S(1)}, f32[10,32,128]{2,1,0:T(8,128)S(1)}, f32[1,10,32,128]{3,2,1,0:T(8,128)S(1)}) custom-call(f32[10,10]{1,0:T(8,128)} %vertical.1, f32[1,10,32,128]{3,2,1,0:T(8,128)} %alpha_hbm.1, f32[1,10,32,128]{3,2,1,0:T(8,128)} %anomaly_hbm.1, f32[10,32,128]{2,1,0:T(8,128)} %lon_hbm.1, f32[10,32,128]{2,1,0:T(8,128)} %lat_hbm.1, ...), custom_call_target="tpu_custom_call" | custom-call | tf_op jit(solution)/shard_map/prepare/pallas_call | solution.py:438
  2.0 3.3 %collective-permute-start = (f32[10,32,128]{2,1,0:T(8,128)S(1)}, f32[10,32,128]{2,1,0:T(8,128)S(1)}, u32[]{:S(2)}, u32[]{:S(2)}) collective-permute-start(f32[10,32,128]{2,1,0:T(8,128)S(1)} %get-tuple-element.29), channel_id=1, source_target_pairs={{0,1},{1,0},{2,3},{3,2},{4,5},{5,4},{6,7},{7,6},{8,9},{9,8},{10,11... | collective-permute-start | bytes 491528 | tf_op jit(solution)/shard_map/ppermute | solution.py:28
  5.4 1.1 %collective-permute-start.1 = (f32[320,128]{1,0:T(8,128)S(1)}, f32[320,128]{1,0:T(8,128)S(1)}, u32[]{:S(2)}, u32[]{:S(2)}) collective-permute-start(f32[320,128]{1,0:T(8,128)S(1)} %get-tuple-element.32), channel_id=1, source_target_pairs={{0,16},{16,32},{32,48},{48,64},{64,80},{80,96},{96,112},{112,128},... | collective-permute-start | bytes 491528 | tf_op jit(solution)/shard_map/ppermute | solution.py:28
  6.5 5.4 %collective-permute-start.2 = (f32[320,128]{1,0:T(8,128)S(1)}, f32[320,128]{1,0:T(8,128)S(1)}, u32[]{:S(2)}, u32[]{:S(2)}) collective-permute-start(f32[320,128]{1,0:T(8,128)S(1)} %get-tuple-element.33), channel_id=1, source_target_pairs={{0,240},{16,0},{32,16},{48,32},{64,48},{80,64},{96,80},{112,96},{1... | collective-permute-start | bytes 491528 | tf_op jit(solution)/shard_map/ppermute | solution.py:28
  11.9 0.0 collective-permute-done.got.source
  11.9 0.1 collective-permute-start.3
  12.0 5.1 %collective-permute-start.4 = (f32[120,128]{1,0:T(8,128)S(1)}, f32[120,128]{1,0:T(8,128)S(1)}, u32[]{:S(2)}, u32[]{:S(2)}) collective-permute-start(f32[120,128]{1,0:T(8,128)S(1)} %get-tuple-element.37), channel_id=1, source_target_pairs={{0,240},{16,0},{32,16},{48,32},{64,48},{80,64},{96,80},{112,96},{1... | collective-permute-start | bytes 184328 | tf_op jit(solution)/shard_map/ppermute | solution.py:28
  17.0 0.3 own_columns.1
  17.4 0.0 collective-permute-done.1.below.kept_below
  17.4 0.0 collective-permute-done.2.above.kept_above
  17.4 0.2 early_columns.1
  17.6 1.1 %collective-permute-done.3.below.got_below = f32[120,128]{1,0:T(8,128)S(1)} collective-permute-done((f32[120,128]{1,0:T(8,128)S(1)}, f32[120,128]{1,0:T(8,128)S(1)}, u32[]{:S(2)}, u32[]{:S(2)}) %collective-permute-start.3) | collective-permute-done | bytes 61472 | tf_op jit(solution)/shard_map/ppermute | solution.py:28
  18.7 0.0 collective-permute-done.4.above.got_above
  18.7 0.1 columns.1
  18.9 0.4 %collective-permute-start.6 = (f32[240,128]{1,0:T(8,128)S(1)}, f32[240,128]{1,0:T(8,128)S(1)}, u32[]{:S(2)}, u32[]{:S(2)}) collective-permute-start(f32[240,128]{1,0:T(8,128)S(1)} %get-tuple-element.40), channel_id=1, source_target_pairs={{0,2},{2,4},{4,6},{6,8},{8,10},{10,12},{12,14},{14,0},{1,3},{3,5},... | collective-permute-start | bytes 368648 | tf_op jit(solution)/shard_map/ppermute | solution.py:28
  19.3 3.3 %collective-permute-start.5 = (f32[240,128]{1,0:T(8,128)S(1)}, f32[240,128]{1,0:T(8,128)S(1)}, u32[]{:S(2)}, u32[]{:S(2)}) collective-permute-start(f32[240,128]{1,0:T(8,128)S(1)} %get-tuple-element.38), channel_id=1, source_target_pairs={{0,14},{2,0},{4,2},{6,4},{8,6},{10,8},{12,10},{14,12},{1,15},{3,1}... | collective-permute-start | bytes 368648 | tf_op jit(solution)/shard_map/ppermute | solution.py:28
  22.5 3.5 %main.1 = (f32[5,32,128]{2,1,0:T(8,128)S(1)}, f32[5,32,128]{2,1,0:T(8,128)S(1)}, f32[5,32,128]{2,1,0:T(8,128)S(1)}, f32[1440,128]{1,0:T(8,128)S(1)}, f32[1440,128]{1,0:T(8,128)S(1)}) custom-call(f32[30,32,128]{2,1,0:T(8,128)S(1)} %get-tuple-element.28.keep.source, f32[10,32,128]{2,1,0:T(8,128)S(1)} %collective-permute-done.got.source, ...), custom_call_target="tpu_custom_call" | custom-call | tf_op jit(solution)/shard_map/main/pallas_call | solution.py:486
  26.1 0.0 collective-permute-done.6.pack
  26.1 2.3 %left_edge.1 = (f32[5,32,128]{2,1,0:T(8,128)S(1)}, f32[5,32,128]{2,1,0:T(8,128)S(1)}, f32[5,32,128]{2,1,0:T(8,128)S(1)}) custom-call(f32[240,128]{1,0:T(8,128)S(1)} %collective-permute-done.6.pack, f32[1440,128]{1,0:T(8,128)S(1)} %get-tuple-element.41.own, f32[5,32,128]{2,1,0:T(8,128)S(1)} %get-tuple-element.42.total_in, ...), custom_call_target="tpu_custom_call" | custom-call | tf_op jit(solution)/shard_map/left_edge/pallas_call | solution.py:496
  28.4 0.0 collective-permute-done.5.pack
  28.4 0.0 copy-start
  28.4 2.9 %right_edge.1 = (f32[5,32,128]{2,1,0:T(8,128)}, f32[5,32,128]{2,1,0:T(8,128)S(1)}, f32[5,32,128]{2,1,0:T(8,128)S(1)}) custom-call(f32[30,32,128]{2,1,0:T(8,128)S(1)} %get-tuple-element.28.keep.source, f32[240,128]{1,0:T(8,128)S(1)} %collective-permute-done.5.pack, f32[1440,128]{1,0:T(8,128)S(1)} %get-tuple-element.39.own, ...), custom_call_target="tpu_custom_call" | custom-call | tf_op jit(solution)/shard_map/right_edge/pallas_call | solution.py:505
  31.2 2.6 %collective-permute-start.7 = (f32[5,32,128]{2,1,0:T(8,128)S(1)}, f32[5,32,128]{2,1,0:T(8,128)S(1)}, u32[]{:S(2)}, u32[]{:S(2)}) collective-permute-start(f32[5,32,128]{2,1,0:T(8,128)S(1)} %get-tuple-element.53), channel_id=1, source_target_pairs={{0,1},{1,0},{2,3},{3,2},{4,5},{5,4},{6,7},{7,6},{8,9},{9,8},{10,11... | collective-permute-start | bytes 245768 | tf_op jit(solution)/shard_map/ppermute | solution.py:28
  33.8 0.0 copy-done
  33.8 0.8 %partial.1 = (f32[10,32,128]{2,1,0:T(8,128)S(1)}, f32[5,10,128]{2,1,0:T(8,128)S(1)}) custom-call(f32[10,10]{1,0:T(8,128)S(1)} %copy-done, f32[1,10,32,128]{3,2,1,0:T(8,128)S(1)} %get-tuple-element.49.alpha, f32[5,32,128]{2,1,0:T(8,128)S(1)} %get-tuple-element.50.mine), custom_call_target="tpu_custom_call" | custom-call | tf_op jit(solution)/shard_map/partial/pallas_call | solution.py:516
  34.6 0.2 collective-permute-done.7.got
  34.7 0.7 %gradient.1 = f32[1,10,32,128]{3,2,1,0:T(8,128)} custom-call(f32[10,32,128]{2,1,0:T(8,128)S(1)} %get-tuple-element.51.partial, f32[5,10,128]{2,1,0:T(8,128)S(1)} %get-tuple-element.52.splat, f32[5,32,128]{2,1,0:T(8,128)S(1)} %collective-permute-done.7.got), custom_call_target="tpu_custom_call" | custom-call | tf_op jit(solution)/shard_map/gradient/pallas_call | solution.py:524
  (2 shorter events, 0.0 us)
Async XLA Ops:
  2.0 9.8 %collective-permute-start = (f32[10,32,128]{2,1,0:T(8,128)S(1)}, f32[10,32,128]{2,1,0:T(8,128)S(1)}, u32[]{:S(2)}, u32[]{:S(2)}) collective-permute-start(f32[10,32,128]{2,1,0:T(8,128)S(1)} %get-tuple-element.29), channel_id=1, source_target_pairs={{0,1},{1,0},{2,3},{3,2},{4,5},{5,4},{6,7},{7,6},{8,9},{9,8},{10,11... | collective-permute-start | bytes 491528 | tf_op jit(solution)/shard_map/ppermute | solution.py:28
  5.4 12.0 %collective-permute-start.1 = (f32[320,128]{1,0:T(8,128)S(1)}, f32[320,128]{1,0:T(8,128)S(1)}, u32[]{:S(2)}, u32[]{:S(2)}) collective-permute-start(f32[320,128]{1,0:T(8,128)S(1)} %get-tuple-element.32), channel_id=1, source_target_pairs={{0,16},{16,32},{32,48},{48,64},{64,80},{80,96},{96,112},{112,128},... | collective-permute-start | bytes 491528 | tf_op jit(solution)/shard_map/ppermute | solution.py:28
  6.5 10.9 %collective-permute-start.2 = (f32[320,128]{1,0:T(8,128)S(1)}, f32[320,128]{1,0:T(8,128)S(1)}, u32[]{:S(2)}, u32[]{:S(2)}) collective-permute-start(f32[320,128]{1,0:T(8,128)S(1)} %get-tuple-element.33), channel_id=1, source_target_pairs={{0,240},{16,0},{32,16},{48,32},{64,48},{80,64},{96,80},{112,96},{1... | collective-permute-start | bytes 491528 | tf_op jit(solution)/shard_map/ppermute | solution.py:28
  11.9 6.9 %collective-permute-start.3 = (f32[120,128]{1,0:T(8,128)S(1)}, f32[120,128]{1,0:T(8,128)S(1)}, u32[]{:S(2)}, u32[]{:S(2)}) collective-permute-start(f32[120,128]{1,0:T(8,128)S(1)} %get-tuple-element.36), channel_id=1, source_target_pairs={{0,16},{16,32},{32,48},{48,64},{64,80},{80,96},{96,112},{112,128},... | collective-permute-start | bytes 184328 | tf_op jit(solution)/shard_map/ppermute | solution.py:28
  12.0 6.8 %collective-permute-start.4 = (f32[120,128]{1,0:T(8,128)S(1)}, f32[120,128]{1,0:T(8,128)S(1)}, u32[]{:S(2)}, u32[]{:S(2)}) collective-permute-start(f32[120,128]{1,0:T(8,128)S(1)} %get-tuple-element.37), channel_id=1, source_target_pairs={{0,240},{16,0},{32,16},{48,32},{64,48},{80,64},{96,80},{112,96},{1... | collective-permute-start | bytes 184328 | tf_op jit(solution)/shard_map/ppermute | solution.py:28
  18.9 7.2 %collective-permute-start.6 = (f32[240,128]{1,0:T(8,128)S(1)}, f32[240,128]{1,0:T(8,128)S(1)}, u32[]{:S(2)}, u32[]{:S(2)}) collective-permute-start(f32[240,128]{1,0:T(8,128)S(1)} %get-tuple-element.40), channel_id=1, source_target_pairs={{0,2},{2,4},{4,6},{6,8},{8,10},{10,12},{12,14},{14,0},{1,3},{3,5},... | collective-permute-start | bytes 368648 | tf_op jit(solution)/shard_map/ppermute | solution.py:28
  19.3 9.1 %collective-permute-start.5 = (f32[240,128]{1,0:T(8,128)S(1)}, f32[240,128]{1,0:T(8,128)S(1)}, u32[]{:S(2)}, u32[]{:S(2)}) collective-permute-start(f32[240,128]{1,0:T(8,128)S(1)} %get-tuple-element.38), channel_id=1, source_target_pairs={{0,14},{2,0},{4,2},{6,4},{8,6},{10,8},{12,10},{14,12},{1,15},{3,1}... | collective-permute-start | bytes 368648 | tf_op jit(solution)/shard_map/ppermute | solution.py:28
  28.4 5.4 %copy-start = (f32[10,10]{1,0:T(8,128)S(1)}, f32[10,10]{1,0:T(8,128)}, u32[]{:S(2)}) copy-start(f32[10,10]{1,0:T(8,128)} %vertical.1) | copy-start | bytes 1204
  31.2 3.5 %collective-permute-start.7 = (f32[5,32,128]{2,1,0:T(8,128)S(1)}, f32[5,32,128]{2,1,0:T(8,128)S(1)}, u32[]{:S(2)}, u32[]{:S(2)}) collective-permute-start(f32[5,32,128]{2,1,0:T(8,128)S(1)} %get-tuple-element.53), channel_id=1, source_target_pairs={{0,1},{1,0},{2,3},{3,2},{4,5},{5,4},{6,7},{7,6},{8,9},{9,8},{10,11... | collective-permute-start | bytes 245768 | tf_op jit(solution)/shard_map/ppermute | solution.py:28

commit v9 on v7

--- a/solution.py
+++ b/solution.py
@@ -212,7 +212,7 @@
     return tiles[:half], tiles[half : 2 * half], tiles[2 * half], tiles[2 * half + 1]
 
 
-def diffusion(half, tiles, totals):
+def diffusion(half, tiles, totals, straight):
     fields, others, face_tiles, shallow_tiles = split_tiles(half, tiles)
     high = fields[0].shape[1] - 2 * STEPS
     rows = high - 2 * DEEP
@@ -249,6 +249,12 @@
 
     def root(margin):
         begin, end = STEPS + margin, STEPS + high - margin
+        if straight:
+            refs = fields, others
+            for n in range(STEPS):
+                cut = TILE if n == STEPS - 1 else 0
+                step(refs[n % 2], refs[1 - n % 2], begin + cut, end - cut)
+            return
 
         def steps(_, carry):
             for _ in range(STEPS // 4):
@@ -310,7 +316,7 @@
             edge_own[edge_at : edge_at + count] = own
             offset += count
             edge_at += count
-    diffusion(half, tiles, total)
+    diffusion(half, tiles, total, False)
     own = pl.ds(STEPS + DEEP, rows)
     for i in range(half):
         mine[i] = tiles[i][0, own]
@@ -319,20 +325,19 @@
 
 def edge_kernel(
     half,
-    keep,
     left,
     right,
     main_total,
     main_mine,
     main_theirs,
     edge_own,
-    increment,
+    total,
     mine,
     theirs,
     totals,
     *tiles,
 ):
-    rows, lanes = keep.shape[1:]
+    rows, lanes = mine.shape[1:]
     lane = lax.broadcasted_iota(jnp.int32, (1, lanes), 1)
     high = rows + 2 * DEEP
     groups = 1 + max(group for _, group, _, _ in lane_places(half))
@@ -344,7 +349,7 @@
         sides = jnp.where(in_lanes(lane, place, width), right[here], left[here])
         out[...] = jnp.where(lane < 2 * DEEP, turned(sides, -place), edge_own[at : at + count])
         at += count
-    diffusion(half, tiles, totals)
+    diffusion(half, tiles, totals, True)
     body = pl.ds(STEPS + DEEP, rows)
 
     def joined(main, sides):
@@ -352,20 +357,22 @@
         return jnp.where(in_lanes(lane, DEEP, lanes - 2 * DEEP), main, sides)
 
     for i in range(half):
-        increment[i] = joined(main_total[i], totals[i]) * keep[5 * half + i]
+        total[i] = joined(main_total[i], totals[i])
         mine[i] = joined(main_mine[i], tiles[i][0, body])
         theirs[i] = joined(main_theirs[i], tiles[i][1, body])
 
 
-def partial_kernel(half, vertical, alpha, mine, partial, splat):
+def partial_kernel(half, vertical, alpha, mine, keep, total, partial, splat, increment):
+    for i in range(half):
+        increment[i] = total[i] * keep[5 * half + i]
     base = lax.axis_index("mem") * half
     other = half - base
     for k in range(2 * half):
-        total = alpha[0, k]
+        result = alpha[0, k]
         for i in range(half):
-            total = total + vertical[base + i, k] * mine[i]
+            result = result + vertical[base + i, k] * mine[i]
             splat[i, k : k + 1] = jnp.full((1, splat.shape[2]), vertical[other + i, k])
-        partial[k] = total
+        partial[k] = result
 
 
 def gradient_kernel(half, partial, splat, got, gradient):
@@ -468,25 +475,25 @@
         compiler_params=PARAMS,
         name="main",
     )(*blocks)
-    increment, mine, theirs = pl.pallas_call(
+    total, mine, theirs = pl.pallas_call(
         functools.partial(edge_kernel, half),
         out_shape=(block, block, block),
-        in_specs=[VMEM] * 7,
+        in_specs=[VMEM] * 6,
         out_specs=(VMEM,) * 3,
         scratch_shapes=[pltpu.VMEM(block.shape, jnp.float32)] + tiles,
         compiler_params=PARAMS,
         name="edge",
-    )(keep, left, right, *main)
+    )(left, right, *main)
     got = around(theirs, "mem", 1)
 
-    partial, splat = pl.pallas_call(
+    partial, splat, increment = pl.pallas_call(
         functools.partial(partial_kernel, half),
-        out_shape=(f32(levels, rows, lanes), f32(half, levels, lanes)),
-        in_specs=[SMEM] + [VMEM] * 2,
-        out_specs=(VMEM, VMEM),
+        out_shape=(f32(levels, rows, lanes), f32(half, levels, lanes), block),
+        in_specs=[SMEM] + [VMEM] * 4,
+        out_specs=(VMEM,) * 3,
         compiler_params=PARAMS,
         name="partial",
-    )(vertical, alpha, mine)
+    )(vertical, alpha, mine, keep, total)
     gradient = pl.pallas_call(
         functools.partial(gradient_kernel, half),
         out_shape=f32(*alpha_fields.shape),

time: 33.9 us -> 33.5 us (0.988)
  Pallas kernels: 10.4 us -> 9.99 us
    pallas_call x1, Pallas kernels: 3.76 us -> 2.75 us  [local(): pl.pallas_call(functools.partial(edge_kernel, half), out_shape=(block, bl...]
    pallas_call x1, Pallas kernels: 0.75 us -> 1.37 us  [local(): pl.pallas_call(functools.partial(partial_kernel, half), out_shape=(f32(le...]
  transfers between devices with their start and end apart: 8 -> 8, of which waited for: 2 -> 1; matrix products, arithmetic and copies ran while one was open for 0% -> 0% of each run, Pallas kernels for 13% -> 15%
where the time goes in v9:
time: 33.5 us; the launch traced here: 33.3 us
  starting transfers between devices  21.4 us (64%)
  Pallas kernels  9.99 us (30%)
  waiting for transfers between devices  1.15 us (3%)
  between operations  0.74 us (2%)
    ppermute x8, starting transfers between devices, around(): return lax.ppermute(value, axis, pairs)  21.4 us
    pallas_call x1, Pallas kernels, local(): pl.pallas_call(functools.partial(main_kernel, half), out_shape=(block, bl...  3.05 us
    pallas_call x1, Pallas kernels, local(): pl.pallas_call(functools.partial(edge_kernel, half), out_shape=(block, bl...  2.75 us
    pallas_call x1, Pallas kernels, local(): pl.pallas_call(functools.partial(prepare_kernel, half), out_shape=(f32(6...  1.39 us
    pallas_call x1, Pallas kernels, local(): pl.pallas_call(functools.partial(partial_kernel, half), out_shape=(f32(le...  1.37 us
    ppermute x8, waiting for transfers between devices, around(): return lax.ppermute(value, axis, pairs)  1.15 us
    pallas_call x1, Pallas kernels, local(): pl.pallas_call(functools.partial(gradient_kernel, half), out_shape=f32(*a...  0.72 us
  transfers between devices with their start and end apart: 8, of which 1 were waited for; matrix products, arithmetic and copies ran while one was open for 0% of the time, Pallas kernels for 15%

profile of v9, /device:TPU:1, one launch (start us, length us, event | category | flops | bytes accessed | tf_op | source)
XLA Modules:
  0.0 33.3 jit_solution(8926071828861845961)
XLA Ops:
  0.6 1.4 %prepare.1 = (f32[30,32,128]{2,1,0:T(8,128)S(1)}, f32[10,32,128]{2,1,0:T(8,128)S(1)}, f32[1,10,32,128]{3,2,1,0:T(8,128)S(1)}) custom-call(f32[10,10]{1,0:T(8,128)} %vertical.1, f32[1,10,32,128]{3,2,1,0:T(8,128)} %alpha_hbm.1, f32[1,10,32,128]{3,2,1,0:T(8,128)} %anomaly_hbm.1, f32[10,32,128]{2,1,0:T(8,128)} %lon_hbm.1, f32[10,32,128]{2,1,0:T(8,128)} %lat_hbm.1, ...), custom_call_target="tpu_custom_call" | custom-call | tf_op jit(solution)/shard_map/prepare/pallas_call | solution.py:421
  2.0 3.3 %collective-permute-start = (f32[10,32,128]{2,1,0:T(8,128)S(1)}, f32[10,32,128]{2,1,0:T(8,128)S(1)}, u32[]{:S(2)}, u32[]{:S(2)}) collective-permute-start(f32[10,32,128]{2,1,0:T(8,128)S(1)} %get-tuple-element.27), channel_id=1, source_target_pairs={{0,1},{1,0},{2,3},{3,2},{4,5},{5,4},{6,7},{7,6},{8,9},{9,8},{10,11... | collective-permute-start | bytes 491528 | tf_op jit(solution)/shard_map/ppermute | solution.py:28
  5.4 1.1 %collective-permute-start.1 = (f32[320,128]{1,0:T(8,128)S(1)}, f32[320,128]{1,0:T(8,128)S(1)}, u32[]{:S(2)}, u32[]{:S(2)}) collective-permute-start(f32[320,128]{1,0:T(8,128)S(1)} %get-tuple-element.30), channel_id=1, source_target_pairs={{0,16},{16,32},{32,48},{48,64},{64,80},{80,96},{96,112},{112,128},... | collective-permute-start | bytes 491528 | tf_op jit(solution)/shard_map/ppermute | solution.py:28
  6.5 5.4 %collective-permute-start.2 = (f32[320,128]{1,0:T(8,128)S(1)}, f32[320,128]{1,0:T(8,128)S(1)}, u32[]{:S(2)}, u32[]{:S(2)}) collective-permute-start(f32[320,128]{1,0:T(8,128)S(1)} %get-tuple-element.31), channel_id=1, source_target_pairs={{0,240},{16,0},{32,16},{48,32},{64,48},{80,64},{96,80},{112,96},{1... | collective-permute-start | bytes 491528 | tf_op jit(solution)/shard_map/ppermute | solution.py:28
  11.9 0.0 collective-permute-done.got.source
  11.9 0.1 collective-permute-start.3
  12.0 5.1 %collective-permute-start.4 = (f32[120,128]{1,0:T(8,128)S(1)}, f32[120,128]{1,0:T(8,128)S(1)}, u32[]{:S(2)}, u32[]{:S(2)}) collective-permute-start(f32[120,128]{1,0:T(8,128)S(1)} %get-tuple-element.35), channel_id=1, source_target_pairs={{0,240},{16,0},{32,16},{48,32},{64,48},{80,64},{96,80},{112,96},{1... | collective-permute-start | bytes 184328 | tf_op jit(solution)/shard_map/ppermute | solution.py:28
  17.0 0.3 own_columns.1
  17.4 0.0 collective-permute-done.1.below.kept_below
  17.4 0.0 collective-permute-done.2.above.kept_above
  17.4 0.2 early_columns.1
  17.6 1.1 %collective-permute-done.3.below.got_below = f32[120,128]{1,0:T(8,128)S(1)} collective-permute-done((f32[120,128]{1,0:T(8,128)S(1)}, f32[120,128]{1,0:T(8,128)S(1)}, u32[]{:S(2)}, u32[]{:S(2)}) %collective-permute-start.3) | collective-permute-done | bytes 61472 | tf_op jit(solution)/shard_map/ppermute | solution.py:28
  18.7 0.0 collective-permute-done.4.above.got_above
  18.7 0.1 columns.1
  18.9 0.4 %collective-permute-start.5 = (f32[240,128]{1,0:T(8,128)S(1)}, f32[240,128]{1,0:T(8,128)S(1)}, u32[]{:S(2)}, u32[]{:S(2)}) collective-permute-start(f32[240,128]{1,0:T(8,128)S(1)} %get-tuple-element.36), channel_id=1, source_target_pairs={{0,2},{2,4},{4,6},{6,8},{8,10},{10,12},{12,14},{14,0},{1,3},{3,5},... | collective-permute-start | bytes 368648 | tf_op jit(solution)/shard_map/ppermute | solution.py:28
  19.3 3.3 %collective-permute-start.6 = (f32[240,128]{1,0:T(8,128)S(1)}, f32[240,128]{1,0:T(8,128)S(1)}, u32[]{:S(2)}, u32[]{:S(2)}) collective-permute-start(f32[240,128]{1,0:T(8,128)S(1)} %get-tuple-element.37), channel_id=1, source_target_pairs={{0,14},{2,0},{4,2},{6,4},{8,6},{10,8},{12,10},{14,12},{1,15},{3,1}... | collective-permute-start | bytes 368648 | tf_op jit(solution)/shard_map/ppermute | solution.py:28
  22.5 3.0 %main.1 = (f32[5,32,128]{2,1,0:T(8,128)S(1)}, f32[5,32,128]{2,1,0:T(8,128)S(1)}, f32[5,32,128]{2,1,0:T(8,128)S(1)}, f32[2000,128]{1,0:T(8,128)S(1)}) custom-call(f32[30,32,128]{2,1,0:T(8,128)S(1)} %get-tuple-element.26.keep.source, f32[10,32,128]{2,1,0:T(8,128)S(1)} %collective-permute-done.got.source, ...), custom_call_target="tpu_custom_call" | custom-call | tf_op jit(solution)/shard_map/main/pallas_call | solution.py:469
  25.6 0.0 collective-permute-done.5.left
  25.6 0.0 collective-permute-done.6.right
  25.6 0.0 copy-start
  25.6 2.8 %edge.1 = (f32[5,32,128]{2,1,0:T(8,128)S(1)}, f32[5,32,128]{2,1,0:T(8,128)S(1)}, f32[5,32,128]{2,1,0:T(8,128)S(1)}) custom-call(f32[240,128]{1,0:T(8,128)S(1)} %collective-permute-done.5.left, f32[240,128]{1,0:T(8,128)S(1)} %collective-permute-done.6.right, f32[5,32,128]{2,1,0:T(8,128)S(1)} %get-tuple-element.38.main_total, ...), custom_call_target="tpu_custom_call" | custom-call | tf_op jit(solution)/shard_map/edge/pallas_call | solution.py:478
  28.4 2.8 %collective-permute-start.7 = (f32[5,32,128]{2,1,0:T(8,128)S(1)}, f32[5,32,128]{2,1,0:T(8,128)S(1)}, u32[]{:S(2)}, u32[]{:S(2)}) collective-permute-start(f32[5,32,128]{2,1,0:T(8,128)S(1)} %get-tuple-element.47), channel_id=1, source_target_pairs={{0,1},{1,0},{2,3},{3,2},{4,5},{5,4},{6,7},{7,6},{8,9},{9,8},{10,11... | collective-permute-start | bytes 245768 | tf_op jit(solution)/shard_map/ppermute | solution.py:28
  31.2 0.0 copy-done
  31.2 1.4 %partial.1 = (f32[10,32,128]{2,1,0:T(8,128)S(1)}, f32[5,10,128]{2,1,0:T(8,128)S(1)}, f32[5,32,128]{2,1,0:T(8,128)}) custom-call(f32[10,10]{1,0:T(8,128)S(1)} %copy-done, f32[1,10,32,128]{3,2,1,0:T(8,128)S(1)} %get-tuple-element.25.alpha, f32[5,32,128]{2,1,0:T(8,128)S(1)} %get-tuple-element.42.mine, f32[30,32,128]{2,1,0:T(8,128)S(1)} %get-tuple-element.26.keep.source, ...), custom_call_target="tpu_custom_call" | custom-call | tf_op jit(solution)/shard_map/partial/pallas_call | solution.py:489
  32.6 0.0 collective-permute-done.7.got
  32.6 0.7 %gradient.1 = f32[1,10,32,128]{3,2,1,0:T(8,128)} custom-call(f32[10,32,128]{2,1,0:T(8,128)S(1)} %get-tuple-element.45.partial, f32[5,10,128]{2,1,0:T(8,128)S(1)} %get-tuple-element.46.splat, f32[5,32,128]{2,1,0:T(8,128)S(1)} %collective-permute-done.7.got), custom_call_target="tpu_custom_call" | custom-call | tf_op jit(solution)/shard_map/gradient/pallas_call | solution.py:497
  (2 shorter events, 0.0 us)
Async XLA Ops:
  2.0 9.8 %collective-permute-start = (f32[10,32,128]{2,1,0:T(8,128)S(1)}, f32[10,32,128]{2,1,0:T(8,128)S(1)}, u32[]{:S(2)}, u32[]{:S(2)}) collective-permute-start(f32[10,32,128]{2,1,0:T(8,128)S(1)} %get-tuple-element.27), channel_id=1, source_target_pairs={{0,1},{1,0},{2,3},{3,2},{4,5},{5,4},{6,7},{7,6},{8,9},{9,8},{10,11... | collective-permute-start | bytes 491528 | tf_op jit(solution)/shard_map/ppermute | solution.py:28
  5.4 12.0 %collective-permute-start.1 = (f32[320,128]{1,0:T(8,128)S(1)}, f32[320,128]{1,0:T(8,128)S(1)}, u32[]{:S(2)}, u32[]{:S(2)}) collective-permute-start(f32[320,128]{1,0:T(8,128)S(1)} %get-tuple-element.30), channel_id=1, source_target_pairs={{0,16},{16,32},{32,48},{48,64},{64,80},{80,96},{96,112},{112,128},... | collective-permute-start | bytes 491528 | tf_op jit(solution)/shard_map/ppermute | solution.py:28
  6.5 10.9 %collective-permute-start.2 = (f32[320,128]{1,0:T(8,128)S(1)}, f32[320,128]{1,0:T(8,128)S(1)}, u32[]{:S(2)}, u32[]{:S(2)}) collective-permute-start(f32[320,128]{1,0:T(8,128)S(1)} %get-tuple-element.31), channel_id=1, source_target_pairs={{0,240},{16,0},{32,16},{48,32},{64,48},{80,64},{96,80},{112,96},{1... | collective-permute-start | bytes 491528 | tf_op jit(solution)/shard_map/ppermute | solution.py:28
  11.9 6.9 %collective-permute-start.3 = (f32[120,128]{1,0:T(8,128)S(1)}, f32[120,128]{1,0:T(8,128)S(1)}, u32[]{:S(2)}, u32[]{:S(2)}) collective-permute-start(f32[120,128]{1,0:T(8,128)S(1)} %get-tuple-element.34), channel_id=1, source_target_pairs={{0,16},{16,32},{32,48},{48,64},{64,80},{80,96},{96,112},{112,128},... | collective-permute-start | bytes 184328 | tf_op jit(solution)/shard_map/ppermute | solution.py:28
  12.0 6.8 %collective-permute-start.4 = (f32[120,128]{1,0:T(8,128)S(1)}, f32[120,128]{1,0:T(8,128)S(1)}, u32[]{:S(2)}, u32[]{:S(2)}) collective-permute-start(f32[120,128]{1,0:T(8,128)S(1)} %get-tuple-element.35), channel_id=1, source_target_pairs={{0,240},{16,0},{32,16},{48,32},{64,48},{80,64},{96,80},{112,96},{1... | collective-permute-start | bytes 184328 | tf_op jit(solution)/shard_map/ppermute | solution.py:28
  18.9 6.7 %collective-permute-start.5 = (f32[240,128]{1,0:T(8,128)S(1)}, f32[240,128]{1,0:T(8,128)S(1)}, u32[]{:S(2)}, u32[]{:S(2)}) collective-permute-start(f32[240,128]{1,0:T(8,128)S(1)} %get-tuple-element.36), channel_id=1, source_target_pairs={{0,2},{2,4},{4,6},{6,8},{8,10},{10,12},{12,14},{14,0},{1,3},{3,5},... | collective-permute-start | bytes 368648 | tf_op jit(solution)/shard_map/ppermute | solution.py:28
  19.3 6.3 %collective-permute-start.6 = (f32[240,128]{1,0:T(8,128)S(1)}, f32[240,128]{1,0:T(8,128)S(1)}, u32[]{:S(2)}, u32[]{:S(2)}) collective-permute-start(f32[240,128]{1,0:T(8,128)S(1)} %get-tuple-element.37), channel_id=1, source_target_pairs={{0,14},{2,0},{4,2},{6,4},{8,6},{10,8},{12,10},{14,12},{1,15},{3,1}... | collective-permute-start | bytes 368648 | tf_op jit(solution)/shard_map/ppermute | solution.py:28
  25.6 5.6 %copy-start = (f32[10,10]{1,0:T(8,128)S(1)}, f32[10,10]{1,0:T(8,128)}, u32[]{:S(2)}) copy-start(f32[10,10]{1,0:T(8,128)} %vertical.1) | copy-start | bytes 1204
  28.4 4.2 %collective-permute-start.7 = (f32[5,32,128]{2,1,0:T(8,128)S(1)}, f32[5,32,128]{2,1,0:T(8,128)S(1)}, u32[]{:S(2)}, u32[]{:S(2)}) collective-permute-start(f32[5,32,128]{2,1,0:T(8,128)S(1)} %get-tuple-element.47), channel_id=1, source_target_pairs={{0,1},{1,0},{2,3},{3,2},{4,5},{5,4},{6,7},{7,6},{8,9},{9,8},{10,11... | collective-permute-start | bytes 245768 | tf_op jit(solution)/shard_map/ppermute | solution.py:28
